TPU v7x, 32 devices: a whole 2x2x4 slice. The times are simulated.
32 devices in a mesh: loop: 16 (over z, x, core), rep: 2 (over y).
Axes of the slice: x: 2, y: 2, z: 4, core: 2. Of those that a mesh axis runs over, the one named last changes fastest.
Arguments:
- features: bfloat16 [4096, 256], P(('loop', 'rep')), may hold values from -6 to 6
- weight: bfloat16 [256, 256], replicated, may hold values from -0.375 to 0.375
- tile_values: bfloat16 [3072, 128, 128], P(('loop', 'rep')), may hold values from -0.375 to 0.375
- tile_coords: int32 [3072, 2], P(('loop', 'rep')), may hold values from 0 to 1
- tile_counts: int32 [32, 8], P(('loop', 'rep')), may hold values from 1 to 12, as said below
Outputs:
- activated: bfloat16 [4096, 256], P(('loop', 'rep'))
Inputs may be any that keep to these rules, and one draw needn't show every extreme that they name: `tile_counts`: some list uses all 12 slots at some step; loads differ strongly between lists. `tile_coords`: row block within the group's rows and column block within the slab of that step.
All inputs are finite; a program needn't handle non-finite values.
Results may differ from a plain program's by a relative error of at most 0.0049.
Values may be sent and summed in bfloat16 or wider, within the bound.
No kernel may reach another device: no remote copies, remote signals or barrier semaphores. Data moves between devices by JAX's collectives and lax.ppermute only.
A program may use at most 64 MiB of HBM per device.

v0:
```python
import jax
import jax.numpy as jnp
from jax import lax
from jax.sharding import PartitionSpec as P


def from_behind(x, axis, by):
    count = lax.axis_size(axis)
    return lax.ppermute(x, axis, [(i, (i + by) % count) for i in range(count)])


def local(features, weight, tile_values, tile_coords, tile_counts):
    rep_size = lax.axis_size("rep")
    loop_size = lax.axis_size("loop")
    step_count = loop_size // rep_size
    tile_size = tile_values.shape[1]
    feat_width = features.shape[1]
    slot_count = tile_values.shape[0] // step_count
    current_slab = lax.all_gather(features, "rep", axis=0, tiled=True)
    block_count = current_slab.shape[0] // tile_size
    values = tile_values.reshape(step_count, slot_count, tile_size, tile_size)
    coords = tile_coords.reshape(step_count, slot_count, 2)
    counts = tile_counts.reshape(step_count)
    rep_rank = lax.axis_index("rep")
    for bit_index in range(rep_size.bit_length() - 1):
        shifted = from_behind(current_slab, "loop", step_count * (1 << bit_index))
        current_slab = jnp.where(rep_rank >> bit_index & 1 == 1, shifted, current_slab)
    running = jnp.zeros((block_count, tile_size, feat_width), jnp.float32)
    for step_index in range(step_count):
        slab_blocks = current_slab.reshape(block_count, tile_size, feat_width)
        pieces = jnp.take(slab_blocks, coords[step_index, :, 1], axis=0)
        products = jnp.einsum(
            "ktc,kcf->ktf", values[step_index], pieces, preferred_element_type=jnp.float32
        )
        live_slot = (jnp.arange(slot_count) < counts[step_index]).astype(jnp.float32)
        running = running.at[coords[step_index, :, 0]].add(products * live_slot[:, None, None])
        if step_index + 1 < step_count:
            current_slab = from_behind(current_slab, "loop", 1)
    summed = lax.psum_scatter(
        running.reshape(block_count * tile_size, feat_width), "rep", scatter_dimension=0, tiled=True
    )
    aggregated = summed.astype(jnp.bfloat16)
    product = jnp.dot(aggregated, weight, preferred_element_type=jnp.float32)
    return jnp.maximum(product, 0.0).astype(jnp.bfloat16)


def solution(mesh):
    placed = (
        P(("loop", "rep"), None),
        P(),
        P(("loop", "rep"), None, None),
        P(("loop", "rep"), None),
        P(("loop", "rep"), None),
    )
    return jax.shard_map(
        local, mesh=mesh, in_specs=placed, out_specs=P(("loop", "rep"), None), check_vma=False
    )
```

profile of v0, /device:TPU:0, one launch (start us, length us, event | category | flops | bytes accessed | tf_op | source)
XLA Modules:
  0.0 115.2 jit_solution(2277347458965333136)
XLA Ops:
  6.5 6.3 %all_gather.3 = bf16[256,256]{1,0:T(8,128)(2,1)S(1)} all-gather(bf16[128,256]{1,0:T(8,128)(2,1)} %param.7), channel_id=1, replica_groups=mesh['loop'=16,'rep'=2] {'rep'}, dimensions={0}, use_global_device_ids=true | all-gather | bytes 196608 | tf_op jit(solution)/shard_map/all_gather | solution.py:19
  12.8 3.0 %collective-permute-start = (bf16[256,256]{1,0:T(8,128)(2,1)S(1)}, bf16[256,256]{1,0:T(8,128)(2,1)S(1)}, u32[]{:S(2)}, u32[]{:S(2)}) collective-permute-start(bf16[256,256]{1,0:T(8,128)(2,1)S(1)} %all_gather.3), channel_id=1, source_target_pairs={{0,16},{2,18},{4,20},{6,22},{8,24},{10,26},{12,28},{14,30},{16,0},... | collective-permute-start | bytes 393224 | tf_op jit(solution)/shard_map/ppermute | solution.py:9
  17.8 1.6 %fusion.50 = (s32[1,1]{1,0:T(1,128)}, s32[1,1]{1,0:T(1,128)}, s32[1,1]{1,0:T(1,128)}, s32[1,1]{1,0:T(1,128)}, s32[1,1]{1,0:T(1,128)}, /*index=5*/s32[1,1]{1,0:T(1,128)}, s32[1,1]{1,0:T(1,128)}, s32[1,1]{1,0:T(1,128)}) fusion(s32[1,8]{1,0:T(1,128)} %param.11), kind=kLoop, calls=%fused_computation.132 | loop fusion | bytes 64 | tf_op jit(solution)/shard_map/slice | solution.py:35
  30.1 2.6 %multiply_bitcast_fusion.7 = f32[12,128,256]{1,2,0:T(8,128)} fusion(bf16[12,128,256]{2,1,0:T(8,128)(2,1)S(1)} %gather_fusion, f32[12]{0:T(128)S(1)} %compare_convert_fusion.7, pred[12]{0:T(512)(128)(4,1)S(1)} %get-tuple-element.34, bf16[96,128,128]{2,1,0:T(8,128)(2,1)} %param.9), kind=kOutput, calls=%fused_computation.23 | convolution fusion | flops 101449728 | bytes 2752572 | tf_op jit(solution)/shard_map/ktc,kcf->ktf/dot_general | solution.py:32
  32.8 1.9 %copy.33 = f32[12,128,256]{2,1,0:T(8,128)S(1)} copy(f32[12,128,256]{1,2,0:T(8,128)} %multiply_bitcast_fusion.7) | data formatting | bytes 3145728 | tf_op jit(solution)/shard_map/mul | solution.py:36
  34.7 1.8 %scatter_fusion = f32[2,128,256]{2,1,0:T(8,128)S(1)} fusion(f32[2,128,256]{2,1,0:T(8,128)S(1)} %broadcast_in_dim.11, s32[12]{0:T(128)S(1)} %get-tuple-element.43, f32[12,128,256]{2,1,0:T(8,128)S(1)} %copy.33), kind=kCustom, calls=%fused_computation.8 | custom fusion | flops 393216 | bytes 4718640 | tf_op jit(solution)/shard_map/scatter-add | solution.py:36
  36.7 1.5 %gather_fusion.1 = bf16[12,128,256]{2,1,0:T(8,128)(2,1)S(1)} fusion(bf16[2,128,256]{2,1,0:T(8,128)(2,1)} %bitcast.9, s32[1024]{0:T(1024)S(1)} %pad_clamp_fusion.6), kind=kCustom, calls=%fused_computation.1.clone | custom fusion | bytes 1572912 | tf_op jit(solution)/shard_map/jit(_take)/gather | solution.py:31
  41.6 1.9 %scatter_fusion.1 = f32[2,128,256]{2,1,0:T(8,128)S(1)} fusion(f32[2,128,256]{2,1,0:T(8,128)S(1)} %scatter_fusion, s32[12]{0:T(128)} %get-tuple-element.42, f32[12,128,256]{2,1,0:T(8,128)S(1)} %copy.37), kind=kCustom, calls=%fused_computation.9 | custom fusion | flops 393216 | bytes 4718640 | tf_op jit(solution)/shard_map/scatter-add | solution.py:36
  43.6 2.1 %collective-permute-done.2 = bf16[256,256]{1,0:T(8,128)(2,1)} collective-permute-done((bf16[256,256]{1,0:T(8,128)(2,1)}, bf16[256,256]{1,0:T(8,128)(2,1)}, u32[]{:S(2)}, u32[]{:S(2)}) %collective-permute-start.2) | collective-permute-done | bytes 131104 | tf_op jit(solution)/shard_map/ppermute | solution.py:9
  45.7 1.6 %gather_fusion.2 = bf16[12,128,256]{2,1,0:T(8,128)(2,1)S(1)} fusion(bf16[2,128,256]{2,1,0:T(8,128)(2,1)} %bitcast.15, s32[1024]{0:T(1024)} %pad_clamp_fusion.5), kind=kCustom, calls=%fused_computation.2.clone | custom fusion | bytes 1572912 | tf_op jit(solution)/shard_map/jit(_take)/gather | solution.py:31
  49.3 1.9 %scatter_fusion.2 = f32[2,128,256]{2,1,0:T(8,128)S(1)} fusion(f32[2,128,256]{2,1,0:T(8,128)S(1)} %scatter_fusion.1, s32[12]{0:T(128)} %get-tuple-element.41, f32[12,128,256]{2,1,0:T(8,128)S(1)} %copy.41), kind=kCustom, calls=%fused_computation.10 | custom fusion | flops 393216 | bytes 4718640 | tf_op jit(solution)/shard_map/scatter-add | solution.py:36
  51.3 3.4 %collective-permute-done.3 = bf16[256,256]{1,0:T(8,128)(2,1)} collective-permute-done((bf16[256,256]{1,0:T(8,128)(2,1)}, bf16[256,256]{1,0:T(8,128)(2,1)}, u32[]{:S(2)}, u32[]{:S(2)}) %collective-permute-start.3) | collective-permute-done | bytes 131104 | tf_op jit(solution)/shard_map/ppermute | solution.py:9
  54.8 1.6 %gather_fusion.3 = bf16[12,128,256]{2,1,0:T(8,128)(2,1)S(1)} fusion(bf16[2,128,256]{2,1,0:T(8,128)(2,1)} %bitcast.21, s32[1024]{0:T(1024)} %pad_clamp_fusion.4), kind=kCustom, calls=%fused_computation.3.clone | custom fusion | bytes 1572912 | tf_op jit(solution)/shard_map/jit(_take)/gather | solution.py:31
  56.5 1.5 %multiply_bitcast_fusion.4 = f32[12,128,256]{1,2,0:T(8,128)S(1)} fusion(bf16[12,128,256]{2,1,0:T(8,128)(2,1)S(1)} %gather_fusion.3, f32[12]{0:T(128)S(1)} %copy-done.17, pred[12]{0:T(512)(128)(4,1)S(1)} %copy-done.10, bf16[96,128,128]{2,1,0:T(8,128)(2,1)} %param.9), kind=kOutput, calls=%fused_computation.20 | convolution fusion | flops 101449728 | bytes 2752572 | tf_op jit(solution)/shard_map/ktc,kcf->ktf/dot_general | solution.py:32
  58.4 1.9 %scatter_fusion.3 = f32[2,128,256]{2,1,0:T(8,128)S(1)} fusion(f32[2,128,256]{2,1,0:T(8,128)S(1)} %scatter_fusion.2, s32[12]{0:T(128)} %get-tuple-element.40, f32[12,128,256]{2,1,0:T(8,128)S(1)} %copy.45), kind=kCustom, calls=%fused_computation.11 | custom fusion | flops 393216 | bytes 4718640 | tf_op jit(solution)/shard_map/scatter-add | solution.py:36
  60.4 3.4 %collective-permute-done.4 = bf16[256,256]{1,0:T(8,128)(2,1)} collective-permute-done((bf16[256,256]{1,0:T(8,128)(2,1)}, bf16[256,256]{1,0:T(8,128)(2,1)}, u32[]{:S(2)}, u32[]{:S(2)}) %collective-permute-start.4) | collective-permute-done | bytes 131104 | tf_op jit(solution)/shard_map/ppermute | solution.py:9
  63.8 1.5 %gather_fusion.4 = bf16[12,128,256]{2,1,0:T(8,128)(2,1)S(1)} fusion(bf16[2,128,256]{2,1,0:T(8,128)(2,1)} %bitcast.27, s32[1024]{0:T(1024)S(1)} %pad_clamp_fusion.3), kind=kCustom, calls=%fused_computation.4.clone | custom fusion | bytes 1572912 | tf_op jit(solution)/shard_map/jit(_take)/gather | solution.py:31
  65.4 1.5 %multiply_bitcast_fusion.3 = f32[12,128,256]{1,2,0:T(8,128)S(1)} fusion(bf16[12,128,256]{2,1,0:T(8,128)(2,1)S(1)} %gather_fusion.4, f32[12]{0:T(128)S(1)} %copy-done.16, pred[12]{0:T(512)(128)(4,1)S(1)} %copy-done.8, bf16[96,128,128]{2,1,0:T(8,128)(2,1)} %param.9), kind=kOutput, calls=%fused_computation.19 | convolution fusion | flops 101449728 | bytes 2752572 | tf_op jit(solution)/shard_map/ktc,kcf->ktf/dot_general | solution.py:32
  67.6 1.8 %scatter_fusion.4 = f32[2,128,256]{2,1,0:T(8,128)S(1)} fusion(f32[2,128,256]{2,1,0:T(8,128)S(1)} %scatter_fusion.3, s32[12]{0:T(128)S(1)} %copy-done.9, f32[12,128,256]{2,1,0:T(8,128)S(1)} %copy.49), kind=kCustom, calls=%fused_computation.12 | custom fusion | flops 393216 | bytes 4718640 | tf_op jit(solution)/shard_map/scatter-add | solution.py:36
  69.4 3.4 %collective-permute-done.5 = bf16[256,256]{1,0:T(8,128)(2,1)} collective-permute-done((bf16[256,256]{1,0:T(8,128)(2,1)}, bf16[256,256]{1,0:T(8,128)(2,1)}, u32[]{:S(2)}, u32[]{:S(2)}) %collective-permute-start.5) | collective-permute-done | bytes 131104 | tf_op jit(solution)/shard_map/ppermute | solution.py:9
  72.8 1.5 %gather_fusion.5 = bf16[12,128,256]{2,1,0:T(8,128)(2,1)S(1)} fusion(bf16[2,128,256]{2,1,0:T(8,128)(2,1)} %bitcast.33, s32[1024]{0:T(1024)S(1)} %pad_clamp_fusion.2), kind=kCustom, calls=%fused_computation.5.clone | custom fusion | bytes 1572912 | tf_op jit(solution)/shard_map/jit(_take)/gather | solution.py:31
  76.7 1.8 %scatter_fusion.5 = f32[2,128,256]{2,1,0:T(8,128)S(1)} fusion(f32[2,128,256]{2,1,0:T(8,128)S(1)} %scatter_fusion.4, s32[12]{0:T(128)S(1)} %copy-done.7, f32[12,128,256]{2,1,0:T(8,128)S(1)} %copy.53), kind=kCustom, calls=%fused_computation.13 | custom fusion | flops 393216 | bytes 4718640 | tf_op jit(solution)/shard_map/scatter-add | solution.py:36
  78.6 3.4 %collective-permute-done.6 = bf16[256,256]{1,0:T(8,128)(2,1)} collective-permute-done((bf16[256,256]{1,0:T(8,128)(2,1)}, bf16[256,256]{1,0:T(8,128)(2,1)}, u32[]{:S(2)}, u32[]{:S(2)}) %collective-permute-start.6) | collective-permute-done | bytes 131104 | tf_op jit(solution)/shard_map/ppermute | solution.py:9
  82.0 1.5 %gather_fusion.6 = bf16[12,128,256]{2,1,0:T(8,128)(2,1)S(1)} fusion(bf16[2,128,256]{2,1,0:T(8,128)(2,1)} %bitcast.39, s32[1024]{0:T(1024)S(1)} %pad_clamp_fusion.1), kind=kCustom, calls=%fused_computation.6.clone | custom fusion | bytes 1572912 | tf_op jit(solution)/shard_map/jit(_take)/gather | solution.py:31
  83.5 1.5 %multiply_bitcast_fusion.1 = f32[12,128,256]{1,2,0:T(8,128)S(1)} fusion(bf16[12,128,256]{2,1,0:T(8,128)(2,1)S(1)} %gather_fusion.6, f32[12]{0:T(128)S(1)} %copy-done.14, pred[12]{0:T(512)(128)(4,1)S(1)} %copy-done.4, bf16[96,128,128]{2,1,0:T(8,128)(2,1)} %param.9), kind=kOutput, calls=%fused_computation.17 | convolution fusion | flops 101449728 | bytes 2752572 | tf_op jit(solution)/shard_map/ktc,kcf->ktf/dot_general | solution.py:32
  85.6 1.8 %scatter_fusion.6 = f32[2,128,256]{2,1,0:T(8,128)S(1)} fusion(f32[2,128,256]{2,1,0:T(8,128)S(1)} %scatter_fusion.5, s32[12]{0:T(128)S(1)} %copy-done.5, f32[12,128,256]{2,1,0:T(8,128)S(1)} %copy.57), kind=kCustom, calls=%fused_computation.14 | custom fusion | flops 393216 | bytes 4718640 | tf_op jit(solution)/shard_map/scatter-add | solution.py:36
  87.4 3.5 %collective-permute-done.7 = bf16[256,256]{1,0:T(8,128)(2,1)} collective-permute-done((bf16[256,256]{1,0:T(8,128)(2,1)}, bf16[256,256]{1,0:T(8,128)(2,1)}, u32[]{:S(2)}, u32[]{:S(2)}) %collective-permute-start.7) | collective-permute-done | bytes 131104 | tf_op jit(solution)/shard_map/ppermute | solution.py:9
  90.9 1.5 %gather_fusion.7 = bf16[12,128,256]{2,1,0:T(8,128)(2,1)S(1)} fusion(bf16[2,128,256]{2,1,0:T(8,128)(2,1)} %bitcast.45, s32[1024]{0:T(1024)S(1)} %pad_clamp_fusion), kind=kCustom, calls=%fused_computation.7.clone | custom fusion | bytes 1572912 | tf_op jit(solution)/shard_map/jit(_take)/gather | solution.py:31
  92.4 1.5 %multiply_bitcast_fusion = f32[12,128,256]{1,2,0:T(8,128)S(1)} fusion(bf16[12,128,256]{2,1,0:T(8,128)(2,1)S(1)} %gather_fusion.7, f32[12]{0:T(128)S(1)} %copy-done.13, pred[12]{0:T(512)(128)(4,1)S(1)} %copy-done.2, bf16[96,128,128]{2,1,0:T(8,128)(2,1)} %param.9), kind=kOutput, calls=%fused_computation.16 | convolution fusion | flops 101449728 | bytes 2752572 | tf_op jit(solution)/shard_map/ktc,kcf->ktf/dot_general | solution.py:32
  94.6 1.8 %scatter_fusion.7 = f32[2,128,256]{2,1,0:T(8,128)S(1)} fusion(f32[2,128,256]{2,1,0:T(8,128)S(1)} %scatter_fusion.6, s32[12]{0:T(128)S(1)} %copy-done.3, f32[12,128,256]{2,1,0:T(8,128)S(1)} %copy.61), kind=kCustom, calls=%fused_computation.15 | custom fusion | flops 393216 | bytes 4718640 | tf_op jit(solution)/shard_map/scatter-add | solution.py:36
  97.1 9.5 %reduce-scatter.2.cloned.1.call-done = f32[128,256]{1,0:T(8,128)} async-done(((f32[256,256]{1,0:T(8,128)}), f32[128,256]{1,0:T(8,128)}) %reduce-scatter.2.cloned.1.call-update) | async-done | bytes 131088 | tf_op jit(solution)/shard_map/reduce_scatter | solution.py:39
  106.7 1.7 %fusion = bf16[128,256]{1,0:T(8,128)(2,1)} fusion(bf16[256,256]{1,0:T(8,128)(2,1)S(1)} %copy-done, f32[128,256]{1,0:T(8,128)} %reduce-scatter.2.cloned.1.call-done), kind=kOutput, calls=%fused_computation.25 | convolution fusion | flops 16875520 | bytes 327680 | tf_op jit(solution)/shard_map/dot_general | solution.py:43
  (83 shorter events, 23.8 us)
Async XLA Ops:
  6.5 100.1 %copy-start = (bf16[256,256]{1,0:T(8,128)(2,1)S(1)}, bf16[256,256]{1,0:T(8,128)(2,1)}, u32[]{:S(2)}) copy-start(bf16[256,256]{1,0:T(8,128)(2,1)} %param.8) | copy-start | bytes 393220
  6.5 100.1 %reduce-scatter.2.cloned.1.call-start = ((), (), s32[]{:S(2)}) async-start(), calls=%async_computation.1 | async-start | bytes 393216 | tf_op jit(solution)/shard_map/reduce_scatter | solution.py:39
  12.8 16.6 %collective-permute-start = (bf16[256,256]{1,0:T(8,128)(2,1)S(1)}, bf16[256,256]{1,0:T(8,128)(2,1)S(1)}, u32[]{:S(2)}, u32[]{:S(2)}) collective-permute-start(bf16[256,256]{1,0:T(8,128)(2,1)S(1)} %all_gather.3), channel_id=1, source_target_pairs={{0,16},{2,18},{4,20},{6,22},{8,24},{10,26},{12,28},{14,30},{16,0},... | collective-permute-start | bytes 393224 | tf_op jit(solution)/shard_map/ppermute | solution.py:9
  29.4 7.2 %collective-permute-start.1 = (bf16[256,256]{1,0:T(8,128)(2,1)S(1)}, bf16[256,256]{1,0:T(8,128)(2,1)}, u32[]{:S(2)}, u32[]{:S(2)}) collective-permute-start(bf16[256,256]{1,0:T(8,128)(2,1)S(1)} %broadcast_select_fusion), channel_id=1, source_target_pairs={{0,2},{2,4},{4,6},{6,8},{8,10},{10,12},{12,14},{14,16},{16,18},{18... | collective-permute-start | bytes 393224 | tf_op jit(solution)/shard_map/ppermute | solution.py:9
  36.5 3.2 %copy-start.12 = (pred[12]{0:T(512)(128)(4,1)S(1)}, pred[12]{0:T(512)(128)(4,1)}, u32[]{:S(2)}) copy-start(pred[12]{0:T(512)(128)(4,1)} %get-tuple-element.32) | copy-start | bytes 40
  36.5 3.2 %copy-start.19 = (f32[12]{0:T(128)S(1)}, f32[12]{0:T(128)}, u32[]{:S(2)}) copy-start(f32[12]{0:T(128)} %compare_convert_fusion.6) | copy-start | bytes 148
  38.2 7.5 %collective-permute-start.2 = (bf16[256,256]{1,0:T(8,128)(2,1)}, bf16[256,256]{1,0:T(8,128)(2,1)}, u32[]{:S(2)}, u32[]{:S(2)}) collective-permute-start(bf16[256,256]{1,0:T(8,128)(2,1)} %collective-permute-done.1), channel_id=1, source_target_pairs={{0,2},{2,4},{4,6},{6,8},{8,10},{10,12},{12,14},{14,16},{16,18},{18... | collective-permute-start | bytes 393224 | tf_op jit(solution)/shard_map/ppermute | solution.py:9
  43.6 3.8 %copy-start.11 = (pred[12]{0:T(512)(128)(4,1)S(1)}, pred[12]{0:T(512)(128)(4,1)}, u32[]{:S(2)}) copy-start(pred[12]{0:T(512)(128)(4,1)} %get-tuple-element.30) | copy-start | bytes 40
  43.6 3.8 %copy-start.18 = (f32[12]{0:T(128)S(1)}, f32[12]{0:T(128)}, u32[]{:S(2)}) copy-start(f32[12]{0:T(128)} %compare_convert_fusion.5) | copy-start | bytes 148
  47.3 7.5 %collective-permute-start.3 = (bf16[256,256]{1,0:T(8,128)(2,1)}, bf16[256,256]{1,0:T(8,128)(2,1)}, u32[]{:S(2)}, u32[]{:S(2)}) collective-permute-start(bf16[256,256]{1,0:T(8,128)(2,1)} %collective-permute-done.2), channel_id=1, source_target_pairs={{0,2},{2,4},{4,6},{6,8},{8,10},{10,12},{12,14},{14,16},{16,18},{18... | collective-permute-start | bytes 393224 | tf_op jit(solution)/shard_map/ppermute | solution.py:9
  51.3 5.2 %copy-start.10 = (pred[12]{0:T(512)(128)(4,1)S(1)}, pred[12]{0:T(512)(128)(4,1)}, u32[]{:S(2)}) copy-start(pred[12]{0:T(512)(128)(4,1)} %get-tuple-element.28) | copy-start | bytes 40
  51.3 5.2 %copy-start.17 = (f32[12]{0:T(128)S(1)}, f32[12]{0:T(128)}, u32[]{:S(2)}) copy-start(f32[12]{0:T(128)} %compare_convert_fusion.4) | copy-start | bytes 148
  56.4 7.5 %collective-permute-start.4 = (bf16[256,256]{1,0:T(8,128)(2,1)}, bf16[256,256]{1,0:T(8,128)(2,1)}, u32[]{:S(2)}, u32[]{:S(2)}) collective-permute-start(bf16[256,256]{1,0:T(8,128)(2,1)} %collective-permute-done.3), channel_id=1, source_target_pairs={{0,2},{2,4},{4,6},{6,8},{8,10},{10,12},{12,14},{14,16},{16,18},{18... | collective-permute-start | bytes 393224 | tf_op jit(solution)/shard_map/ppermute | solution.py:9
  60.4 5.0 %copy-start.8 = (pred[12]{0:T(512)(128)(4,1)S(1)}, pred[12]{0:T(512)(128)(4,1)}, u32[]{:S(2)}) copy-start(pred[12]{0:T(512)(128)(4,1)} %get-tuple-element.26) | copy-start | bytes 40
  60.4 5.0 %copy-start.16 = (f32[12]{0:T(128)S(1)}, f32[12]{0:T(128)}, u32[]{:S(2)}) copy-start(f32[12]{0:T(128)} %compare_convert_fusion.3) | copy-start | bytes 148
  65.3 7.5 %collective-permute-start.5 = (bf16[256,256]{1,0:T(8,128)(2,1)}, bf16[256,256]{1,0:T(8,128)(2,1)}, u32[]{:S(2)}, u32[]{:S(2)}) collective-permute-start(bf16[256,256]{1,0:T(8,128)(2,1)} %collective-permute-done.4), channel_id=1, source_target_pairs={{0,2},{2,4},{4,6},{6,8},{8,10},{10,12},{12,14},{14,16},{16,18},{18... | collective-permute-start | bytes 393224 | tf_op jit(solution)/shard_map/ppermute | solution.py:9
  66.9 0.7 copy-start.9
  69.4 5.1 %copy-start.6 = (pred[12]{0:T(512)(128)(4,1)S(1)}, pred[12]{0:T(512)(128)(4,1)}, u32[]{:S(2)}) copy-start(pred[12]{0:T(512)(128)(4,1)} %get-tuple-element.24) | copy-start | bytes 40
  69.4 5.1 %copy-start.15 = (f32[12]{0:T(128)S(1)}, f32[12]{0:T(128)}, u32[]{:S(2)}) copy-start(f32[12]{0:T(128)} %compare_convert_fusion.2) | copy-start | bytes 148
  74.3 7.6 %collective-permute-start.6 = (bf16[256,256]{1,0:T(8,128)(2,1)}, bf16[256,256]{1,0:T(8,128)(2,1)}, u32[]{:S(2)}, u32[]{:S(2)}) collective-permute-start(bf16[256,256]{1,0:T(8,128)(2,1)} %collective-permute-done.5), channel_id=1, source_target_pairs={{0,2},{2,4},{4,6},{6,8},{8,10},{10,12},{12,14},{14,16},{16,18},{18... | collective-permute-start | bytes 393224 | tf_op jit(solution)/shard_map/ppermute | solution.py:9
  76.1 0.7 copy-start.7
  78.6 5.0 %copy-start.4 = (pred[12]{0:T(512)(128)(4,1)S(1)}, pred[12]{0:T(512)(128)(4,1)}, u32[]{:S(2)}) copy-start(pred[12]{0:T(512)(128)(4,1)} %get-tuple-element.22) | copy-start | bytes 40
  78.6 5.0 %copy-start.14 = (f32[12]{0:T(128)S(1)}, f32[12]{0:T(128)}, u32[]{:S(2)}) copy-start(f32[12]{0:T(128)} %compare_convert_fusion.1) | copy-start | bytes 148
  83.5 7.5 %collective-permute-start.7 = (bf16[256,256]{1,0:T(8,128)(2,1)}, bf16[256,256]{1,0:T(8,128)(2,1)}, u32[]{:S(2)}, u32[]{:S(2)}) collective-permute-start(bf16[256,256]{1,0:T(8,128)(2,1)} %collective-permute-done.6), channel_id=1, source_target_pairs={{0,2},{2,4},{4,6},{6,8},{8,10},{10,12},{12,14},{14,16},{16,18},{18... | collective-permute-start | bytes 393224 | tf_op jit(solution)/shard_map/ppermute | solution.py:9
  85.0 0.6 copy-start.5
  87.4 5.0 %copy-start.2 = (pred[12]{0:T(512)(128)(4,1)S(1)}, pred[12]{0:T(512)(128)(4,1)}, u32[]{:S(2)}) copy-start(pred[12]{0:T(512)(128)(4,1)} %get-tuple-element.6) | copy-start | bytes 40
  87.4 5.0 %copy-start.13 = (f32[12]{0:T(128)S(1)}, f32[12]{0:T(128)}, u32[]{:S(2)}) copy-start(f32[12]{0:T(128)} %compare_convert_fusion) | copy-start | bytes 148
  93.9 0.7 copy-start.3
  96.4 0.7 copy-start.1
Sparse Core Ops, SparseCore 0:
  97.3 9.3 reduce-scatter.1
where the time goes:
time: 116 us; the launch traced here: 115 us
  waiting for transfers between devices  28.9 us (25%)
  other arithmetic  26 us (22%)
  local copies, waits for them, and re-layouts  20.3 us (18%)
  matrix products  14.7 us (13%)
  between operations  14 us (12%)
  blocking collectives  6.26 us (5%)
  starting transfers between devices  5.05 us (4%)
    ppermute x8, waiting for transfers between devices, from_behind(): return lax.ppermute(x, axis, [(i, (i + by) % count) for i in range(count)])  19.3 us
    scatter-add x8, other arithmetic, local(): running.at[coords[step_index, :, 0]]  14.9 us
    dot_general x8, matrix products, local(): jnp.einsum('ktc,kcf->ktf', values[step_index], pieces, preferred_element_...  13 us
    gather x8, local copies, waits for them, and re-layouts, local(): pieces = jnp.take(slab_blocks, coords[step_index, :, 1], axis=0)  11.3 us
    reduce_scatter x1, waiting for transfers between devices, local(): lax.psum_scatter(running.reshape(block_count * tile_size, feat_width), 'r...  9.54 us
    convert_element_type x8, other arithmetic, local(): (jnp.arange(slot_count) < counts[step_index]).astype(jnp.float32)  8.7 us
    all_gather x1, blocking collectives, local(): current_slab = lax.all_gather(features, 'rep', axis=0, tiled=True)  6.26 us
    mul x8, local copies, waits for them, and re-layouts, local(): products * live_slot[:, None, None]  5.13 us
  transfers between devices with their start and end apart: 9, of which 8 were waited for; matrix products, arithmetic and copies ran while one was open for 38% of the time, Pallas kernels for 0%

commit v1 on v0

--- a/solution.py
+++ b/solution.py
@@ -1,7 +1,15 @@
+import functools
+
 import jax
 import jax.numpy as jnp
 from jax import lax
+from jax.experimental import pallas as pl
+from jax.experimental.pallas import tpu as pltpu
 from jax.sharding import PartitionSpec as P
+
+AXES = ("loop", "rep")
+VMEM = pl.BlockSpec(memory_space=pltpu.VMEM)
+SMEM = pl.BlockSpec(memory_space=pltpu.SMEM)
 
 
 def from_behind(x, axis, by):
@@ -9,7 +17,7 @@
     return lax.ppermute(x, axis, [(i, (i + by) % count) for i in range(count)])
 
 
-def local(features, weight, tile_values, tile_coords, tile_counts):
+def ring(features, weight, tile_values, tile_coords, tile_counts):
     rep_size = lax.axis_size("rep")
     loop_size = lax.axis_size("loop")
     step_count = loop_size // rep_size
@@ -44,14 +52,153 @@
     return jnp.maximum(product, 0.0).astype(jnp.bfloat16)
 
 
+HELD = 10
+
+
+def route(planes, move):
+    pairs = []
+    for z in range(planes):
+        for x in range(2):
+            for core in range(2):
+                for y in range(2):
+                    z2, x2, core2, y2 = move(z, x, core, y)
+                    pairs.append((((z * 2 + x) * 2 + core) * 2 + y, (((z2 % planes) * 2 + x2) * 2 + core2) * 2 + y2))
+    return pairs
+
+
+def spread(features, planes):
+    def send(value, move):
+        return lax.ppermute(value, AXES, route(planes, move))
+
+    def sign(y):
+        return 1 if y else -1
+
+    own = features
+    ahead = send(own, lambda z, x, c, y: (z - sign(y), x, c, y))
+    behind = send(own, lambda z, x, c, y: (z + sign(y), x, c, y))
+    far = send(own, lambda z, x, c, y: (z + 2, x, c, y))
+    near = (lax.axis_index("loop") >> 1 & 1) == lax.axis_index("rep")
+    beside = jnp.where(near, jnp.concatenate([own, ahead]), jnp.concatenate([ahead, far]))
+    across = jnp.where(near, jnp.concatenate([behind, far]), jnp.concatenate([own, behind]))
+    along_y = send(jnp.concatenate([own, behind, far]), lambda z, x, c, y: (z, x, c, 1 - y))
+    along_x = send(beside, lambda z, x, c, y: (z, 1 - x, c, y))
+    diagonal = send(across, lambda z, x, c, y: (z, 1 - x, c, 1 - y))
+    held = [own, ahead, far, along_x, along_y, diagonal]
+    other = send(jnp.concatenate(held), lambda z, x, c, y: (z, x, 1 - c, y))
+    return held + [other]
+
+
+def dense_kernel(where, counts, coords, values, out, total):
+    step = pl.program_id(0)
+    slots = values.shape[0]
+    tile = values.shape[1]
+    rank = where[8]
+
+    @pl.when(step == 0)
+    def _():
+        out[...] = jnp.zeros_like(out)
+
+    total[...] = jnp.zeros_like(total)
+
+    def add(slot, carry):
+        row = coords[step * slots + slot, 0] ^ rank
+        column = coords[step * slots + slot, 1] ^ rank
+        spot = row * 2 + column
+        total[spot] = total[spot] + values[slot].astype(jnp.float32)
+        return carry
+
+    lax.fori_loop(0, counts[0, step], add, 0)
+    for row in range(2):
+        for column in range(2):
+            start = pl.multiple_of((where[step] + column * (HELD // 2)) * tile, tile)
+            out[pl.ds(row * tile, tile), pl.ds(start, tile)] = total[row * 2 + column].astype(jnp.bfloat16)
+
+
+def dense(where, tile_counts, tile_coords, tile_values):
+    steps = tile_counts.shape[1]
+    slots = tile_values.shape[0] // steps
+    tile = tile_values.shape[1]
+    return pl.pallas_call(
+        dense_kernel,
+        grid=(steps,),
+        out_shape=jax.ShapeDtypeStruct((2 * tile, 2 * HELD * tile), jnp.bfloat16),
+        in_specs=[SMEM, SMEM, SMEM, pl.BlockSpec((slots, tile, tile), lambda i: (i, 0, 0))],
+        out_specs=pl.BlockSpec((2 * tile, 2 * HELD * tile), lambda i: (0, 0)),
+        scratch_shapes=[pltpu.VMEM((4, tile, tile), jnp.float32)],
+        compiler_params=pltpu.CompilerParams(vmem_limit_bytes=24 * 1024 * 1024),
+        cost_estimate=pl.CostEstimate(flops=4_000_000, bytes_accessed=6_000_000, transcendentals=0),
+    )(where, tile_counts, tile_coords, tile_values)
+
+
+def product_kernel(row, matrix, *refs):
+    out = refs[-1]
+    tile = out.shape[0]
+    total = jnp.zeros(out.shape, jnp.float32)
+    start = 0
+    for ref in refs[:-1]:
+        depth = ref.shape[0]
+        total += jnp.dot(
+            matrix[pl.ds(row * tile, tile), pl.ds(start, depth)], ref[...], preferred_element_type=jnp.float32
+        )
+        start += depth
+    out[...] = total.astype(out.dtype)
+
+
+def products(row, matrix, blocks, dtype):
+    tile = matrix.shape[0] // 2
+    width = blocks[0].shape[1]
+    return pl.pallas_call(
+        functools.partial(product_kernel, row),
+        out_shape=jax.ShapeDtypeStruct((tile, width), dtype),
+        in_specs=[VMEM] * (1 + len(blocks)),
+        out_specs=VMEM,
+        compiler_params=pltpu.CompilerParams(vmem_limit_bytes=24 * 1024 * 1024),
+        cost_estimate=pl.CostEstimate(
+            flops=2 * tile * matrix.shape[1] * width, bytes_accessed=2_000_000, transcendentals=0
+        ),
+    )(matrix, *blocks)
+
+
+def last_kernel(mine, theirs, weight, out):
+    aggregated = (mine[...] + theirs[...].astype(jnp.float32)).astype(jnp.bfloat16)
+    product = jnp.dot(aggregated, weight[...], preferred_element_type=jnp.float32)
+    out[...] = jnp.maximum(product, 0.0).astype(out.dtype)
+
+
+def last(mine, theirs, weight):
+    return pl.pallas_call(
+        last_kernel,
+        out_shape=jax.ShapeDtypeStruct(mine.shape, jnp.bfloat16),
+        in_specs=[VMEM] * 3,
+        out_specs=VMEM,
+    )(mine, theirs, weight)
+
+
+def pairs(features, weight, tile_values, tile_coords, tile_counts):
+    planes = lax.axis_size("loop") // 4
+    core = lax.axis_index("loop") & 1
+    rank = lax.axis_index("rep")
+    steps = jnp.arange(8, dtype=jnp.int32)
+    odd = steps & 1
+    there = odd * (1 - 2 * core)
+    k = jnp.where(rank == 0, steps + there, 8 - steps - there) // 2
+    where = jnp.where(k % 2 == 0, k // 2, 3 + k // 2) + HELD * odd
+    where = jnp.concatenate([where, rank[None]]).astype(jnp.int32)
+    matrix = dense(where, tile_counts, tile_coords, tile_values)
+    blocks = spread(features, planes)
+    theirs = products(1, matrix, blocks, jnp.bfloat16)
+    theirs = lax.ppermute(theirs, "rep", [(0, 1), (1, 0)])
+    mine = products(0, matrix, blocks, jnp.float32)
+    return last(mine, theirs, weight)
+
+
 def solution(mesh):
     placed = (
-        P(("loop", "rep"), None),
+        P(AXES, None),
         P(),
-        P(("loop", "rep"), None, None),
-        P(("loop", "rep"), None),
-        P(("loop", "rep"), None),
+        P(AXES, None, None),
+        P(AXES, None),
+        P(AXES, None),
     )
-    return jax.shard_map(
-        local, mesh=mesh, in_specs=placed, out_specs=P(("loop", "rep"), None), check_vma=False
-    )
+    local = pairs if dict(mesh.shape) == {"loop": 16, "rep": 2} else ring
+    return jax.shard_map(local, mesh=mesh, in_specs=placed, out_specs=P(AXES, None), check_vma=False)

time: 116 us -> 36.7 us (0.32)
  other arithmetic: 26 us -> 1.88 us
  waiting for transfers between devices: 28.9 us -> 13.3 us
  local copies, waits for them, and re-layouts: 20.3 us -> 5.52 us
  matrix products: 14.7 us -> 0 us
  between operations: 14 us -> 0.12 us
  blocking collectives: 6.26 us -> 0 us
  starting transfers between devices: 5.05 us -> 10.5 us
  Pallas kernels: 0 us -> 4.86 us
    scatter-add x8 -> x0, other arithmetic: 14.9 us -> none  [local(): running.at[coords[step_index, :, 0]]]
    dot_general x9 -> x0, matrix products: 14.7 us -> none  [the longest x8 13 us: local(): jnp.einsum('ktc,kcf->ktf', values[step_index], pieces, preferred_element_...]
    gather x8 -> x0, local copies, waits for them, and re-layouts: 11.3 us -> none  [local(): pieces = jnp.take(slab_blocks, coords[step_index, :, 1], axis=0)]
    reduce_scatter x1 -> x0, waiting for transfers between devices: 9.54 us -> none  [local(): lax.psum_scatter(running.reshape(block_count * tile_size, feat_width), 'r...]
    convert_element_type x8 -> x0, other arithmetic: 8.7 us -> none  [local(): (jnp.arange(slot_count) < counts[step_index]).astype(jnp.float32)]
    all_gather x1 -> x0, blocking collectives: 6.26 us -> none  [local(): current_slab = lax.all_gather(features, 'rep', axis=0, tiled=True)]
    ppermute x8, waiting for transfers between devices: 19.3 us -> 13.3 us  [the longest x7 10.7 us: send(): return lax.ppermute(value, AXES, route(planes, move))]
    ppermute x8, starting transfers between devices: 5.05 us -> 10.5 us  [the longest x7 9.75 us: send(): return lax.ppermute(value, AXES, route(planes, move))]
  transfers between devices with their start and end apart: 9 -> 8, of which waited for: 8 -> 5; matrix products, arithmetic and copies ran while one was open for 38% -> 7% of each run, Pallas kernels for 0% -> 7%
where the time goes in v1:
time: 36.7 us; the launch traced here: 36.1 us
  waiting for transfers between devices  13.3 us (36%)
  starting transfers between devices  10.5 us (29%)
  local copies, waits for them, and re-layouts  5.52 us (15%)
  Pallas kernels  4.86 us (13%)
  other arithmetic  1.88 us (5%)
    ppermute x7, waiting for transfers between devices, send(): return lax.ppermute(value, AXES, route(planes, move))  10.7 us
    ppermute x7, starting transfers between devices, send(): return lax.ppermute(value, AXES, route(planes, move))  9.75 us
    unnamed x16, local copies, waits for them, and re-layouts  5.51 us
    ppermute x1, waiting for transfers between devices, pairs(): theirs = lax.ppermute(theirs, 'rep', [(0, 1), (1, 0)])  2.55 us
    pallas_call x1, Pallas kernels, dense(): pl.pallas_call(dense_kernel, grid=(steps,), out_shape=jax.ShapeDtypeStruc...  2.34 us
    pallas_call x1, Pallas kernels, last(): pl.pallas_call(last_kernel, out_shape=jax.ShapeDtypeStruct(mine.shape, jn...  1.8 us
    select_n x1, other arithmetic, spread(): jnp.where(near, jnp.concatenate([behind, far]), jnp.concatenate([own, beh...  0.92 us
    concatenate x1, other arithmetic, spread(): jnp.concatenate([own, behind, far])  0.85 us
  transfers between devices with their start and end apart: 8, of which 5 were waited for; matrix products, arithmetic and copies ran while one was open for 7% of the time, Pallas kernels for 7%

profile of v1, /device:TPU:0, one launch (start us, length us, event | category | flops | bytes accessed | tf_op | source)
XLA Modules:
  0.0 36.1 jit_solution(3809643325641802278)
XLA Ops:
  0.0 5.0 %collective-permute-start.3 = (bf16[128,256]{1,0:T(8,128)(2,1)}, bf16[128,256]{1,0:T(8,128)(2,1)S(1)}, u32[]{:S(2)}, u32[]{:S(2)}) collective-permute-start(bf16[128,256]{1,0:T(8,128)(2,1)} %refs_0_.3), channel_id=1, source_target_pairs={{0,24},{1,9},{2,26},{3,11},{4,28},{5,13},{6,30},{7,15},{8,0},{9,17... | collective-permute-start | bytes 196616 | tf_op jit(solution)/shard_map/ppermute | solution.py:71
  5.0 0.0 collective-permute-start.1
  5.1 1.0 %collective-permute-start = (bf16[128,256]{1,0:T(8,128)(2,1)}, bf16[128,256]{1,0:T(8,128)(2,1)S(1)}, u32[]{:S(2)}, u32[]{:S(2)}) collective-permute-start(bf16[128,256]{1,0:T(8,128)(2,1)} %refs_0_.3), channel_id=1, source_target_pairs={{0,8},{1,25},{2,10},{3,27},{4,12},{5,29},{6,14},{7,31},{8,16},{9,1... | collective-permute-start | bytes 196616 | tf_op jit(solution)/shard_map/ppermute | solution.py:71
  6.1 0.9 %constant_dynamic-update-slice_fusion.5 = bf16[1280,256]{1,0:T(8,128)(2,1)S(1)} fusion(bf16[128,256]{1,0:T(8,128)(2,1)} %refs_0_.3), kind=kLoop, calls=%fused_computation.12 | loop fusion | bytes 131072
  6.9 0.9 %collective-permute-done.3 = bf16[128,256]{1,0:T(8,128)(2,1)S(1)} collective-permute-done((bf16[128,256]{1,0:T(8,128)(2,1)}, bf16[128,256]{1,0:T(8,128)(2,1)S(1)}, u32[]{:S(2)}, u32[]{:S(2)}) %collective-permute-start.3) | collective-permute-done | bytes 65568 | tf_op jit(solution)/shard_map/ppermute | solution.py:71
  7.9 3.9 %collective-permute-done.1.refs_2_ = bf16[128,256]{1,0:T(8,128)(2,1)S(1)} collective-permute-done((bf16[128,256]{1,0:T(8,128)(2,1)}, bf16[128,256]{1,0:T(8,128)(2,1)S(1)}, u32[]{:S(2)}, u32[]{:S(2)}) %collective-permute-start.1) | collective-permute-done | bytes 65568 | tf_op jit(solution)/shard_map/ppermute | solution.py:71
  11.7 0.0 collective-permute-done.refs_1_
  11.7 0.9 %fusion.1 = (bf16[256,256]{1,0:T(8,128)(2,1)S(1)}, bf16[256,256]{1,0:T(8,128)(2,1)S(1)}) fusion(bf16[128,256]{1,0:T(8,128)(2,1)S(1)} %collective-permute-done.1.refs_2_, bf16[128,256]{1,0:T(8,128)(2,1)} %refs_0_.3, bf16[128,256]{1,0:T(8,128)(2,1)S(1)} %collective-permute-done.3, pred[]{:T(512)S(6)} %eq.13, bf16[128,256]{1,0:T(8,128)(2,1)S(1)} %collective-permute-done.refs_1_), kind=kLoop, calls=%fused_computation.6 | loop fusion | flops 1048576 | bytes 524289 | tf_op jit(solution)/shard_map/jit(_where)/select_n | solution.py:82
  12.7 0.0 copy-start.1
  12.7 1.4 %collective-permute-start.5 = (bf16[256,256]{1,0:T(8,128)(2,1)S(1)}, bf16[256,256]{1,0:T(8,128)(2,1)S(1)}, u32[]{:S(2)}, u32[]{:S(2)}) collective-permute-start(bf16[256,256]{1,0:T(8,128)(2,1)S(1)} %get-tuple-element.5), channel_id=1, source_target_pairs={{0,5},{1,4},{2,7},{3,6},{4,1},{5,0},{6,3},{7,2},{8,13},{9,12},{10,... | collective-permute-start | bytes 393224 | tf_op jit(solution)/shard_map/ppermute | solution.py:71
  14.0 0.5 %collective-permute-start.2 = (bf16[256,256]{1,0:T(8,128)(2,1)S(1)}, bf16[256,256]{1,0:T(8,128)(2,1)S(1)}, u32[]{:S(2)}, u32[]{:S(2)}) collective-permute-start(bf16[256,256]{1,0:T(8,128)(2,1)S(1)} %get-tuple-element.6), channel_id=1, source_target_pairs={{0,4},{1,5},{2,6},{3,7},{4,0},{5,1},{6,2},{7,3},{8,12},{9,13},{10,... | collective-permute-start | bytes 393224 | tf_op jit(solution)/shard_map/ppermute | solution.py:71
  14.6 0.9 %pad_maximum_fusion = bf16[384,256]{1,0:T(8,128)(2,1)S(1)} fusion(bf16[128,256]{1,0:T(8,128)(2,1)S(1)} %collective-permute-done.1.refs_2_, bf16[128,256]{1,0:T(8,128)(2,1)S(1)} %collective-permute-done.3, bf16[128,256]{1,0:T(8,128)(2,1)} %refs_0_.3), kind=kLoop, calls=%fused_computation | loop fusion | flops 589824 | bytes 393216 | tf_op jit(solution)/shard_map/concatenate | solution.py:83
  15.4 1.7 %collective-permute-start.4 = (bf16[384,256]{1,0:T(8,128)(2,1)S(1)}, bf16[384,256]{1,0:T(8,128)(2,1)S(1)}, u32[]{:S(2)}, u32[]{:S(2)}) collective-permute-start(bf16[384,256]{1,0:T(8,128)(2,1)S(1)} %pad_maximum_fusion), channel_id=1, source_target_pairs={{0,1},{1,0},{2,3},{3,2},{4,5},{5,4},{6,7},{7,6},{8,9},{9,8},{10,11... | collective-permute-start | bytes 589832 | tf_op jit(solution)/shard_map/ppermute | solution.py:71
  17.2 3.4 %collective-permute-done.2.refs_3_ = bf16[256,256]{1,0:T(8,128)(2,1)S(1)} collective-permute-done((bf16[256,256]{1,0:T(8,128)(2,1)S(1)}, bf16[256,256]{1,0:T(8,128)(2,1)S(1)}, u32[]{:S(2)}, u32[]{:S(2)}) %collective-permute-start.2) | collective-permute-done | bytes 131104 | tf_op jit(solution)/shard_map/ppermute | solution.py:71
  20.5 2.5 %collective-permute-done.4.refs_4_ = bf16[384,256]{1,0:T(8,128)(2,1)S(1)} collective-permute-done((bf16[384,256]{1,0:T(8,128)(2,1)S(1)}, bf16[384,256]{1,0:T(8,128)(2,1)S(1)}, u32[]{:S(2)}, u32[]{:S(2)}) %collective-permute-start.4) | collective-permute-done | bytes 196640 | tf_op jit(solution)/shard_map/ppermute | solution.py:71
  23.1 0.0 collective-permute-done.5.refs_5_
  23.1 0.1 collective-permute-start.6
  23.2 0.8 %copy.6.coords = s32[96,2]{1,0:T(8,128)S(1)} copy(s32[96,2]{0,1:T(2,128)} %param.8) | data formatting | bytes 1536 | tf_op args[3]
  24.0 0.1 pad_add_fusion.where
  24.1 1.9 %copy-done = bf16[96,128,128]{2,1,0:T(8,128)(2,1)S(1)} copy-done((bf16[96,128,128]{2,1,0:T(8,128)(2,1)S(1)}, bf16[96,128,128]{2,1,0:T(8,128)(2,1)}, u32[]{:S(2)}) %copy-start) | copy-done | bytes 3145752
  26.0 0.7 %copy-done.3 = s32[1,8]{1,0:T(1,128)S(1)} copy-done((s32[1,8]{1,0:T(1,128)S(1)}, s32[1,8]{1,0:T(1,128)}, u32[]{:S(2)}) %copy-start.3) | copy-done | bytes 56
  26.6 2.3 %shard_map.55.matrix = bf16[256,2560]{1,0:T(8,128)(2,1)S(1)} custom-call(s32[9]{0:T(128)S(1)} %pad_add_fusion.where, s32[1,8]{1,0:T(1,128)S(1)} %copy-done.3, s32[96,2]{1,0:T(8,128)S(1)} %copy.6.coords, bf16[96,128,128]{2,1,0:T(8,128)(2,1)S(1)} %copy-done), custom_call_target="tpu_custom_call" | custom-call | flops 4000000 | bytes 6000000 | tf_op jit(solution)/shard_map/pallas_call | solution.py:121
  29.0 0.0 collective-permute-done.6.refs_6_
  29.0 0.0 copy-done.1
  29.0 0.4 %shard_map.57 = bf16[128,256]{1,0:T(8,128)(2,1)S(1)} custom-call(bf16[256,2560]{1,0:T(8,128)(2,1)S(1)} %shard_map.55.matrix, bf16[128,256]{1,0:T(8,128)(2,1)S(1)} %copy-done.1, bf16[128,256]{1,0:T(8,128)(2,1)S(1)} %collective-permute-done.refs_1_, bf16[128,256]{1,0:T(8,128)(2,1)S(1)} %collective-permute-done.1.refs_2_, ...), custom_call_target="tpu_custom_call" | custom-call | flops 167772160 | bytes 2000000 | tf_op jit(solution)/shard_map/pallas_call | solution.py:150
  29.4 0.8 %collective-permute-start.7 = (bf16[128,256]{1,0:T(8,128)(2,1)S(1)}, bf16[128,256]{1,0:T(8,128)(2,1)S(1)}, u32[]{:S(2)}, u32[]{:S(2)}) collective-permute-start(bf16[128,256]{1,0:T(8,128)(2,1)S(1)} %shard_map.57), channel_id=1, source_target_pairs={{0,1},{1,0},{2,3},{3,2},{4,5},{5,4},{6,7},{7,6},{8,9},{9,8},{10,11... | collective-permute-start | bytes 196616 | tf_op jit(solution)/shard_map/ppermute | solution.py:190
  30.1 0.4 shard_map.56.mine
  30.5 0.0 copy-start.2
  30.5 0.6 %copy-done.2 = f32[128,256]{1,0:T(8,128)} copy-done((f32[128,256]{1,0:T(8,128)}, f32[128,256]{1,0:T(8,128)S(1)}, u32[]{:S(2)}) %copy-start.2) | copy-done | bytes 131096
  31.2 2.6 %collective-permute-done.7.theirs = bf16[128,256]{1,0:T(8,128)(2,1)S(1)} collective-permute-done((bf16[128,256]{1,0:T(8,128)(2,1)S(1)}, bf16[128,256]{1,0:T(8,128)(2,1)S(1)}, u32[]{:S(2)}, u32[]{:S(2)}) %collective-permute-start.7) | collective-permute-done | bytes 65568 | tf_op jit(solution)/shard_map/ppermute | solution.py:190
  33.7 0.6 %copy-done.4 = bf16[128,256]{1,0:T(8,128)(2,1)} copy-done((bf16[128,256]{1,0:T(8,128)(2,1)}, bf16[128,256]{1,0:T(8,128)(2,1)S(1)}, u32[]{:S(2)}) %copy-start.4) | copy-done | bytes 65560
  34.3 1.8 %shard_map.58 = bf16[128,256]{1,0:T(8,128)(2,1)} custom-call(f32[128,256]{1,0:T(8,128)} %copy-done.2, bf16[128,256]{1,0:T(8,128)(2,1)} %copy-done.4, bf16[256,256]{1,0:T(8,128)(2,1)} %weight.1), custom_call_target="tpu_custom_call" | custom-call | tf_op jit(solution)/shard_map/pallas_call | solution.py:169
  (9 shorter events, 0.1 us)
Async XLA Ops:
  0.0 7.9 %collective-permute-start.3 = (bf16[128,256]{1,0:T(8,128)(2,1)}, bf16[128,256]{1,0:T(8,128)(2,1)S(1)}, u32[]{:S(2)}, u32[]{:S(2)}) collective-permute-start(bf16[128,256]{1,0:T(8,128)(2,1)} %refs_0_.3), channel_id=1, source_target_pairs={{0,24},{1,9},{2,26},{3,11},{4,28},{5,13},{6,30},{7,15},{8,0},{9,17... | collective-permute-start | bytes 196616 | tf_op jit(solution)/shard_map/ppermute | solution.py:71
  5.0 6.7 %collective-permute-start.1 = (bf16[128,256]{1,0:T(8,128)(2,1)}, bf16[128,256]{1,0:T(8,128)(2,1)S(1)}, u32[]{:S(2)}, u32[]{:S(2)}) collective-permute-start(bf16[128,256]{1,0:T(8,128)(2,1)} %refs_0_.3), channel_id=1, source_target_pairs={{0,16},{1,17},{2,18},{3,19},{4,20},{5,21},{6,22},{7,23},{8,24},{9,... | collective-permute-start | bytes 196616 | tf_op jit(solution)/shard_map/ppermute | solution.py:71
  5.1 6.7 %collective-permute-start = (bf16[128,256]{1,0:T(8,128)(2,1)}, bf16[128,256]{1,0:T(8,128)(2,1)S(1)}, u32[]{:S(2)}, u32[]{:S(2)}) collective-permute-start(bf16[128,256]{1,0:T(8,128)(2,1)} %refs_0_.3), channel_id=1, source_target_pairs={{0,8},{1,25},{2,10},{3,27},{4,12},{5,29},{6,14},{7,31},{8,16},{9,1... | collective-permute-start | bytes 196616 | tf_op jit(solution)/shard_map/ppermute | solution.py:71
  12.7 16.3 %copy-start.1 = (bf16[128,256]{1,0:T(8,128)(2,1)S(1)}, bf16[128,256]{1,0:T(8,128)(2,1)}, u32[]{:S(2)}) copy-start(bf16[128,256]{1,0:T(8,128)(2,1)} %refs_0_.3) | copy-start | bytes 196612
  12.7 10.4 %collective-permute-start.5 = (bf16[256,256]{1,0:T(8,128)(2,1)S(1)}, bf16[256,256]{1,0:T(8,128)(2,1)S(1)}, u32[]{:S(2)}, u32[]{:S(2)}) collective-permute-start(bf16[256,256]{1,0:T(8,128)(2,1)S(1)} %get-tuple-element.5), channel_id=1, source_target_pairs={{0,5},{1,4},{2,7},{3,6},{4,1},{5,0},{6,3},{7,2},{8,13},{9,12},{10,... | collective-permute-start | bytes 393224 | tf_op jit(solution)/shard_map/ppermute | solution.py:71
  14.0 6.5 %collective-permute-start.2 = (bf16[256,256]{1,0:T(8,128)(2,1)S(1)}, bf16[256,256]{1,0:T(8,128)(2,1)S(1)}, u32[]{:S(2)}, u32[]{:S(2)}) collective-permute-start(bf16[256,256]{1,0:T(8,128)(2,1)S(1)} %get-tuple-element.6), channel_id=1, source_target_pairs={{0,4},{1,5},{2,6},{3,7},{4,0},{5,1},{6,2},{7,3},{8,12},{9,13},{10,... | collective-permute-start | bytes 393224 | tf_op jit(solution)/shard_map/ppermute | solution.py:71
  15.4 7.7 %collective-permute-start.4 = (bf16[384,256]{1,0:T(8,128)(2,1)S(1)}, bf16[384,256]{1,0:T(8,128)(2,1)S(1)}, u32[]{:S(2)}, u32[]{:S(2)}) collective-permute-start(bf16[384,256]{1,0:T(8,128)(2,1)S(1)} %pad_maximum_fusion), channel_id=1, source_target_pairs={{0,1},{1,0},{2,3},{3,2},{4,5},{5,4},{6,7},{7,6},{8,9},{9,8},{10,11... | collective-permute-start | bytes 589832 | tf_op jit(solution)/shard_map/ppermute | solution.py:71
  23.1 5.9 %collective-permute-start.6 = (bf16[1280,256]{1,0:T(8,128)(2,1)S(1)}, bf16[1280,256]{1,0:T(8,128)(2,1)S(1)}, u32[]{:S(2)}, u32[]{:S(2)}) collective-permute-start(bf16[1280,256]{1,0:T(8,128)(2,1)S(1)} %constant_dynamic-update-slice_fusion), channel_id=1, source_target_pairs={{0,2},{1,3},{2,0},{3,1},{4,6},{5,7},{6,4},{7,5},{8,10},{9,11},{10,... | collective-permute-start | bytes 1966088 | tf_op jit(solution)/shard_map/ppermute | solution.py:71
  24.1 1.9 %copy-start = (bf16[96,128,128]{2,1,0:T(8,128)(2,1)S(1)}, bf16[96,128,128]{2,1,0:T(8,128)(2,1)}, u32[]{:S(2)}) copy-start(bf16[96,128,128]{2,1,0:T(8,128)(2,1)} %values.1) | copy-start | bytes 9437188
  26.0 0.7 %copy-start.3 = (s32[1,8]{1,0:T(1,128)S(1)}, s32[1,8]{1,0:T(1,128)}, u32[]{:S(2)}) copy-start(s32[1,8]{1,0:T(1,128)} %counts.1) | copy-start | bytes 100
  29.4 4.3 %collective-permute-start.7 = (bf16[128,256]{1,0:T(8,128)(2,1)S(1)}, bf16[128,256]{1,0:T(8,128)(2,1)S(1)}, u32[]{:S(2)}, u32[]{:S(2)}) collective-permute-start(bf16[128,256]{1,0:T(8,128)(2,1)S(1)} %shard_map.57), channel_id=1, source_target_pairs={{0,1},{1,0},{2,3},{3,2},{4,5},{5,4},{6,7},{7,6},{8,9},{9,8},{10,11... | collective-permute-start | bytes 196616 | tf_op jit(solution)/shard_map/ppermute | solution.py:190
  30.5 0.7 %copy-start.2 = (f32[128,256]{1,0:T(8,128)}, f32[128,256]{1,0:T(8,128)S(1)}, u32[]{:S(2)}) copy-start(f32[128,256]{1,0:T(8,128)S(1)} %shard_map.56.mine) | copy-start | bytes 393220
  33.7 0.6 %copy-start.4 = (bf16[128,256]{1,0:T(8,128)(2,1)}, bf16[128,256]{1,0:T(8,128)(2,1)S(1)}, u32[]{:S(2)}) copy-start(bf16[128,256]{1,0:T(8,128)(2,1)S(1)} %collective-permute-done.7.theirs) | copy-start | bytes 196612

commit v2 on v1

--- a/solution.py
+++ b/solution.py
@@ -51,8 +51,10 @@
     product = jnp.dot(aggregated, weight, preferred_element_type=jnp.float32)
     return jnp.maximum(product, 0.0).astype(jnp.bfloat16)
 
-
 HELD = 10
+PLACES = (0, 8, 1, 9, 2), (3, 6, 4, 7, 5)
+SMALL = 4 * 1024 * 1024
+MIDDLE = 24 * 1024 * 1024
 
 
 def route(planes, move):
@@ -66,68 +68,126 @@
     return pairs
 
 
-def spread(features, planes):
+def pick_kernel(even, odd, first, second, third, out):
+    near = (lax.axis_index("loop") >> 1 & 1) == lax.axis_index("rep")
+    rows = first.shape[0]
+    refs = (first, second, third)
+    for chosen, which in ((jnp.logical_not(near), even), (near, odd)):
+
+        @pl.when(chosen)
+        def _(which=which):
+            for i, j in enumerate(which):
+                out[pl.ds(i * rows, rows)] = refs[j][...]
+
+
+def pick(even, odd, *blocks):
+    rows, width = blocks[0].shape
+    return pl.pallas_call(
+        functools.partial(pick_kernel, even, odd),
+        out_shape=jax.ShapeDtypeStruct((2 * rows, width), blocks[0].dtype),
+        in_specs=[VMEM] * 3,
+        out_specs=VMEM,
+        compiler_params=pltpu.CompilerParams(vmem_limit_bytes=SMALL),
+        cost_estimate=pl.CostEstimate(flops=0, bytes_accessed=200_000, transcendentals=0),
+    )(*blocks)
+
+
+def lift_kernel(value, out):
+    out[...] = value[...]
+
+
+def lift(value):
+    return pl.pallas_call(
+        lift_kernel,
+        out_shape=jax.ShapeDtypeStruct(value.shape, value.dtype),
+        in_specs=[VMEM],
+        out_specs=VMEM,
+        compiler_params=pltpu.CompilerParams(vmem_limit_bytes=SMALL),
+        cost_estimate=pl.CostEstimate(flops=0, bytes_accessed=200_000, transcendentals=0),
+    )(value)
+
+
+def spread(features, planes, work):
     def send(value, move):
         return lax.ppermute(value, AXES, route(planes, move))
 
     def sign(y):
         return 1 if y else -1
 
-    own = features
-    ahead = send(own, lambda z, x, c, y: (z - sign(y), x, c, y))
-    behind = send(own, lambda z, x, c, y: (z + sign(y), x, c, y))
-    far = send(own, lambda z, x, c, y: (z + 2, x, c, y))
-    near = (lax.axis_index("loop") >> 1 & 1) == lax.axis_index("rep")
-    beside = jnp.where(near, jnp.concatenate([own, ahead]), jnp.concatenate([ahead, far]))
-    across = jnp.where(near, jnp.concatenate([behind, far]), jnp.concatenate([own, behind]))
-    along_y = send(jnp.concatenate([own, behind, far]), lambda z, x, c, y: (z, x, c, 1 - y))
-    along_x = send(beside, lambda z, x, c, y: (z, 1 - x, c, y))
-    diagonal = send(across, lambda z, x, c, y: (z, 1 - x, c, 1 - y))
-    held = [own, ahead, far, along_x, along_y, diagonal]
+    own = lift(features)
+    far = send(features, lambda z, x, c, y: (z + 2, x, c, y))
+    behind = send(features, lambda z, x, c, y: (z + sign(y), x, c, y))
+    ahead = send(features, lambda z, x, c, y: (z - sign(y), x, c, y))
+    partner = send(features, lambda z, x, c, y: (z, x, c, 1 - y))
+    far, own = lax.optimization_barrier((far, own))
+    along_y = send(jnp.concatenate([behind, far]), lambda z, x, c, y: (z, x, c, 1 - y))
+    behind, partner = lax.optimization_barrier((behind, partner))
+    diagonal = send(pick((0, 1), (1, 2), own, behind, far), lambda z, x, c, y: (z, 1 - x, c, 1 - y))
+    along_x = send(pick((1, 2), (0, 1), own, ahead, far), lambda z, x, c, y: (z, 1 - x, c, y))
+    held = [own, ahead, far, partner, along_y, diagonal, along_x]
+    held, work = lax.optimization_barrier((held, work))
     other = send(jnp.concatenate(held), lambda z, x, c, y: (z, x, 1 - c, y))
-    return held + [other]
-
-
-def dense_kernel(where, counts, coords, values, out, total):
-    step = pl.program_id(0)
-    slots = values.shape[0]
+    return held + [other], work
+
+
+def dense_kernel(counts, coords, values, out, tiles, total, sems):
+    steps = counts.shape[1]
+    slots = values.shape[0] // steps
     tile = values.shape[1]
-    rank = where[8]
-
-    @pl.when(step == 0)
-    def _():
-        out[...] = jnp.zeros_like(out)
-
-    total[...] = jnp.zeros_like(total)
-
-    def add(slot, carry):
-        row = coords[step * slots + slot, 0] ^ rank
-        column = coords[step * slots + slot, 1] ^ rank
-        spot = row * 2 + column
-        total[spot] = total[spot] + values[slot].astype(jnp.float32)
+    core = lax.axis_index("loop") & 1
+    rank = lax.axis_index("rep")
+
+    def fetch(step):
+        span = pl.ds(step * slots, slots)
+        return pltpu.make_async_copy(values.at[span], tiles.at[span], sems.at[step])
+
+    for step in range(steps):
+        fetch(step).start()
+    out[...] = jnp.zeros_like(out)
+
+    def one(step, carry):
+        total[...] = jnp.zeros_like(total)
+        fetch(step).wait()
+
+        def add(slot, carry):
+            row = coords[0, step * slots + slot] ^ rank
+            column = coords[1, step * slots + slot] ^ rank
+            spot = row * 2 + column
+            total[spot] = total[spot] + tiles[step * slots + slot].astype(jnp.float32)
+            return carry
+
+        lax.fori_loop(0, counts[0, step], add, 0)
+        odd = step & 1
+        there = odd * (1 - 2 * core)
+        k = jnp.where(rank == 0, step + there, 8 - step - there) >> 1
+        for column in range(2):
+            place = jnp.int32(0)
+            for i, j in enumerate(PLACES[column]):
+                place = jnp.where(k == i, j, place)
+            start = pl.multiple_of((place + HELD * odd) * tile, tile)
+            for row in range(2):
+                out[pl.ds(row * tile, tile), pl.ds(start, tile)] = total[row * 2 + column].astype(jnp.bfloat16)
         return carry
 
-    lax.fori_loop(0, counts[0, step], add, 0)
-    for row in range(2):
-        for column in range(2):
-            start = pl.multiple_of((where[step] + column * (HELD // 2)) * tile, tile)
-            out[pl.ds(row * tile, tile), pl.ds(start, tile)] = total[row * 2 + column].astype(jnp.bfloat16)
-
-
-def dense(where, tile_counts, tile_coords, tile_values):
+    lax.fori_loop(0, steps, one, 0)
+
+
+def dense(tile_counts, tile_coords, tile_values):
     steps = tile_counts.shape[1]
-    slots = tile_values.shape[0] // steps
     tile = tile_values.shape[1]
     return pl.pallas_call(
         dense_kernel,
-        grid=(steps,),
         out_shape=jax.ShapeDtypeStruct((2 * tile, 2 * HELD * tile), jnp.bfloat16),
-        in_specs=[SMEM, SMEM, SMEM, pl.BlockSpec((slots, tile, tile), lambda i: (i, 0, 0))],
-        out_specs=pl.BlockSpec((2 * tile, 2 * HELD * tile), lambda i: (0, 0)),
-        scratch_shapes=[pltpu.VMEM((4, tile, tile), jnp.float32)],
-        compiler_params=pltpu.CompilerParams(vmem_limit_bytes=24 * 1024 * 1024),
-        cost_estimate=pl.CostEstimate(flops=4_000_000, bytes_accessed=6_000_000, transcendentals=0),
-    )(where, tile_counts, tile_coords, tile_values)
+        in_specs=[SMEM, SMEM, pl.BlockSpec(memory_space=pltpu.HBM)],
+        out_specs=VMEM,
+        scratch_shapes=[
+            pltpu.VMEM(tile_values.shape, jnp.bfloat16),
+            pltpu.VMEM((4, tile, tile), jnp.float32),
+            pltpu.SemaphoreType.DMA((steps,)),
+        ],
+        compiler_params=pltpu.CompilerParams(vmem_limit_bytes=52 * 1024 * 1024),
+        cost_estimate=pl.CostEstimate(flops=4_000_000, bytes_accessed=12_000_000, transcendentals=0),
+    )(tile_counts, tile_coords.T, tile_values)
 
 
 def product_kernel(row, matrix, *refs):
@@ -152,7 +212,7 @@
         out_shape=jax.ShapeDtypeStruct((tile, width), dtype),
         in_specs=[VMEM] * (1 + len(blocks)),
         out_specs=VMEM,
-        compiler_params=pltpu.CompilerParams(vmem_limit_bytes=24 * 1024 * 1024),
+        compiler_params=pltpu.CompilerParams(vmem_limit_bytes=MIDDLE),
         cost_estimate=pl.CostEstimate(
             flops=2 * tile * matrix.shape[1] * width, bytes_accessed=2_000_000, transcendentals=0
         ),
@@ -171,21 +231,14 @@
         out_shape=jax.ShapeDtypeStruct(mine.shape, jnp.bfloat16),
         in_specs=[VMEM] * 3,
         out_specs=VMEM,
+        compiler_params=pltpu.CompilerParams(vmem_limit_bytes=SMALL),
+        cost_estimate=pl.CostEstimate(flops=17_000_000, bytes_accessed=400_000, transcendentals=0),
     )(mine, theirs, weight)
 
 
 def pairs(features, weight, tile_values, tile_coords, tile_counts):
-    planes = lax.axis_size("loop") // 4
-    core = lax.axis_index("loop") & 1
-    rank = lax.axis_index("rep")
-    steps = jnp.arange(8, dtype=jnp.int32)
-    odd = steps & 1
-    there = odd * (1 - 2 * core)
-    k = jnp.where(rank == 0, steps + there, 8 - steps - there) // 2
-    where = jnp.where(k % 2 == 0, k // 2, 3 + k // 2) + HELD * odd
-    where = jnp.concatenate([where, rank[None]]).astype(jnp.int32)
-    matrix = dense(where, tile_counts, tile_coords, tile_values)
-    blocks = spread(features, planes)
+    matrix = dense(tile_counts, tile_coords, tile_values)
+    blocks, matrix = spread(features, lax.axis_size("loop") // 4, matrix)
     theirs = products(1, matrix, blocks, jnp.bfloat16)
     theirs = lax.ppermute(theirs, "rep", [(0, 1), (1, 0)])
     mine = products(0, matrix, blocks, jnp.float32)

time: 36.7 us -> 29.4 us (0.80); the launches traced: 36.1 us -> 29.2 us
  waiting for transfers between devices: 13.3 us -> 9.7 us
  local copies, waits for them, and re-layouts: 5.52 us -> 2.27 us
  starting transfers between devices: 10.5 us -> 12.6 us
  other arithmetic: 1.88 us -> 0.01 us
    ppermute x7 -> x8, waiting for transfers between devices: 10.7 us -> 7.07 us  [send(): return lax.ppermute(value, AXES, route(planes, move))]
    unnamed x16 -> x14, local copies, waits for them, and re-layouts: 5.51 us -> 2.26 us
    ppermute x7 -> x8, starting transfers between devices: 9.75 us -> 11.3 us  [send(): return lax.ppermute(value, AXES, route(planes, move))]
    pallas_call x1, Pallas kernels: 1.8 us -> 0.8 us  [last(): pl.pallas_call(last_kernel, out_shape=jax.ShapeDtypeStruct(mine.shape, jn...]
    select_n x1 -> x0, other arithmetic: 0.92 us -> none  [spread(): jnp.where(near, jnp.concatenate([behind, far]), jnp.concatenate([own, beh...]
    concatenate x2 -> x1, other arithmetic: 0.93 us -> 0.01 us  [spread(): jnp.concatenate([behind, far])]
    pallas_call x1 -> x4, Pallas kernels: 2.34 us -> 3.01 us  [the longest x1 2.98 us: dense(): pl.pallas_call(dense_kernel, out_shape=jax.ShapeDtypeStruct((2 * tile, 2...]
    ppermute x1, starting transfers between devices: 0.77 us -> 1.33 us  [pairs(): theirs = lax.ppermute(theirs, 'rep', [(0, 1), (1, 0)])]
  transfers between devices with their start and end apart: 8 -> 9, of which waited for: 5 -> 5; matrix products, arithmetic and copies ran while one was open for 7% -> 0% of each run, Pallas kernels for 7% -> 12%
where the time goes in v2:
time: 29.4 us; the launch traced here: 29.2 us
  starting transfers between devices  12.6 us (43%)
  waiting for transfers between devices  9.7 us (33%)
  Pallas kernels  4.53 us (15%)
  local copies, waits for them, and re-layouts  2.27 us (8%)
    ppermute x8, starting transfers between devices, send(): return lax.ppermute(value, AXES, route(planes, move))  11.3 us
    ppermute x8, waiting for transfers between devices, send(): return lax.ppermute(value, AXES, route(planes, move))  7.07 us
    pallas_call x1, Pallas kernels, dense(): pl.pallas_call(dense_kernel, out_shape=jax.ShapeDtypeStruct((2 * tile, 2...  2.98 us
    ppermute x1, waiting for transfers between devices, pairs(): theirs = lax.ppermute(theirs, 'rep', [(0, 1), (1, 0)])  2.63 us
    unnamed x14, local copies, waits for them, and re-layouts  2.26 us
    ppermute x1, starting transfers between devices, pairs(): theirs = lax.ppermute(theirs, 'rep', [(0, 1), (1, 0)])  1.33 us
    pallas_call x1, Pallas kernels, last(): pl.pallas_call(last_kernel, out_shape=jax.ShapeDtypeStruct(mine.shape, jn...  0.8 us
    pallas_call x2, Pallas kernels, products(): pl.pallas_call(functools.partial(product_kernel, row), out_shape=jax.Shap...  0.72 us
  transfers between devices with their start and end apart: 9, of which 5 were waited for; matrix products, arithmetic and copies ran while one was open for 0% of the time, Pallas kernels for 12%

profile of v2, /device:TPU:0, one launch (start us, length us, event | category | flops | bytes accessed | tf_op | source)
XLA Modules:
  0.0 29.2 jit_solution(9045765960423788996)
XLA Ops:
  0.0 4.0 %collective-permute-start = (bf16[128,256]{1,0:T(8,128)(2,1)}, bf16[128,256]{1,0:T(8,128)(2,1)S(1)}, u32[]{:S(2)}, u32[]{:S(2)}) collective-permute-start(bf16[128,256]{1,0:T(8,128)(2,1)} %value.1), channel_id=1, source_target_pairs={{0,16},{1,17},{2,18},{3,19},{4,20},{5,21},{6,22},{7,23},{8,24},{9,... | collective-permute-start | bytes 196616 | tf_op jit(solution)/shard_map/ppermute | solution.py:112
  4.0 1.5 %collective-permute-start.3 = (bf16[128,256]{1,0:T(8,128)(2,1)}, bf16[128,256]{1,0:T(8,128)(2,1)S(1)}, u32[]{:S(2)}, u32[]{:S(2)}) collective-permute-start(bf16[128,256]{1,0:T(8,128)(2,1)} %value.1), channel_id=1, source_target_pairs={{0,1},{1,0},{2,3},{3,2},{4,5},{5,4},{6,7},{7,6},{8,9},{9,8},{10,11... | collective-permute-start | bytes 196616 | tf_op jit(solution)/shard_map/ppermute | solution.py:112
  5.6 1.3 %collective-permute-start.2 = (bf16[128,256]{1,0:T(8,128)(2,1)}, bf16[128,256]{1,0:T(8,128)(2,1)S(1)}, u32[]{:S(2)}, u32[]{:S(2)}) collective-permute-start(bf16[128,256]{1,0:T(8,128)(2,1)} %value.1), channel_id=1, source_target_pairs={{0,24},{1,9},{2,26},{3,11},{4,28},{5,13},{6,30},{7,15},{8,0},{9,17... | collective-permute-start | bytes 196616 | tf_op jit(solution)/shard_map/ppermute | solution.py:112
  6.9 0.7 %collective-permute-start.1 = (bf16[128,256]{1,0:T(8,128)(2,1)}, bf16[128,256]{1,0:T(8,128)(2,1)S(1)}, u32[]{:S(2)}, u32[]{:S(2)}) collective-permute-start(bf16[128,256]{1,0:T(8,128)(2,1)} %value.1), channel_id=1, source_target_pairs={{0,8},{1,25},{2,10},{3,27},{4,12},{5,29},{6,14},{7,31},{8,16},{9,1... | collective-permute-start | bytes 196616 | tf_op jit(solution)/shard_map/ppermute | solution.py:112
  7.6 0.0 copy-start.1
  7.6 0.9 %copy-done.1 = bf16[128,256]{1,0:T(8,128)(2,1)S(1)} copy-done((bf16[128,256]{1,0:T(8,128)(2,1)S(1)}, bf16[128,256]{1,0:T(8,128)(2,1)}, u32[]{:S(2)}) %copy-start.1) | copy-done | bytes 65560
  8.5 0.0 collective-permute-done.third.refs_2_
  8.5 0.0 collective-permute-done.3.refs_3_
  8.5 1.5 %collective-permute-done.2.second = bf16[128,256]{1,0:T(8,128)(2,1)S(1)} collective-permute-done((bf16[128,256]{1,0:T(8,128)(2,1)}, bf16[128,256]{1,0:T(8,128)(2,1)S(1)}, u32[]{:S(2)}, u32[]{:S(2)}) %collective-permute-start.2) | collective-permute-done | bytes 65568 | tf_op jit(solution)/shard_map/ppermute | solution.py:112
  10.0 3.1 %collective-permute-done.1.second.refs_1_ = bf16[128,256]{1,0:T(8,128)(2,1)S(1)} collective-permute-done((bf16[128,256]{1,0:T(8,128)(2,1)}, bf16[128,256]{1,0:T(8,128)(2,1)S(1)}, u32[]{:S(2)}, u32[]{:S(2)}) %collective-permute-start.1) | collective-permute-done | bytes 65568 | tf_op jit(solution)/shard_map/ppermute | solution.py:112
  13.2 1.6 %collective-permute-start.6 = (bf16[256,256]{1,0:T(8,128)(2,1)S(1)}, bf16[256,256]{1,0:T(8,128)(2,1)S(1)}, u32[]{:S(2)}, u32[]{:S(2)}) collective-permute-start(bf16[256,256]{1,0:T(8,128)(2,1)S(1)} %shard_map.57), channel_id=1, source_target_pairs={{0,4},{1,5},{2,6},{3,7},{4,0},{5,1},{6,2},{7,3},{8,12},{9,13},{10,... | collective-permute-start | bytes 393224 | tf_op jit(solution)/shard_map/ppermute | solution.py:112
  14.8 0.1 collective-permute-start.4
  14.8 2.0 %collective-permute-start.5 = (bf16[256,256]{1,0:T(8,128)(2,1)S(1)}, bf16[256,256]{1,0:T(8,128)(2,1)S(1)}, u32[]{:S(2)}, u32[]{:S(2)}) collective-permute-start(bf16[256,256]{1,0:T(8,128)(2,1)S(1)} %shard_map.56), channel_id=1, source_target_pairs={{0,5},{1,4},{2,7},{3,6},{4,1},{5,0},{6,3},{7,2},{8,13},{9,12},{10,... | collective-permute-start | bytes 393224 | tf_op jit(solution)/shard_map/ppermute | solution.py:112
  16.8 0.0 copy-start.2
  16.8 0.7 %copy-done.2 = s32[96,2]{0,1:T(2,128)S(1)} copy-done((s32[96,2]{0,1:T(2,128)S(1)}, s32[96,2]{0,1:T(2,128)}, u32[]{:S(2)}) %copy-start.2) | copy-done | bytes 792
  17.5 0.0 copy-start.3
  17.5 0.7 %copy-done.3 = s32[1,8]{1,0:T(1,128)S(1)} copy-done((s32[1,8]{1,0:T(1,128)S(1)}, s32[1,8]{1,0:T(1,128)}, u32[]{:S(2)}) %copy-start.3) | copy-done | bytes 56
  18.2 3.0 %shard_map.58.matrix = bf16[256,2560]{1,0:T(8,128)(2,1)S(1)} custom-call(s32[1,8]{1,0:T(1,128)S(1)} %copy-done.3, s32[2,96]{1,0:T(2,128)S(1)} %bitcast.1, bf16[96,128,128]{2,1,0:T(8,128)(2,1)} %values.1), custom_call_target="tpu_custom_call" | custom-call | flops 4000000 | bytes 12000000 | tf_op jit(solution)/shard_map/pallas_call | solution.py:178
  21.2 0.0 collective-permute-done.6.refs_6_
  21.2 0.3 collective-permute-done.4.refs_4_
  21.4 0.0 collective-permute-done.5.refs_5_
  21.5 0.0 copy-start
  21.6 0.1 collective-permute-start.7
  21.7 2.1 %collective-permute-done.7.refs_7_ = bf16[1280,256]{1,0:T(8,128)(2,1)S(1)} collective-permute-done((bf16[1280,256]{1,0:T(8,128)(2,1)S(1)}, bf16[1280,256]{1,0:T(8,128)(2,1)S(1)}, u32[]{:S(2)}, u32[]{:S(2)}) %collective-permute-start.7) | collective-permute-done | bytes 655392 | tf_op jit(solution)/shard_map/ppermute | solution.py:112
  23.7 0.4 %shard_map.60 = bf16[128,256]{1,0:T(8,128)(2,1)S(1)} custom-call(bf16[256,2560]{1,0:T(8,128)(2,1)S(1)} %shard_map.58.matrix, bf16[128,256]{1,0:T(8,128)(2,1)S(1)} %shard_map.55.first.refs_0_, bf16[128,256]{1,0:T(8,128)(2,1)S(1)} %collective-permute-done.1.second.refs_1_, bf16[128,256]{1,0:T(8,128)(2,1)S(1)} %collective-permute-done.third.refs_2_, ...), custom_call_target="tpu_custom_call" | custom-call | flops 167772160 | bytes 2000000 | tf_op jit(solution)/shard_map/pallas_call | solution.py:210
  24.1 1.3 %collective-permute-start.8 = (bf16[128,256]{1,0:T(8,128)(2,1)S(1)}, bf16[128,256]{1,0:T(8,128)(2,1)S(1)}, u32[]{:S(2)}, u32[]{:S(2)}) collective-permute-start(bf16[128,256]{1,0:T(8,128)(2,1)S(1)} %shard_map.60), channel_id=1, source_target_pairs={{0,1},{1,0},{2,3},{3,2},{4,5},{5,4},{6,7},{7,6},{8,9},{9,8},{10,11... | collective-permute-start | bytes 196616 | tf_op jit(solution)/shard_map/ppermute | solution.py:243
  25.4 0.4 %shard_map.59.mine = f32[128,256]{1,0:T(8,128)S(1)} custom-call(bf16[256,2560]{1,0:T(8,128)(2,1)S(1)} %shard_map.58.matrix, bf16[128,256]{1,0:T(8,128)(2,1)S(1)} %shard_map.55.first.refs_0_, bf16[128,256]{1,0:T(8,128)(2,1)S(1)} %collective-permute-done.1.second.refs_1_, bf16[128,256]{1,0:T(8,128)(2,1)S(1)} %collective-permute-done.third.refs_2_, ...), custom_call_target="tpu_custom_call" | custom-call | flops 167772160 | bytes 2000000 | tf_op jit(solution)/shard_map/pallas_call | solution.py:210
  25.8 2.6 %collective-permute-done.8.theirs = bf16[128,256]{1,0:T(8,128)(2,1)S(1)} collective-permute-done((bf16[128,256]{1,0:T(8,128)(2,1)S(1)}, bf16[128,256]{1,0:T(8,128)(2,1)S(1)}, u32[]{:S(2)}, u32[]{:S(2)}) %collective-permute-start.8) | collective-permute-done | bytes 65568 | tf_op jit(solution)/shard_map/ppermute | solution.py:243
  28.4 0.0 copy-done
  28.4 0.8 %shard_map.61 = bf16[128,256]{1,0:T(8,128)(2,1)} custom-call(f32[128,256]{1,0:T(8,128)S(1)} %shard_map.59.mine, bf16[128,256]{1,0:T(8,128)(2,1)S(1)} %collective-permute-done.8.theirs, bf16[256,256]{1,0:T(8,128)(2,1)S(1)} %copy-done), custom_call_target="tpu_custom_call" | custom-call | flops 17000000 | bytes 400000 | tf_op jit(solution)/shard_map/pallas_call | solution.py:229
  (11 shorter events, 0.1 us)
Async XLA Ops:
  0.0 8.5 %collective-permute-start = (bf16[128,256]{1,0:T(8,128)(2,1)}, bf16[128,256]{1,0:T(8,128)(2,1)S(1)}, u32[]{:S(2)}, u32[]{:S(2)}) collective-permute-start(bf16[128,256]{1,0:T(8,128)(2,1)} %value.1), channel_id=1, source_target_pairs={{0,16},{1,17},{2,18},{3,19},{4,20},{5,21},{6,22},{7,23},{8,24},{9,... | collective-permute-start | bytes 196616 | tf_op jit(solution)/shard_map/ppermute | solution.py:112
  4.0 4.5 %collective-permute-start.3 = (bf16[128,256]{1,0:T(8,128)(2,1)}, bf16[128,256]{1,0:T(8,128)(2,1)S(1)}, u32[]{:S(2)}, u32[]{:S(2)}) collective-permute-start(bf16[128,256]{1,0:T(8,128)(2,1)} %value.1), channel_id=1, source_target_pairs={{0,1},{1,0},{2,3},{3,2},{4,5},{5,4},{6,7},{7,6},{8,9},{9,8},{10,11... | collective-permute-start | bytes 196616 | tf_op jit(solution)/shard_map/ppermute | solution.py:112
  5.6 4.5 %collective-permute-start.2 = (bf16[128,256]{1,0:T(8,128)(2,1)}, bf16[128,256]{1,0:T(8,128)(2,1)S(1)}, u32[]{:S(2)}, u32[]{:S(2)}) collective-permute-start(bf16[128,256]{1,0:T(8,128)(2,1)} %value.1), channel_id=1, source_target_pairs={{0,24},{1,9},{2,26},{3,11},{4,28},{5,13},{6,30},{7,15},{8,0},{9,17... | collective-permute-start | bytes 196616 | tf_op jit(solution)/shard_map/ppermute | solution.py:112
  6.9 6.3 %collective-permute-start.1 = (bf16[128,256]{1,0:T(8,128)(2,1)}, bf16[128,256]{1,0:T(8,128)(2,1)S(1)}, u32[]{:S(2)}, u32[]{:S(2)}) collective-permute-start(bf16[128,256]{1,0:T(8,128)(2,1)} %value.1), channel_id=1, source_target_pairs={{0,8},{1,25},{2,10},{3,27},{4,12},{5,29},{6,14},{7,31},{8,16},{9,1... | collective-permute-start | bytes 196616 | tf_op jit(solution)/shard_map/ppermute | solution.py:112
  7.6 0.9 %copy-start.1 = (bf16[128,256]{1,0:T(8,128)(2,1)S(1)}, bf16[128,256]{1,0:T(8,128)(2,1)}, u32[]{:S(2)}) copy-start(bf16[128,256]{1,0:T(8,128)(2,1)} %value.1) | copy-start | bytes 196612
  13.2 8.0 %collective-permute-start.6 = (bf16[256,256]{1,0:T(8,128)(2,1)S(1)}, bf16[256,256]{1,0:T(8,128)(2,1)S(1)}, u32[]{:S(2)}, u32[]{:S(2)}) collective-permute-start(bf16[256,256]{1,0:T(8,128)(2,1)S(1)} %shard_map.57), channel_id=1, source_target_pairs={{0,4},{1,5},{2,6},{3,7},{4,0},{5,1},{6,2},{7,3},{8,12},{9,13},{10,... | collective-permute-start | bytes 393224 | tf_op jit(solution)/shard_map/ppermute | solution.py:112
  14.8 6.7 %collective-permute-start.4 = (bf16[256,256]{1,0:T(8,128)(2,1)S(1)}, bf16[256,256]{1,0:T(8,128)(2,1)S(1)}, u32[]{:S(2)}, u32[]{:S(2)}) collective-permute-start(bf16[256,256]{1,0:T(8,128)(2,1)S(1)} %pad_maximum_fusion), channel_id=1, source_target_pairs={{0,1},{1,0},{2,3},{3,2},{4,5},{5,4},{6,7},{7,6},{8,9},{9,8},{10,11... | collective-permute-start | bytes 393224 | tf_op jit(solution)/shard_map/ppermute | solution.py:112
  14.8 6.6 %collective-permute-start.5 = (bf16[256,256]{1,0:T(8,128)(2,1)S(1)}, bf16[256,256]{1,0:T(8,128)(2,1)S(1)}, u32[]{:S(2)}, u32[]{:S(2)}) collective-permute-start(bf16[256,256]{1,0:T(8,128)(2,1)S(1)} %shard_map.56), channel_id=1, source_target_pairs={{0,5},{1,4},{2,7},{3,6},{4,1},{5,0},{6,3},{7,2},{8,13},{9,12},{10,... | collective-permute-start | bytes 393224 | tf_op jit(solution)/shard_map/ppermute | solution.py:112
  16.8 0.7 %copy-start.2 = (s32[96,2]{0,1:T(2,128)S(1)}, s32[96,2]{0,1:T(2,128)}, u32[]{:S(2)}) copy-start(s32[96,2]{0,1:T(2,128)} %param.8) | copy-start | bytes 2308
  17.5 0.7 %copy-start.3 = (s32[1,8]{1,0:T(1,128)S(1)}, s32[1,8]{1,0:T(1,128)}, u32[]{:S(2)}) copy-start(s32[1,8]{1,0:T(1,128)} %counts.1) | copy-start | bytes 100
  21.5 6.9 %copy-start = (bf16[256,256]{1,0:T(8,128)(2,1)S(1)}, bf16[256,256]{1,0:T(8,128)(2,1)}, u32[]{:S(2)}) copy-start(bf16[256,256]{1,0:T(8,128)(2,1)} %weight.1) | copy-start | bytes 393220
  21.6 2.2 %collective-permute-start.7 = (bf16[1280,256]{1,0:T(8,128)(2,1)S(1)}, bf16[1280,256]{1,0:T(8,128)(2,1)S(1)}, u32[]{:S(2)}, u32[]{:S(2)}) collective-permute-start(bf16[1280,256]{1,0:T(8,128)(2,1)S(1)} %constant_dynamic-update-slice_fusion), channel_id=1, source_target_pairs={{0,2},{1,3},{2,0},{3,1},{4,6},{5,7},{6,4},{7,5},{8,10},{9,11},{10,... | collective-permute-start | bytes 1966088 | tf_op jit(solution)/shard_map/ppermute | solution.py:112
  24.1 4.3 %collective-permute-start.8 = (bf16[128,256]{1,0:T(8,128)(2,1)S(1)}, bf16[128,256]{1,0:T(8,128)(2,1)S(1)}, u32[]{:S(2)}, u32[]{:S(2)}) collective-permute-start(bf16[128,256]{1,0:T(8,128)(2,1)S(1)} %shard_map.60), channel_id=1, source_target_pairs={{0,1},{1,0},{2,3},{3,2},{4,5},{5,4},{6,7},{7,6},{8,9},{9,8},{10,11... | collective-permute-start | bytes 196616 | tf_op jit(solution)/shard_map/ppermute | solution.py:243

commit v3 on v2

--- a/solution.py
+++ b/solution.py
@@ -52,7 +52,6 @@
     return jnp.maximum(product, 0.0).astype(jnp.bfloat16)
 
 HELD = 10
-PLACES = (0, 8, 1, 9, 2), (3, 6, 4, 7, 5)
 SMALL = 4 * 1024 * 1024
 MIDDLE = 24 * 1024 * 1024
 
@@ -68,10 +67,10 @@
     return pairs
 
 
-def pick_kernel(even, odd, first, second, third, out):
+def pick_kernel(even, odd, *refs):
+    out = refs[-1]
     near = (lax.axis_index("loop") >> 1 & 1) == lax.axis_index("rep")
-    rows = first.shape[0]
-    refs = (first, second, third)
+    rows = refs[0].shape[0]
     for chosen, which in ((jnp.logical_not(near), even), (near, odd)):
 
         @pl.when(chosen)
@@ -84,50 +83,50 @@
     rows, width = blocks[0].shape
     return pl.pallas_call(
         functools.partial(pick_kernel, even, odd),
-        out_shape=jax.ShapeDtypeStruct((2 * rows, width), blocks[0].dtype),
-        in_specs=[VMEM] * 3,
+        out_shape=jax.ShapeDtypeStruct((len(even) * rows, width), blocks[0].dtype),
+        in_specs=[VMEM] * len(blocks),
         out_specs=VMEM,
         compiler_params=pltpu.CompilerParams(vmem_limit_bytes=SMALL),
         cost_estimate=pl.CostEstimate(flops=0, bytes_accessed=200_000, transcendentals=0),
     )(*blocks)
 
 
-def lift_kernel(value, out):
-    out[...] = value[...]
-
-
-def lift(value):
+def lift_kernel(*refs):
+    for value, out in zip(refs[:3], refs[3:], strict=True):
+        out[...] = value[...]
+
+
+def lift(*values):
     return pl.pallas_call(
         lift_kernel,
-        out_shape=jax.ShapeDtypeStruct(value.shape, value.dtype),
-        in_specs=[VMEM],
-        out_specs=VMEM,
+        out_shape=[jax.ShapeDtypeStruct(value.shape, value.dtype) for value in values],
+        in_specs=[VMEM] * 3,
+        out_specs=[VMEM] * 3,
         compiler_params=pltpu.CompilerParams(vmem_limit_bytes=SMALL),
         cost_estimate=pl.CostEstimate(flops=0, bytes_accessed=200_000, transcendentals=0),
-    )(value)
-
-
-def spread(features, planes, work):
+    )(*values)
+
+
+def spread(features, own, planes, matrix):
     def send(value, move):
         return lax.ppermute(value, AXES, route(planes, move))
 
     def sign(y):
         return 1 if y else -1
 
-    own = lift(features)
+    def core(z, x, c, y):
+        return z, x, 1 - c, y
+
+    behind = send(features, lambda z, x, c, y: (z + sign(y), x, c, y))
     far = send(features, lambda z, x, c, y: (z + 2, x, c, y))
-    behind = send(features, lambda z, x, c, y: (z + sign(y), x, c, y))
-    ahead = send(features, lambda z, x, c, y: (z - sign(y), x, c, y))
-    partner = send(features, lambda z, x, c, y: (z, x, c, 1 - y))
-    far, own = lax.optimization_barrier((far, own))
-    along_y = send(jnp.concatenate([behind, far]), lambda z, x, c, y: (z, x, c, 1 - y))
-    behind, partner = lax.optimization_barrier((behind, partner))
-    diagonal = send(pick((0, 1), (1, 2), own, behind, far), lambda z, x, c, y: (z, 1 - x, c, 1 - y))
+    behind, late_own = lax.optimization_barrier((behind, own))
+    ahead = send(late_own, lambda z, x, c, y: (z - sign(y), x, c, y))
+    across = send(pick((0, 1), (1, 2), own, behind, far), lambda z, x, c, y: (z, 1 - x, c, 1 - y))
+    along_y = send(pick((0, 1, 2), (0, 1, 2), own, behind, far), lambda z, x, c, y: (z, x, c, 1 - y))
     along_x = send(pick((1, 2), (0, 1), own, ahead, far), lambda z, x, c, y: (z, 1 - x, c, y))
-    held = [own, ahead, far, partner, along_y, diagonal, along_x]
-    held, work = lax.optimization_barrier((held, work))
-    other = send(jnp.concatenate(held), lambda z, x, c, y: (z, x, 1 - c, y))
-    return held + [other], work
+    held = [own, ahead, far, along_y, across, along_x]
+    held, matrix = lax.optimization_barrier((held, matrix))
+    return held + [send(jnp.concatenate(held), core)], matrix
 
 
 def dense_kernel(counts, coords, values, out, tiles, total, sems):
@@ -160,10 +159,9 @@
         odd = step & 1
         there = odd * (1 - 2 * core)
         k = jnp.where(rank == 0, step + there, 8 - step - there) >> 1
-        for column in range(2):
-            place = jnp.int32(0)
-            for i, j in enumerate(PLACES[column]):
-                place = jnp.where(k == i, j, place)
+        half = k >> 1
+        places = (jnp.where(k & 1 == 1, 8, 0) + half, jnp.where(k & 1 == 1, 6, 3) + half)
+        for column, place in enumerate(places):
             start = pl.multiple_of((place + HELD * odd) * tile, tile)
             for row in range(2):
                 out[pl.ds(row * tile, tile), pl.ds(start, tile)] = total[row * 2 + column].astype(jnp.bfloat16)
@@ -187,7 +185,7 @@
         ],
         compiler_params=pltpu.CompilerParams(vmem_limit_bytes=52 * 1024 * 1024),
         cost_estimate=pl.CostEstimate(flops=4_000_000, bytes_accessed=12_000_000, transcendentals=0),
-    )(tile_counts, tile_coords.T, tile_values)
+    )(tile_counts, tile_coords, tile_values)
 
 
 def product_kernel(row, matrix, *refs):
@@ -237,8 +235,9 @@
 
 
 def pairs(features, weight, tile_values, tile_coords, tile_counts):
+    own, tile_counts, tile_coords = lift(features, tile_counts, tile_coords.T)
     matrix = dense(tile_counts, tile_coords, tile_values)
-    blocks, matrix = spread(features, lax.axis_size("loop") // 4, matrix)
+    blocks, matrix = spread(features, own, lax.axis_size("loop") // 4, matrix)
     theirs = products(1, matrix, blocks, jnp.bfloat16)
     theirs = lax.ppermute(theirs, "rep", [(0, 1), (1, 0)])
     mine = products(0, matrix, blocks, jnp.float32)

time: 29.4 us -> 27.3 us (0.929)
  waiting for transfers between devices: 9.7 us -> 7.68 us
    ppermute x8 -> x7, waiting for transfers between devices: 7.07 us -> 5.52 us  [send(): return lax.ppermute(value, AXES, route(planes, move))]
    ppermute x8 -> x7, starting transfers between devices: 11.3 us -> 10.7 us  [send(): return lax.ppermute(value, AXES, route(planes, move))]
    ppermute x1, starting transfers between devices: 1.33 us -> 1.81 us  [pairs(): theirs = lax.ppermute(theirs, 'rep', [(0, 1), (1, 0)])]
    ppermute x1, waiting for transfers between devices: 2.63 us -> 2.16 us  [pairs(): theirs = lax.ppermute(theirs, 'rep', [(0, 1), (1, 0)])]
    unnamed x14 -> x13, local copies, waits for them, and re-layouts: 2.26 us -> 2.29 us
  transfers between devices with their start and end apart: 9 -> 8, of which waited for: 5 -> 8; matrix products, arithmetic and copies ran while one was open for 0% -> 0% of each run, Pallas kernels for 12% -> 12%
where the time goes in v3:
time: 27.3 us; the launch traced here: 27.1 us
  starting transfers between devices  12.5 us (46%)
  waiting for transfers between devices  7.68 us (28%)
  Pallas kernels  4.52 us (17%)
  local copies, waits for them, and re-layouts  2.3 us (8%)
    ppermute x7, starting transfers between devices, send(): return lax.ppermute(value, AXES, route(planes, move))  10.7 us
    ppermute x7, waiting for transfers between devices, send(): return lax.ppermute(value, AXES, route(planes, move))  5.52 us
    pallas_call x1, Pallas kernels, dense(): pl.pallas_call(dense_kernel, out_shape=jax.ShapeDtypeStruct((2 * tile, 2...  2.97 us
    unnamed x13, local copies, waits for them, and re-layouts  2.29 us
    ppermute x1, waiting for transfers between devices, pairs(): theirs = lax.ppermute(theirs, 'rep', [(0, 1), (1, 0)])  2.16 us
    ppermute x1, starting transfers between devices, pairs(): theirs = lax.ppermute(theirs, 'rep', [(0, 1), (1, 0)])  1.81 us
    pallas_call x1, Pallas kernels, last(): pl.pallas_call(last_kernel, out_shape=jax.ShapeDtypeStruct(mine.shape, jn...  0.8 us
    pallas_call x2, Pallas kernels, products(): pl.pallas_call(functools.partial(product_kernel, row), out_shape=jax.Shap...  0.71 us
  transfers between devices with their start and end apart: 8, of which 8 were waited for; matrix products, arithmetic and copies ran while one was open for 0% of the time, Pallas kernels for 12%

profile of v3, /device:TPU:0, one launch (start us, length us, event | category | flops | bytes accessed | tf_op | source)
XLA Modules:
  0.0 27.1 jit_solution(16245449585302269619)
XLA Ops:
  0.0 5.0 %collective-permute-start = (bf16[128,256]{1,0:T(8,128)(2,1)}, bf16[128,256]{1,0:T(8,128)(2,1)S(1)}, u32[]{:S(2)}, u32[]{:S(2)}) collective-permute-start(bf16[128,256]{1,0:T(8,128)(2,1)} %refs_0_.1), channel_id=1, source_target_pairs={{0,24},{1,9},{2,26},{3,11},{4,28},{5,13},{6,30},{7,15},{8,0},{9,17... | collective-permute-start | bytes 196616 | tf_op jit(solution)/shard_map/ppermute | solution.py:112
  5.0 0.0 collective-permute-start.2
  5.1 0.0 copy-start.1
  5.1 0.9 %copy-done.1 = bf16[128,256]{1,0:T(8,128)(2,1)S(1)} copy-done((bf16[128,256]{1,0:T(8,128)(2,1)S(1)}, bf16[128,256]{1,0:T(8,128)(2,1)}, u32[]{:S(2)}) %copy-start.1) | copy-done | bytes 65560
  6.0 0.0 copy-start.2
  6.0 0.7 %copy-done.2 = s32[96,2]{0,1:T(2,128)S(1)} copy-done((s32[96,2]{0,1:T(2,128)S(1)}, s32[96,2]{0,1:T(2,128)}, u32[]{:S(2)}) %copy-start.2) | copy-done | bytes 792
  6.6 0.0 copy-start.3
  6.6 0.7 %copy-done.3 = s32[1,8]{1,0:T(1,128)S(1)} copy-done((s32[1,8]{1,0:T(1,128)S(1)}, s32[1,8]{1,0:T(1,128)}, u32[]{:S(2)}) %copy-start.3) | copy-done | bytes 56
  7.3 0.1 collective-permute-done.refs_1_
  7.4 0.9 %collective-permute-start.1 = (bf16[128,256]{1,0:T(8,128)(2,1)S(1)}, bf16[128,256]{1,0:T(8,128)(2,1)S(1)}, u32[]{:S(2)}, u32[]{:S(2)}) collective-permute-start(bf16[128,256]{1,0:T(8,128)(2,1)S(1)} %get-tuple-element.23.refs_0_), channel_id=1, source_target_pairs={{0,8},{1,25},{2,10},{3,27},{4,12},{5,29},{6,14},{7,31},{8,16},{9,1... | collective-permute-start | bytes 196616 | tf_op jit(solution)/shard_map/ppermute | solution.py:112
  8.3 2.1 %collective-permute-done.2.refs_2_ = bf16[128,256]{1,0:T(8,128)(2,1)S(1)} collective-permute-done((bf16[128,256]{1,0:T(8,128)(2,1)}, bf16[128,256]{1,0:T(8,128)(2,1)S(1)}, u32[]{:S(2)}, u32[]{:S(2)}) %collective-permute-start.2) | collective-permute-done | bytes 65568 | tf_op jit(solution)/shard_map/ppermute | solution.py:112
  10.4 1.7 %collective-permute-start.3 = (bf16[384,256]{1,0:T(8,128)(2,1)S(1)}, bf16[384,256]{1,0:T(8,128)(2,1)S(1)}, u32[]{:S(2)}, u32[]{:S(2)}) collective-permute-start(bf16[384,256]{1,0:T(8,128)(2,1)S(1)} %shard_map.56), channel_id=1, source_target_pairs={{0,1},{1,0},{2,3},{3,2},{4,5},{5,4},{6,7},{7,6},{8,9},{9,8},{10,11... | collective-permute-start | bytes 589832 | tf_op jit(solution)/shard_map/ppermute | solution.py:112
  12.2 1.3 %collective-permute-start.4 = (bf16[256,256]{1,0:T(8,128)(2,1)S(1)}, bf16[256,256]{1,0:T(8,128)(2,1)S(1)}, u32[]{:S(2)}, u32[]{:S(2)}) collective-permute-start(bf16[256,256]{1,0:T(8,128)(2,1)S(1)} %shard_map.57), channel_id=1, source_target_pairs={{0,5},{1,4},{2,7},{3,6},{4,1},{5,0},{6,3},{7,2},{8,13},{9,12},{10,... | collective-permute-start | bytes 393224 | tf_op jit(solution)/shard_map/ppermute | solution.py:112
  13.5 0.4 %collective-permute-done.1.refs_1_ = bf16[128,256]{1,0:T(8,128)(2,1)S(1)} collective-permute-done((bf16[128,256]{1,0:T(8,128)(2,1)S(1)}, bf16[128,256]{1,0:T(8,128)(2,1)S(1)}, u32[]{:S(2)}, u32[]{:S(2)}) %collective-permute-start.1) | collective-permute-done | bytes 65568 | tf_op jit(solution)/shard_map/ppermute | solution.py:112
  13.9 1.6 %collective-permute-start.5 = (bf16[256,256]{1,0:T(8,128)(2,1)S(1)}, bf16[256,256]{1,0:T(8,128)(2,1)S(1)}, u32[]{:S(2)}, u32[]{:S(2)}) collective-permute-start(bf16[256,256]{1,0:T(8,128)(2,1)S(1)} %shard_map.58), channel_id=1, source_target_pairs={{0,4},{1,5},{2,6},{3,7},{4,0},{5,1},{6,2},{7,3},{8,12},{9,13},{10,... | collective-permute-start | bytes 393224 | tf_op jit(solution)/shard_map/ppermute | solution.py:112
  15.5 3.0 %shard_map.59.matrix = bf16[256,2560]{1,0:T(8,128)(2,1)S(1)} custom-call(s32[1,8]{1,0:T(1,128)S(1)} %get-tuple-element.20.counts, s32[2,96]{1,0:T(2,128)S(1)} %get-tuple-element.21.coords, bf16[96,128,128]{2,1,0:T(8,128)(2,1)} %values.1), custom_call_target="tpu_custom_call" | custom-call | flops 4000000 | bytes 12000000 | tf_op jit(solution)/shard_map/pallas_call | solution.py:176
  18.5 0.6 %collective-permute-done.4.refs_4_ = bf16[256,256]{1,0:T(8,128)(2,1)S(1)} collective-permute-done((bf16[256,256]{1,0:T(8,128)(2,1)S(1)}, bf16[256,256]{1,0:T(8,128)(2,1)S(1)}, u32[]{:S(2)}, u32[]{:S(2)}) %collective-permute-start.4) | collective-permute-done | bytes 131104 | tf_op jit(solution)/shard_map/ppermute | solution.py:112
  19.1 0.1 collective-permute-done.5.refs_5_
  19.3 0.1 collective-permute-done.3.refs_3_
  19.4 0.0 copy-start
  19.4 0.1 collective-permute-start.6
  19.5 2.1 %collective-permute-done.6.refs_6_ = bf16[1280,256]{1,0:T(8,128)(2,1)S(1)} collective-permute-done((bf16[1280,256]{1,0:T(8,128)(2,1)S(1)}, bf16[1280,256]{1,0:T(8,128)(2,1)S(1)}, u32[]{:S(2)}, u32[]{:S(2)}) %collective-permute-start.6) | collective-permute-done | bytes 655392 | tf_op jit(solution)/shard_map/ppermute | solution.py:112
  21.6 0.4 %shard_map.61 = bf16[128,256]{1,0:T(8,128)(2,1)S(1)} custom-call(bf16[256,2560]{1,0:T(8,128)(2,1)S(1)} %shard_map.59.matrix, bf16[128,256]{1,0:T(8,128)(2,1)S(1)} %get-tuple-element.23.refs_0_, bf16[128,256]{1,0:T(8,128)(2,1)S(1)} %collective-permute-done.1.refs_1_, bf16[128,256]{1,0:T(8,128)(2,1)S(1)} %collective-permute-done.2.refs_2_, ...), custom_call_target="tpu_custom_call" | custom-call | flops 167772160 | bytes 2000000 | tf_op jit(solution)/shard_map/pallas_call | solution.py:208
  22.0 1.8 %collective-permute-start.7 = (bf16[128,256]{1,0:T(8,128)(2,1)S(1)}, bf16[128,256]{1,0:T(8,128)(2,1)S(1)}, u32[]{:S(2)}, u32[]{:S(2)}) collective-permute-start(bf16[128,256]{1,0:T(8,128)(2,1)S(1)} %shard_map.61), channel_id=1, source_target_pairs={{0,1},{1,0},{2,3},{3,2},{4,5},{5,4},{6,7},{7,6},{8,9},{9,8},{10,11... | collective-permute-start | bytes 196616 | tf_op jit(solution)/shard_map/ppermute | solution.py:242
  23.8 0.4 %shard_map.60.mine = f32[128,256]{1,0:T(8,128)S(1)} custom-call(bf16[256,2560]{1,0:T(8,128)(2,1)S(1)} %shard_map.59.matrix, bf16[128,256]{1,0:T(8,128)(2,1)S(1)} %get-tuple-element.23.refs_0_, bf16[128,256]{1,0:T(8,128)(2,1)S(1)} %collective-permute-done.1.refs_1_, bf16[128,256]{1,0:T(8,128)(2,1)S(1)} %collective-permute-done.2.refs_2_, ...), custom_call_target="tpu_custom_call" | custom-call | flops 167772160 | bytes 2000000 | tf_op jit(solution)/shard_map/pallas_call | solution.py:208
  24.1 2.2 %collective-permute-done.7.theirs = bf16[128,256]{1,0:T(8,128)(2,1)S(1)} collective-permute-done((bf16[128,256]{1,0:T(8,128)(2,1)S(1)}, bf16[128,256]{1,0:T(8,128)(2,1)S(1)}, u32[]{:S(2)}, u32[]{:S(2)}) %collective-permute-start.7) | collective-permute-done | bytes 65568 | tf_op jit(solution)/shard_map/ppermute | solution.py:242
  26.3 0.0 copy-done
  26.3 0.8 %shard_map.62 = bf16[128,256]{1,0:T(8,128)(2,1)} custom-call(f32[128,256]{1,0:T(8,128)S(1)} %shard_map.60.mine, bf16[128,256]{1,0:T(8,128)(2,1)S(1)} %collective-permute-done.7.theirs, bf16[256,256]{1,0:T(8,128)(2,1)S(1)} %copy-done), custom_call_target="tpu_custom_call" | custom-call | flops 17000000 | bytes 400000 | tf_op jit(solution)/shard_map/pallas_call | solution.py:227
  (10 shorter events, 0.1 us)
Async XLA Ops:
  0.0 7.4 %collective-permute-start = (bf16[128,256]{1,0:T(8,128)(2,1)}, bf16[128,256]{1,0:T(8,128)(2,1)S(1)}, u32[]{:S(2)}, u32[]{:S(2)}) collective-permute-start(bf16[128,256]{1,0:T(8,128)(2,1)} %refs_0_.1), channel_id=1, source_target_pairs={{0,24},{1,9},{2,26},{3,11},{4,28},{5,13},{6,30},{7,15},{8,0},{9,17... | collective-permute-start | bytes 196616 | tf_op jit(solution)/shard_map/ppermute | solution.py:112
  5.0 5.4 %collective-permute-start.2 = (bf16[128,256]{1,0:T(8,128)(2,1)}, bf16[128,256]{1,0:T(8,128)(2,1)S(1)}, u32[]{:S(2)}, u32[]{:S(2)}) collective-permute-start(bf16[128,256]{1,0:T(8,128)(2,1)} %refs_0_.1), channel_id=1, source_target_pairs={{0,16},{1,17},{2,18},{3,19},{4,20},{5,21},{6,22},{7,23},{8,24},{9,... | collective-permute-start | bytes 196616 | tf_op jit(solution)/shard_map/ppermute | solution.py:112
  5.1 0.9 %copy-start.1 = (bf16[128,256]{1,0:T(8,128)(2,1)S(1)}, bf16[128,256]{1,0:T(8,128)(2,1)}, u32[]{:S(2)}) copy-start(bf16[128,256]{1,0:T(8,128)(2,1)} %refs_0_.1) | copy-start | bytes 196612
  6.0 0.7 %copy-start.2 = (s32[96,2]{0,1:T(2,128)S(1)}, s32[96,2]{0,1:T(2,128)}, u32[]{:S(2)}) copy-start(s32[96,2]{0,1:T(2,128)} %param.8) | copy-start | bytes 2308
  6.6 0.7 %copy-start.3 = (s32[1,8]{1,0:T(1,128)S(1)}, s32[1,8]{1,0:T(1,128)}, u32[]{:S(2)}) copy-start(s32[1,8]{1,0:T(1,128)} %refs_1_.1) | copy-start | bytes 100
  7.4 6.5 %collective-permute-start.1 = (bf16[128,256]{1,0:T(8,128)(2,1)S(1)}, bf16[128,256]{1,0:T(8,128)(2,1)S(1)}, u32[]{:S(2)}, u32[]{:S(2)}) collective-permute-start(bf16[128,256]{1,0:T(8,128)(2,1)S(1)} %get-tuple-element.23.refs_0_), channel_id=1, source_target_pairs={{0,8},{1,25},{2,10},{3,27},{4,12},{5,29},{6,14},{7,31},{8,16},{9,1... | collective-permute-start | bytes 196616 | tf_op jit(solution)/shard_map/ppermute | solution.py:112
  10.4 8.9 %collective-permute-start.3 = (bf16[384,256]{1,0:T(8,128)(2,1)S(1)}, bf16[384,256]{1,0:T(8,128)(2,1)S(1)}, u32[]{:S(2)}, u32[]{:S(2)}) collective-permute-start(bf16[384,256]{1,0:T(8,128)(2,1)S(1)} %shard_map.56), channel_id=1, source_target_pairs={{0,1},{1,0},{2,3},{3,2},{4,5},{5,4},{6,7},{7,6},{8,9},{9,8},{10,11... | collective-permute-start | bytes 589832 | tf_op jit(solution)/shard_map/ppermute | solution.py:112
  12.2 6.9 %collective-permute-start.4 = (bf16[256,256]{1,0:T(8,128)(2,1)S(1)}, bf16[256,256]{1,0:T(8,128)(2,1)S(1)}, u32[]{:S(2)}, u32[]{:S(2)}) collective-permute-start(bf16[256,256]{1,0:T(8,128)(2,1)S(1)} %shard_map.57), channel_id=1, source_target_pairs={{0,5},{1,4},{2,7},{3,6},{4,1},{5,0},{6,3},{7,2},{8,13},{9,12},{10,... | collective-permute-start | bytes 393224 | tf_op jit(solution)/shard_map/ppermute | solution.py:112
  13.9 5.3 %collective-permute-start.5 = (bf16[256,256]{1,0:T(8,128)(2,1)S(1)}, bf16[256,256]{1,0:T(8,128)(2,1)S(1)}, u32[]{:S(2)}, u32[]{:S(2)}) collective-permute-start(bf16[256,256]{1,0:T(8,128)(2,1)S(1)} %shard_map.58), channel_id=1, source_target_pairs={{0,4},{1,5},{2,6},{3,7},{4,0},{5,1},{6,2},{7,3},{8,12},{9,13},{10,... | collective-permute-start | bytes 393224 | tf_op jit(solution)/shard_map/ppermute | solution.py:112
  19.4 6.9 %copy-start = (bf16[256,256]{1,0:T(8,128)(2,1)S(1)}, bf16[256,256]{1,0:T(8,128)(2,1)}, u32[]{:S(2)}) copy-start(bf16[256,256]{1,0:T(8,128)(2,1)} %weight.1) | copy-start | bytes 393220
  19.4 2.2 %collective-permute-start.6 = (bf16[1280,256]{1,0:T(8,128)(2,1)S(1)}, bf16[1280,256]{1,0:T(8,128)(2,1)S(1)}, u32[]{:S(2)}, u32[]{:S(2)}) collective-permute-start(bf16[1280,256]{1,0:T(8,128)(2,1)S(1)} %constant_dynamic-update-slice_fusion), channel_id=1, source_target_pairs={{0,2},{1,3},{2,0},{3,1},{4,6},{5,7},{6,4},{7,5},{8,10},{9,11},{10,... | collective-permute-start | bytes 1966088 | tf_op jit(solution)/shard_map/ppermute | solution.py:112
  22.0 4.3 %collective-permute-start.7 = (bf16[128,256]{1,0:T(8,128)(2,1)S(1)}, bf16[128,256]{1,0:T(8,128)(2,1)S(1)}, u32[]{:S(2)}, u32[]{:S(2)}) collective-permute-start(bf16[128,256]{1,0:T(8,128)(2,1)S(1)} %shard_map.61), channel_id=1, source_target_pairs={{0,1},{1,0},{2,3},{3,2},{4,5},{5,4},{6,7},{7,6},{8,9},{9,8},{10,11... | collective-permute-start | bytes 196616 | tf_op jit(solution)/shard_map/ppermute | solution.py:242

commit v4 on v3

--- a/solution.py
+++ b/solution.py
@@ -51,7 +51,8 @@
     product = jnp.dot(aggregated, weight, preferred_element_type=jnp.float32)
     return jnp.maximum(product, 0.0).astype(jnp.bfloat16)
 
-HELD = 10
+HELD = 12
+SENT = 10
 SMALL = 4 * 1024 * 1024
 MIDDLE = 24 * 1024 * 1024
 
@@ -70,25 +71,81 @@
 def pick_kernel(even, odd, *refs):
     out = refs[-1]
     near = (lax.axis_index("loop") >> 1 & 1) == lax.axis_index("rep")
-    rows = refs[0].shape[0]
     for chosen, which in ((jnp.logical_not(near), even), (near, odd)):
 
         @pl.when(chosen)
         def _(which=which):
-            for i, j in enumerate(which):
-                out[pl.ds(i * rows, rows)] = refs[j][...]
+            start = 0
+            for j in which:
+                rows = refs[j].shape[0]
+                out[pl.ds(start, rows)] = refs[j][...]
+                start += rows
 
 
 def pick(even, odd, *blocks):
-    rows, width = blocks[0].shape
+    width = blocks[0].shape[1]
+    rows = sum(blocks[j].shape[0] for j in even)
     return pl.pallas_call(
         functools.partial(pick_kernel, even, odd),
-        out_shape=jax.ShapeDtypeStruct((len(even) * rows, width), blocks[0].dtype),
+        out_shape=jax.ShapeDtypeStruct((rows, width), blocks[0].dtype),
         in_specs=[VMEM] * len(blocks),
         out_specs=VMEM,
         compiler_params=pltpu.CompilerParams(vmem_limit_bytes=SMALL),
         cost_estimate=pl.CostEstimate(flops=0, bytes_accessed=200_000, transcendentals=0),
     )(*blocks)
+
+
+def pair_kernel(own, mate, mark, out):
+    core = lax.axis_index("loop") & 1
+    rows = own.shape[0]
+    out[pl.ds(pl.multiple_of(core * rows, rows), rows)] = own[...]
+    out[pl.ds(pl.multiple_of((1 - core) * rows, rows), rows)] = mate[...]
+
+
+def pair(own, mate, mark):
+    return pl.pallas_call(
+        pair_kernel,
+        out_shape=jax.ShapeDtypeStruct((2 * own.shape[0], own.shape[1]), own.dtype),
+        in_specs=[VMEM] * 3,
+        out_specs=VMEM,
+        compiler_params=pltpu.CompilerParams(vmem_limit_bytes=SMALL),
+        cost_estimate=pl.CostEstimate(flops=0, bytes_accessed=200_000, transcendentals=0),
+    )(own, mate, mark)
+
+
+def mark_kernel(*refs):
+    refs[-1][...] = refs[0][pl.ds(0, 16), pl.ds(0, 128)]
+
+
+def mark(cost, *values):
+    return pl.pallas_call(
+        mark_kernel,
+        out_shape=jax.ShapeDtypeStruct((16, 128), values[0].dtype),
+        in_specs=[VMEM] * len(values),
+        out_specs=VMEM,
+        compiler_params=pltpu.CompilerParams(vmem_limit_bytes=SMALL),
+        cost_estimate=pl.CostEstimate(flops=cost, bytes_accessed=4096, transcendentals=0),
+    )(*values)
+
+
+def pack_kernel(*refs):
+    out = refs[-1]
+    start = 0
+    for block in refs[:-2]:
+        out[pl.ds(start, block.shape[0])] = block[...]
+        start += block.shape[0]
+
+
+def pack(blocks, mark):
+    rows = sum(block.shape[0] for block in blocks)
+    return pl.pallas_call(
+        pack_kernel,
+        out_shape=jax.ShapeDtypeStruct((rows, blocks[0].shape[1]), blocks[0].dtype),
+        in_specs=[VMEM] * (len(blocks) + 1),
+        out_specs=VMEM,
+        compiler_params=pltpu.CompilerParams(vmem_limit_bytes=SMALL),
+        cost_estimate=pl.CostEstimate(flops=0, bytes_accessed=1_300_000, transcendentals=0),
+    )(*blocks, mark)
 
 
 def lift_kernel(*refs):
@@ -107,7 +164,7 @@
     )(*values)
 
 
-def spread(features, own, planes, matrix):
+def spread(features, own, planes, counts, coords, tile_values):
     def send(value, move):
         return lax.ppermute(value, AXES, route(planes, move))
 
@@ -119,14 +176,21 @@
 
     behind = send(features, lambda z, x, c, y: (z + sign(y), x, c, y))
     far = send(features, lambda z, x, c, y: (z + 2, x, c, y))
-    behind, late_own = lax.optimization_barrier((behind, own))
-    ahead = send(late_own, lambda z, x, c, y: (z - sign(y), x, c, y))
+    mate = send(features, core)
+    both = pair(own, mate, mark(4_000_000_000, behind))
+    ahead = send(both, lambda z, x, c, y: (z - sign(y), x, c, y) if c else (z, x, c, 1 - y))
+    along_y = send(pick((0, 1), (0, 1), behind, far), lambda z, x, c, y: (z, x, c, 1 - y))
     across = send(pick((0, 1), (1, 2), own, behind, far), lambda z, x, c, y: (z, 1 - x, c, 1 - y))
-    along_y = send(pick((0, 1, 2), (0, 1, 2), own, behind, far), lambda z, x, c, y: (z, x, c, 1 - y))
-    along_x = send(pick((1, 2), (0, 1), own, ahead, far), lambda z, x, c, y: (z, 1 - x, c, y))
-    held = [own, ahead, far, along_y, across, along_x]
-    held, matrix = lax.optimization_barrier((held, matrix))
-    return held + [send(jnp.concatenate(held), core)], matrix
+    along_x = send(pick((1,), (0,), own, far), lambda z, x, c, y: (z, 1 - x, c, y))
+    ahead, counts, coords = lax.optimization_barrier((ahead, counts, coords))
+    matrix = dense(counts, coords, tile_values)
+    beside = send(ahead, lambda z, x, c, y: (z, 1 - x, c, y) if c else (z, x, c, y))
+    sent = [far, along_y, across, along_x, ahead, beside]
+    held = [own, mate] + sent
+    arrived = mark(4_000_000_000, along_y, across, along_x, matrix)
+    sent, held, matrix = lax.optimization_barrier((sent, held, matrix))
+    other = send(pack(sent, arrived), core)
+    return [other], matrix, first_products(matrix, held)
 
 
 def dense_kernel(counts, coords, values, out, tiles, total, sems):
@@ -160,9 +224,19 @@
         there = odd * (1 - 2 * core)
         k = jnp.where(rank == 0, step + there, 8 - step - there) >> 1
         half = k >> 1
-        places = (jnp.where(k & 1 == 1, 8, 0) + half, jnp.where(k & 1 == 1, 6, 3) + half)
+        parity = core ^ odd
+        other = 1 - core
+        near = (lax.axis_index("loop") >> 1 & 1) == rank
+        paired = 8 + parity + SENT * other
+        straight = jnp.where(k == 2, paired, jnp.where(k == 0, odd, 2 + SENT * odd))
+        beside = jnp.where((k == 1) == near, paired + 2, 7 + SENT * odd)
+        turned = jnp.where(k == 0, 8 + parity + SENT * core, 2 + half + SENT * odd)
+        places = (
+            jnp.where(k & 1 == 1, beside, straight),
+            jnp.where(k & 1 == 1, 5 + half + SENT * odd, turned),
+        )
         for column, place in enumerate(places):
-            start = pl.multiple_of((place + HELD * odd) * tile, tile)
+            start = pl.multiple_of(place * tile, tile)
             for row in range(2):
                 out[pl.ds(row * tile, tile), pl.ds(start, tile)] = total[row * 2 + column].astype(jnp.bfloat16)
         return carry
@@ -175,7 +249,7 @@
     tile = tile_values.shape[1]
     return pl.pallas_call(
         dense_kernel,
-        out_shape=jax.ShapeDtypeStruct((2 * tile, 2 * HELD * tile), jnp.bfloat16),
+        out_shape=jax.ShapeDtypeStruct((2 * tile, (HELD + SENT) * tile), jnp.bfloat16),
         in_specs=[SMEM, SMEM, pl.BlockSpec(memory_space=pltpu.HBM)],
         out_specs=VMEM,
         scratch_shapes=[
@@ -188,33 +262,50 @@
     )(tile_counts, tile_coords, tile_values)
 
 
-def product_kernel(row, matrix, *refs):
+def dots(rows, start, matrix, blocks, total):
+    for block in blocks:
+        depth = block.shape[0]
+        part = matrix[rows, pl.ds(start, depth)]
+        total += jnp.dot(part, block[...], preferred_element_type=jnp.float32)
+        start += depth
+    return total
+
+
+def first_kernel(matrix, *refs):
+    out = refs[-1]
+    out[...] = dots(pl.ds(0, out.shape[0]), 0, matrix, refs[:-1], jnp.zeros(out.shape, jnp.float32))
+
+
+def first_products(matrix, blocks):
+    width = blocks[0].shape[1]
+    return pl.pallas_call(
+        first_kernel,
+        out_shape=jax.ShapeDtypeStruct((matrix.shape[0], width), jnp.float32),
+        in_specs=[VMEM] * (1 + len(blocks)),
+        out_specs=VMEM,
+        compiler_params=pltpu.CompilerParams(vmem_limit_bytes=MIDDLE),
+        cost_estimate=pl.CostEstimate(flops=268_000_000, bytes_accessed=2_000_000, transcendentals=0),
+    )(matrix, *blocks)
+
+
+def product_kernel(row, matrix, sums, *refs):
     out = refs[-1]
     tile = out.shape[0]
-    total = jnp.zeros(out.shape, jnp.float32)
-    start = 0
-    for ref in refs[:-1]:
-        depth = ref.shape[0]
-        total += jnp.dot(
-            matrix[pl.ds(row * tile, tile), pl.ds(start, depth)], ref[...], preferred_element_type=jnp.float32
-        )
-        start += depth
-    out[...] = total.astype(out.dtype)
-
-
-def products(row, matrix, blocks, dtype):
+    rows = pl.ds(row * tile, tile)
+    out[...] = dots(rows, HELD * tile, matrix, refs[:-1], sums[rows]).astype(out.dtype)
+
+
+def products(row, matrix, sums, blocks, dtype):
     tile = matrix.shape[0] // 2
     width = blocks[0].shape[1]
     return pl.pallas_call(
         functools.partial(product_kernel, row),
         out_shape=jax.ShapeDtypeStruct((tile, width), dtype),
-        in_specs=[VMEM] * (1 + len(blocks)),
+        in_specs=[VMEM] * (2 + len(blocks)),
         out_specs=VMEM,
         compiler_params=pltpu.CompilerParams(vmem_limit_bytes=MIDDLE),
-        cost_estimate=pl.CostEstimate(
-            flops=2 * tile * matrix.shape[1] * width, bytes_accessed=2_000_000, transcendentals=0
-        ),
-    )(matrix, *blocks)
+        cost_estimate=pl.CostEstimate(flops=100_000_000, bytes_accessed=2_000_000, transcendentals=0),
+    )(matrix, sums, *blocks)
 
 
 def last_kernel(mine, theirs, weight, out):
@@ -236,11 +327,11 @@
 
 def pairs(features, weight, tile_values, tile_coords, tile_counts):
     own, tile_counts, tile_coords = lift(features, tile_counts, tile_coords.T)
-    matrix = dense(tile_counts, tile_coords, tile_values)
-    blocks, matrix = spread(features, own, lax.axis_size("loop") // 4, matrix)
-    theirs = products(1, matrix, blocks, jnp.bfloat16)
+    planes = lax.axis_size("loop") // 4
+    blocks, matrix, sums = spread(features, own, planes, tile_counts, tile_coords, tile_values)
+    theirs = products(1, matrix, sums, blocks, jnp.bfloat16)
     theirs = lax.ppermute(theirs, "rep", [(0, 1), (1, 0)])
-    mine = products(0, matrix, blocks, jnp.float32)
+    mine = products(0, matrix, sums, blocks, jnp.float32)
     return last(mine, theirs, weight)
 
 

time: 27.3 us -> 26.7 us (0.978)
  waiting for transfers between devices: 7.68 us -> 5.71 us
  starting transfers between devices: 12.5 us -> 14.1 us
    ppermute x7 -> x9, waiting for transfers between devices: 5.52 us -> 3.25 us  [send(): return lax.ppermute(value, AXES, route(planes, move))]
    ppermute x7 -> x9, starting transfers between devices: 10.7 us -> 12.4 us  [send(): return lax.ppermute(value, AXES, route(planes, move))]
    ppermute x1, waiting for transfers between devices: 2.16 us -> 2.46 us  [pairs(): theirs = lax.ppermute(theirs, 'rep', [(0, 1), (1, 0)])]
    unnamed x13 -> x8, local copies, waits for them, and re-layouts: 2.29 us -> 2.24 us
    pallas_call x1 -> x6, Pallas kernels: 2.97 us -> 3 us  [the longest x1 2.52 us: dense(): pl.pallas_call(dense_kernel, out_shape=jax.ShapeDtypeStruct((2 * tile, (H...]
  transfers between devices with their start and end apart: 8 -> 10, of which waited for: 8 -> 6; matrix products, arithmetic and copies ran while one was open for 0% -> 0% of each run, Pallas kernels for 12% -> 12%
where the time goes in v4:
time: 26.7 us; the launch traced here: 26.5 us
  starting transfers between devices  14.1 us (53%)
  waiting for transfers between devices  5.71 us (21%)
  Pallas kernels  4.35 us (16%)
  local copies, waits for them, and re-layouts  2.24 us (8%)
    ppermute x9, starting transfers between devices, send(): return lax.ppermute(value, AXES, route(planes, move))  12.4 us
    ppermute x9, waiting for transfers between devices, send(): return lax.ppermute(value, AXES, route(planes, move))  3.25 us
    pallas_call x1, Pallas kernels, dense(): pl.pallas_call(dense_kernel, out_shape=jax.ShapeDtypeStruct((2 * tile, (H...  2.52 us
    ppermute x1, waiting for transfers between devices, pairs(): theirs = lax.ppermute(theirs, 'rep', [(0, 1), (1, 0)])  2.46 us
    unnamed x8, local copies, waits for them, and re-layouts  2.24 us
    ppermute x1, starting transfers between devices, pairs(): theirs = lax.ppermute(theirs, 'rep', [(0, 1), (1, 0)])  1.71 us
    pallas_call x1, Pallas kernels, last(): pl.pallas_call(last_kernel, out_shape=jax.ShapeDtypeStruct(mine.shape, jn...  0.8 us
  transfers between devices with their start and end apart: 10, of which 6 were waited for; matrix products, arithmetic and copies ran while one was open for 0% of the time, Pallas kernels for 12%

profile of v4, /device:TPU:0, one launch (start us, length us, event | category | flops | bytes accessed | tf_op | source)
XLA Modules:
  0.0 26.5 jit_solution(6321603741836367107)
XLA Ops:
  0.0 5.0 %collective-permute-start.1 = (bf16[128,256]{1,0:T(8,128)(2,1)}, bf16[128,256]{1,0:T(8,128)(2,1)S(1)}, u32[]{:S(2)}, u32[]{:S(2)}) collective-permute-start(bf16[128,256]{1,0:T(8,128)(2,1)} %refs_0_.1), channel_id=1, source_target_pairs={{0,24},{1,9},{2,26},{3,11},{4,28},{5,13},{6,30},{7,15},{8,0},{9,17... | collective-permute-start | bytes 196616 | tf_op jit(solution)/shard_map/ppermute | solution.py:169
  5.0 0.0 collective-permute-start
  5.1 0.0 collective-permute-start.5
  5.1 0.0 copy-start.1
  5.1 0.9 %copy-done.1 = bf16[128,256]{1,0:T(8,128)(2,1)S(1)} copy-done((bf16[128,256]{1,0:T(8,128)(2,1)S(1)}, bf16[128,256]{1,0:T(8,128)(2,1)}, u32[]{:S(2)}) %copy-start.1) | copy-done | bytes 65560
  6.0 0.0 copy-start.2
  6.0 0.7 %copy-done.2 = s32[96,2]{0,1:T(2,128)S(1)} copy-done((s32[96,2]{0,1:T(2,128)S(1)}, s32[96,2]{0,1:T(2,128)}, u32[]{:S(2)}) %copy-start.2) | copy-done | bytes 792
  6.6 0.7 %copy-done.3 = s32[1,8]{1,0:T(1,128)S(1)} copy-done((s32[1,8]{1,0:T(1,128)S(1)}, s32[1,8]{1,0:T(1,128)}, u32[]{:S(2)}) %copy-start.3) | copy-done | bytes 56
  7.3 0.1 collective-permute-done.1.refs_0_.refs_1_
  7.4 0.0 collective-permute-done.5.mate.refs_1_
  7.4 2.3 %collective-permute-start.6 = (bf16[256,256]{1,0:T(8,128)(2,1)S(1)}, bf16[256,256]{1,0:T(8,128)(2,1)S(1)}, u32[]{:S(2)}, u32[]{:S(2)}) collective-permute-start(bf16[256,256]{1,0:T(8,128)(2,1)S(1)} %shard_map.60), channel_id=1, source_target_pairs={{0,1},{1,0},{2,10},{3,27},{4,5},{5,4},{6,14},{7,31},{8,9},{9,8},{1... | collective-permute-start | bytes 393224 | tf_op jit(solution)/shard_map/ppermute | solution.py:169
  9.7 0.7 %collective-permute-done.refs_1_.refs_2_.refs_0_ = bf16[128,256]{1,0:T(8,128)(2,1)S(1)} collective-permute-done((bf16[128,256]{1,0:T(8,128)(2,1)}, bf16[128,256]{1,0:T(8,128)(2,1)S(1)}, u32[]{:S(2)}, u32[]{:S(2)}) %collective-permute-start) | collective-permute-done | bytes 65568 | tf_op jit(solution)/shard_map/ppermute | solution.py:169
  10.4 1.3 %collective-permute-start.2 = (bf16[256,256]{1,0:T(8,128)(2,1)S(1)}, bf16[256,256]{1,0:T(8,128)(2,1)S(1)}, u32[]{:S(2)}, u32[]{:S(2)}) collective-permute-start(bf16[256,256]{1,0:T(8,128)(2,1)S(1)} %shard_map.55), channel_id=1, source_target_pairs={{0,1},{1,0},{2,3},{3,2},{4,5},{5,4},{6,7},{7,6},{8,9},{9,8},{10,11... | collective-permute-start | bytes 393224 | tf_op jit(solution)/shard_map/ppermute | solution.py:169
  11.8 1.8 %collective-permute-start.3 = (bf16[256,256]{1,0:T(8,128)(2,1)S(1)}, bf16[256,256]{1,0:T(8,128)(2,1)S(1)}, u32[]{:S(2)}, u32[]{:S(2)}) collective-permute-start(bf16[256,256]{1,0:T(8,128)(2,1)S(1)} %shard_map.57), channel_id=1, source_target_pairs={{0,5},{1,4},{2,7},{3,6},{4,1},{5,0},{6,3},{7,2},{8,13},{9,12},{10,... | collective-permute-start | bytes 393224 | tf_op jit(solution)/shard_map/ppermute | solution.py:169
  13.5 0.5 %collective-permute-start.4 = (bf16[128,256]{1,0:T(8,128)(2,1)S(1)}, bf16[128,256]{1,0:T(8,128)(2,1)S(1)}, u32[]{:S(2)}, u32[]{:S(2)}) collective-permute-start(bf16[128,256]{1,0:T(8,128)(2,1)S(1)} %shard_map.58), channel_id=1, source_target_pairs={{0,4},{1,5},{2,6},{3,7},{4,0},{5,1},{6,2},{7,3},{8,12},{9,13},{10,... | collective-permute-start | bytes 196616 | tf_op jit(solution)/shard_map/ppermute | solution.py:169
  14.1 0.0 collective-permute-done.6.refs_6_.refs_4_
  14.1 0.7 %collective-permute-start.7 = (bf16[256,256]{1,0:T(8,128)(2,1)S(1)}, bf16[256,256]{1,0:T(8,128)(2,1)S(1)}, u32[]{:S(2)}, u32[]{:S(2)}) collective-permute-start(bf16[256,256]{1,0:T(8,128)(2,1)S(1)} %collective-permute-done.6.refs_6_.refs_4_), channel_id=1, source_target_pairs={{0,0},{1,1},{2,6},{3,7},{4,4},{5,5},{6,2},{7,3},{8,8},{9,9},{10,14... | collective-permute-start | bytes 393224 | tf_op jit(solution)/shard_map/ppermute | solution.py:169
  14.8 2.5 %shard_map.61.matrix.refs_3_ = bf16[256,2816]{1,0:T(8,128)(2,1)S(1)} custom-call(s32[1,8]{1,0:T(1,128)S(1)} %get-tuple-element.30.counts, s32[2,96]{1,0:T(2,128)S(1)} %get-tuple-element.31.coords, bf16[96,128,128]{2,1,0:T(8,128)(2,1)} %values.1), custom_call_target="tpu_custom_call" | custom-call | flops 4000000 | bytes 12000000 | tf_op jit(solution)/shard_map/pallas_call | solution.py:250
  17.3 0.6 %collective-permute-done.4.refs_5_.refs_2_.refs_3_ = bf16[128,256]{1,0:T(8,128)(2,1)S(1)} collective-permute-done((bf16[128,256]{1,0:T(8,128)(2,1)S(1)}, bf16[128,256]{1,0:T(8,128)(2,1)S(1)}, u32[]{:S(2)}, u32[]{:S(2)}) %collective-permute-start.4) | collective-permute-done | bytes 65568 | tf_op jit(solution)/shard_map/ppermute | solution.py:169
  17.9 0.0 collective-permute-done.2.refs_3_.refs_0_.refs_1_
  17.9 0.5 %collective-permute-done.3.refs_4_.refs_1_.refs_2_ = bf16[256,256]{1,0:T(8,128)(2,1)S(1)} collective-permute-done((bf16[256,256]{1,0:T(8,128)(2,1)S(1)}, bf16[256,256]{1,0:T(8,128)(2,1)S(1)}, u32[]{:S(2)}, u32[]{:S(2)}) %collective-permute-start.3) | collective-permute-done | bytes 131104 | tf_op jit(solution)/shard_map/ppermute | solution.py:169
  18.4 0.0 collective-permute-done.7.refs_7_.refs_5_
  18.5 0.0 copy-start
  18.5 0.8 %collective-permute-start.8 = (bf16[1280,256]{1,0:T(8,128)(2,1)S(1)}, bf16[1280,256]{1,0:T(8,128)(2,1)S(1)}, u32[]{:S(2)}, u32[]{:S(2)}) collective-permute-start(bf16[1280,256]{1,0:T(8,128)(2,1)S(1)} %shard_map.64), channel_id=1, source_target_pairs={{0,2},{1,3},{2,0},{3,1},{4,6},{5,7},{6,4},{7,5},{8,10},{9,11},{10,... | collective-permute-start | bytes 1966088 | tf_op jit(solution)/shard_map/ppermute | solution.py:169
  19.3 0.4 %shard_map.62.sums = f32[256,256]{1,0:T(8,128)S(1)} custom-call(bf16[256,2816]{1,0:T(8,128)(2,1)S(1)} %shard_map.61.matrix.refs_3_, bf16[128,256]{1,0:T(8,128)(2,1)S(1)} %get-tuple-element.33.refs_0_.own, bf16[128,256]{1,0:T(8,128)(2,1)S(1)} %collective-permute-done.5.mate.refs_1_, bf16[128,256]{1,0:T(8,128)(2,1)S(1)} %collective-permute-done.refs_1_.refs_2_.refs_0_, ...), custom_call_target="tpu_custom_call" | custom-call | flops 268000000 | bytes 2000000 | tf_op jit(solution)/shard_map/pallas_call | solution.py:281
  19.7 1.3 %collective-permute-done.8.refs_0_ = bf16[1280,256]{1,0:T(8,128)(2,1)S(1)} collective-permute-done((bf16[1280,256]{1,0:T(8,128)(2,1)S(1)}, bf16[1280,256]{1,0:T(8,128)(2,1)S(1)}, u32[]{:S(2)}, u32[]{:S(2)}) %collective-permute-start.8) | collective-permute-done | bytes 655392 | tf_op jit(solution)/shard_map/ppermute | solution.py:169
  21.0 0.3 shard_map.66
  21.3 1.7 %collective-permute-start.9 = (bf16[128,256]{1,0:T(8,128)(2,1)S(1)}, bf16[128,256]{1,0:T(8,128)(2,1)S(1)}, u32[]{:S(2)}, u32[]{:S(2)}) collective-permute-start(bf16[128,256]{1,0:T(8,128)(2,1)S(1)} %shard_map.66), channel_id=1, source_target_pairs={{0,1},{1,0},{2,3},{3,2},{4,5},{5,4},{6,7},{7,6},{8,9},{9,8},{10,11... | collective-permute-start | bytes 196616 | tf_op jit(solution)/shard_map/ppermute | solution.py:333
  23.0 0.3 shard_map.65.mine
  23.3 2.5 %collective-permute-done.9.theirs = bf16[128,256]{1,0:T(8,128)(2,1)S(1)} collective-permute-done((bf16[128,256]{1,0:T(8,128)(2,1)S(1)}, bf16[128,256]{1,0:T(8,128)(2,1)S(1)}, u32[]{:S(2)}, u32[]{:S(2)}) %collective-permute-start.9) | collective-permute-done | bytes 65568 | tf_op jit(solution)/shard_map/ppermute | solution.py:333
  25.7 0.0 copy-done
  25.7 0.8 %shard_map.67 = bf16[128,256]{1,0:T(8,128)(2,1)} custom-call(f32[128,256]{1,0:T(8,128)S(1)} %shard_map.65.mine, bf16[128,256]{1,0:T(8,128)(2,1)S(1)} %collective-permute-done.9.theirs, bf16[256,256]{1,0:T(8,128)(2,1)S(1)} %copy-done), custom_call_target="tpu_custom_call" | custom-call | flops 17000000 | bytes 400000 | tf_op jit(solution)/shard_map/pallas_call | solution.py:318
  (9 shorter events, 0.1 us)
Async XLA Ops:
  0.0 7.4 %collective-permute-start.1 = (bf16[128,256]{1,0:T(8,128)(2,1)}, bf16[128,256]{1,0:T(8,128)(2,1)S(1)}, u32[]{:S(2)}, u32[]{:S(2)}) collective-permute-start(bf16[128,256]{1,0:T(8,128)(2,1)} %refs_0_.1), channel_id=1, source_target_pairs={{0,24},{1,9},{2,26},{3,11},{4,28},{5,13},{6,30},{7,15},{8,0},{9,17... | collective-permute-start | bytes 196616 | tf_op jit(solution)/shard_map/ppermute | solution.py:169
  5.0 5.4 %collective-permute-start = (bf16[128,256]{1,0:T(8,128)(2,1)}, bf16[128,256]{1,0:T(8,128)(2,1)S(1)}, u32[]{:S(2)}, u32[]{:S(2)}) collective-permute-start(bf16[128,256]{1,0:T(8,128)(2,1)} %refs_0_.1), channel_id=1, source_target_pairs={{0,16},{1,17},{2,18},{3,19},{4,20},{5,21},{6,22},{7,23},{8,24},{9,... | collective-permute-start | bytes 196616 | tf_op jit(solution)/shard_map/ppermute | solution.py:169
  5.1 2.4 %collective-permute-start.5 = (bf16[128,256]{1,0:T(8,128)(2,1)}, bf16[128,256]{1,0:T(8,128)(2,1)S(1)}, u32[]{:S(2)}, u32[]{:S(2)}) collective-permute-start(bf16[128,256]{1,0:T(8,128)(2,1)} %refs_0_.1), channel_id=1, source_target_pairs={{0,2},{1,3},{2,0},{3,1},{4,6},{5,7},{6,4},{7,5},{8,10},{9,11},{10,... | collective-permute-start | bytes 196616 | tf_op jit(solution)/shard_map/ppermute | solution.py:169
  5.1 0.9 %copy-start.1 = (bf16[128,256]{1,0:T(8,128)(2,1)S(1)}, bf16[128,256]{1,0:T(8,128)(2,1)}, u32[]{:S(2)}) copy-start(bf16[128,256]{1,0:T(8,128)(2,1)} %refs_0_.1) | copy-start | bytes 196612
  6.0 0.7 %copy-start.2 = (s32[96,2]{0,1:T(2,128)S(1)}, s32[96,2]{0,1:T(2,128)}, u32[]{:S(2)}) copy-start(s32[96,2]{0,1:T(2,128)} %param.8) | copy-start | bytes 2308
  6.6 0.7 %copy-start.3 = (s32[1,8]{1,0:T(1,128)S(1)}, s32[1,8]{1,0:T(1,128)}, u32[]{:S(2)}) copy-start(s32[1,8]{1,0:T(1,128)} %refs_1_.1) | copy-start | bytes 100
  7.4 6.6 %collective-permute-start.6 = (bf16[256,256]{1,0:T(8,128)(2,1)S(1)}, bf16[256,256]{1,0:T(8,128)(2,1)S(1)}, u32[]{:S(2)}, u32[]{:S(2)}) collective-permute-start(bf16[256,256]{1,0:T(8,128)(2,1)S(1)} %shard_map.60), channel_id=1, source_target_pairs={{0,1},{1,0},{2,10},{3,27},{4,5},{5,4},{6,14},{7,31},{8,9},{9,8},{1... | collective-permute-start | bytes 393224 | tf_op jit(solution)/shard_map/ppermute | solution.py:169
  10.4 7.5 %collective-permute-start.2 = (bf16[256,256]{1,0:T(8,128)(2,1)S(1)}, bf16[256,256]{1,0:T(8,128)(2,1)S(1)}, u32[]{:S(2)}, u32[]{:S(2)}) collective-permute-start(bf16[256,256]{1,0:T(8,128)(2,1)S(1)} %shard_map.55), channel_id=1, source_target_pairs={{0,1},{1,0},{2,3},{3,2},{4,5},{5,4},{6,7},{7,6},{8,9},{9,8},{10,11... | collective-permute-start | bytes 393224 | tf_op jit(solution)/shard_map/ppermute | solution.py:169
  11.8 6.7 %collective-permute-start.3 = (bf16[256,256]{1,0:T(8,128)(2,1)S(1)}, bf16[256,256]{1,0:T(8,128)(2,1)S(1)}, u32[]{:S(2)}, u32[]{:S(2)}) collective-permute-start(bf16[256,256]{1,0:T(8,128)(2,1)S(1)} %shard_map.57), channel_id=1, source_target_pairs={{0,5},{1,4},{2,7},{3,6},{4,1},{5,0},{6,3},{7,2},{8,13},{9,12},{10,... | collective-permute-start | bytes 393224 | tf_op jit(solution)/shard_map/ppermute | solution.py:169
  13.5 4.3 %collective-permute-start.4 = (bf16[128,256]{1,0:T(8,128)(2,1)S(1)}, bf16[128,256]{1,0:T(8,128)(2,1)S(1)}, u32[]{:S(2)}, u32[]{:S(2)}) collective-permute-start(bf16[128,256]{1,0:T(8,128)(2,1)S(1)} %shard_map.58), channel_id=1, source_target_pairs={{0,4},{1,5},{2,6},{3,7},{4,0},{5,1},{6,2},{7,3},{8,12},{9,13},{10,... | collective-permute-start | bytes 196616 | tf_op jit(solution)/shard_map/ppermute | solution.py:169
  14.1 4.3 %collective-permute-start.7 = (bf16[256,256]{1,0:T(8,128)(2,1)S(1)}, bf16[256,256]{1,0:T(8,128)(2,1)S(1)}, u32[]{:S(2)}, u32[]{:S(2)}) collective-permute-start(bf16[256,256]{1,0:T(8,128)(2,1)S(1)} %collective-permute-done.6.refs_6_.refs_4_), channel_id=1, source_target_pairs={{0,0},{1,1},{2,6},{3,7},{4,4},{5,5},{6,2},{7,3},{8,8},{9,9},{10,14... | collective-permute-start | bytes 393224 | tf_op jit(solution)/shard_map/ppermute | solution.py:169
  18.5 7.2 %copy-start = (bf16[256,256]{1,0:T(8,128)(2,1)S(1)}, bf16[256,256]{1,0:T(8,128)(2,1)}, u32[]{:S(2)}) copy-start(bf16[256,256]{1,0:T(8,128)(2,1)} %weight.1) | copy-start | bytes 393220
  18.5 2.5 %collective-permute-start.8 = (bf16[1280,256]{1,0:T(8,128)(2,1)S(1)}, bf16[1280,256]{1,0:T(8,128)(2,1)S(1)}, u32[]{:S(2)}, u32[]{:S(2)}) collective-permute-start(bf16[1280,256]{1,0:T(8,128)(2,1)S(1)} %shard_map.64), channel_id=1, source_target_pairs={{0,2},{1,3},{2,0},{3,1},{4,6},{5,7},{6,4},{7,5},{8,10},{9,11},{10,... | collective-permute-start | bytes 1966088 | tf_op jit(solution)/shard_map/ppermute | solution.py:169
  21.3 4.4 %collective-permute-start.9 = (bf16[128,256]{1,0:T(8,128)(2,1)S(1)}, bf16[128,256]{1,0:T(8,128)(2,1)S(1)}, u32[]{:S(2)}, u32[]{:S(2)}) collective-permute-start(bf16[128,256]{1,0:T(8,128)(2,1)S(1)} %shard_map.66), channel_id=1, source_target_pairs={{0,1},{1,0},{2,3},{3,2},{4,5},{5,4},{6,7},{7,6},{8,9},{9,8},{10,11... | collective-permute-start | bytes 196616 | tf_op jit(solution)/shard_map/ppermute | solution.py:333

commit v5 on v3

v5 whole, which is shorter than its diff:
```python
import functools

import jax
import jax.numpy as jnp
from jax import lax
from jax.experimental import pallas as pl
from jax.experimental.pallas import tpu as pltpu
from jax.sharding import PartitionSpec as P

AXES = ("loop", "rep")
VMEM = pl.BlockSpec(memory_space=pltpu.VMEM)
SMEM = pl.BlockSpec(memory_space=pltpu.SMEM)


def from_behind(x, axis, by):
    count = lax.axis_size(axis)
    return lax.ppermute(x, axis, [(i, (i + by) % count) for i in range(count)])


def ring(features, weight, tile_values, tile_coords, tile_counts):
    rep_size = lax.axis_size("rep")
    loop_size = lax.axis_size("loop")
    step_count = loop_size // rep_size
    tile_size = tile_values.shape[1]
    feat_width = features.shape[1]
    slot_count = tile_values.shape[0] // step_count
    current_slab = lax.all_gather(features, "rep", axis=0, tiled=True)
    block_count = current_slab.shape[0] // tile_size
    values = tile_values.reshape(step_count, slot_count, tile_size, tile_size)
    coords = tile_coords.reshape(step_count, slot_count, 2)
    counts = tile_counts.reshape(step_count)
    rep_rank = lax.axis_index("rep")
    for bit_index in range(rep_size.bit_length() - 1):
        shifted = from_behind(current_slab, "loop", step_count * (1 << bit_index))
        current_slab = jnp.where(rep_rank >> bit_index & 1 == 1, shifted, current_slab)
    running = jnp.zeros((block_count, tile_size, feat_width), jnp.float32)
    for step_index in range(step_count):
        slab_blocks = current_slab.reshape(block_count, tile_size, feat_width)
        pieces = jnp.take(slab_blocks, coords[step_index, :, 1], axis=0)
        products = jnp.einsum(
            "ktc,kcf->ktf", values[step_index], pieces, preferred_element_type=jnp.float32
        )
        live_slot = (jnp.arange(slot_count) < counts[step_index]).astype(jnp.float32)
        running = running.at[coords[step_index, :, 0]].add(products * live_slot[:, None, None])
        if step_index + 1 < step_count:
            current_slab = from_behind(current_slab, "loop", 1)
    summed = lax.psum_scatter(
        running.reshape(block_count * tile_size, feat_width), "rep", scatter_dimension=0, tiled=True
    )
    aggregated = summed.astype(jnp.bfloat16)
    product = jnp.dot(aggregated, weight, preferred_element_type=jnp.float32)
    return jnp.maximum(product, 0.0).astype(jnp.bfloat16)

HELD = 11
SMALL = 4 * 1024 * 1024
MIDDLE = 24 * 1024 * 1024


def route(planes, move):
    pairs = []
    for z in range(planes):
        for x in range(2):
            for core in range(2):
                for y in range(2):
                    z2, x2, core2, y2 = move(z, x, core, y)
                    pairs.append((((z * 2 + x) * 2 + core) * 2 + y, (((z2 % planes) * 2 + x2) * 2 + core2) * 2 + y2))
    return pairs


def pick_kernel(even, odd, *refs):
    out = refs[-1]
    near = (lax.axis_index("loop") >> 1 & 1) == lax.axis_index("rep")
    for chosen, which in ((jnp.logical_not(near), even), (near, odd)):

        @pl.when(chosen)
        def _(which=which):
            start = 0
            for j in which:
                rows = refs[j].shape[0]
                out[pl.ds(start, rows)] = refs[j][...]
                start += rows


def pick(even, odd, *blocks):
    width = blocks[0].shape[1]
    rows = sum(blocks[j].shape[0] for j in even)
    return pl.pallas_call(
        functools.partial(pick_kernel, even, odd),
        out_shape=jax.ShapeDtypeStruct((rows, width), blocks[0].dtype),
        in_specs=[VMEM] * len(blocks),
        out_specs=VMEM,
        compiler_params=pltpu.CompilerParams(vmem_limit_bytes=SMALL),
        cost_estimate=pl.CostEstimate(flops=0, bytes_accessed=200_000, transcendentals=0),
    )(*blocks)


def pair_kernel(value, mate, mark, matrix, both, own):
    core = lax.axis_index("loop") & 1
    rows = value.shape[0]
    both[pl.ds(pl.multiple_of(core * rows, rows), rows)] = value[...]
    both[pl.ds(pl.multiple_of((1 - core) * rows, rows), rows)] = mate[...]
    own[...] = value[...]


def pair(value, mate, mark, matrix):
    rows, width = value.shape
    return pl.pallas_call(
        pair_kernel,
        out_shape=[jax.ShapeDtypeStruct((n * rows, width), value.dtype) for n in (2, 1)],
        in_specs=[VMEM] * 4,
        out_specs=[VMEM] * 2,
        compiler_params=pltpu.CompilerParams(vmem_limit_bytes=SMALL),
        cost_estimate=pl.CostEstimate(flops=0, bytes_accessed=200_000, transcendentals=0),
    )(value, mate, mark, matrix)


def pause_kernel(out):
    out[...] = jnp.zeros_like(out)


def pause(cost):
    return pl.pallas_call(
        pause_kernel,
        out_shape=jax.ShapeDtypeStruct((16, 128), jnp.bfloat16),
        out_specs=VMEM,
        compiler_params=pltpu.CompilerParams(vmem_limit_bytes=SMALL),
        cost_estimate=pl.CostEstimate(flops=cost, bytes_accessed=4096, transcendentals=0),
    )()


def mark_kernel(*refs):
    refs[-1][...] = refs[0][pl.ds(0, 16), pl.ds(0, 128)]


def mark(cost, *values):
    return pl.pallas_call(
        mark_kernel,
        out_shape=jax.ShapeDtypeStruct((16, 128), values[0].dtype),
        in_specs=[VMEM] * len(values),
        out_specs=VMEM,
        compiler_params=pltpu.CompilerParams(vmem_limit_bytes=SMALL),
        cost_estimate=pl.CostEstimate(flops=cost, bytes_accessed=4096, transcendentals=0),
    )(*values)


def spread(features, planes, counts, coords, tile_values):
    def send(value, move):
        return lax.ppermute(value, AXES, route(planes, move))

    def sign(y):
        return 1 if y else -1

    def core(z, x, c, y):
        return z, x, 1 - c, y

    behind = send(features, lambda z, x, c, y: (z + sign(y), x, c, y))
    far = send(features, lambda z, x, c, y: (z + 2, x, c, y))
    mate = send(features, core)
    kept, given = dense(pause(1_000_000_000), counts, coords, tile_values)
    taken = send(given, core)
    both, own = pair(features, mate, mark(500_000_000, behind), kept)
    ahead = send(both, lambda z, x, c, y: (z - sign(y), x, c, y) if c else (z, x, c, 1 - y))
    ready = mark(40_000_000_000, far)
    done = mark(1, taken)
    along_y = send(pick((0, 1), (0, 1), behind, far, done, ready), lambda z, x, c, y: (z, x, c, 1 - y))
    across = send(pick((0, 1), (1, 2), own, behind, far, done, ready), lambda z, x, c, y: (z, 1 - x, c, 1 - y))
    along_x = send(pick((1,), (0,), own, far, done, ready), lambda z, x, c, y: (z, 1 - x, c, y))
    beside = send(ahead, lambda z, x, c, y: (z, 1 - x, c, y) if c else (z, x, c, y))
    arrived = mark(4_000_000_000, along_y, across, along_x)
    held = [own, far, along_y, across, along_x, ahead, beside]
    other = send(products(taken, held, arrived, jnp.bfloat16), core)
    mine = products(kept, held, arrived, jnp.float32)
    theirs = send(partner_sum(mine, other), lambda z, x, c, y: (z, x, c, 1 - y))
    return mine, other, theirs


def dense_kernel(mark, counts, coords, values, kept, given, total):
    steps = counts.shape[1]
    slots = values.shape[0] // steps
    tile = values.shape[1]
    core = lax.axis_index("loop") & 1
    rank = lax.axis_index("rep")
    near = (lax.axis_index("loop") >> 1 & 1) == rank
    kept[...] = jnp.zeros_like(kept)
    given[...] = jnp.zeros_like(given)

    def one(step, carry):
        total[...] = jnp.zeros_like(total)

        def add(slot, carry):
            row = coords[0, step * slots + slot] ^ rank
            column = coords[1, step * slots + slot] ^ rank
            spot = row * 2 + column
            total[spot] = total[spot] + values[step * slots + slot].astype(jnp.float32)
            return carry

        lax.fori_loop(0, counts[0, step], add, 0)
        odd = step & 1
        there = odd * (1 - 2 * core)
        k = jnp.where(rank == 0, step + there, steps - step - there) >> 1
        half = k >> 1
        parity = core ^ odd
        turned = k & 1 == 1
        paired = (k == 1) == near
        straight = jnp.where(k == 2, 7 + parity, half >> 1)
        homes = (
            jnp.where(jnp.where(turned, paired, k == 2), 1, parity),
            jnp.where(k == 0, 0, parity),
        )
        places = (
            jnp.where(turned, jnp.where(paired, 9 + parity, 6), straight),
            jnp.where(turned, 4 + half, jnp.where(k == 0, 7 + parity, 1 + half)),
        )
        for column in range(2):
            start = pl.multiple_of(places[column] * tile, tile)
            for out, here in ((kept, homes[column] == core), (given, homes[column] != core)):

                @pl.when(here)
                def _(out=out, column=column, start=start):
                    for row in range(2):
                        piece = total[row * 2 + column].astype(jnp.bfloat16)
                        out[pl.ds(row * tile, tile), pl.ds(start, tile)] = piece

        return carry

    lax.fori_loop(0, steps, one, 0)


def dense(mark, tile_counts, tile_coords, tile_values):
    tile = tile_values.shape[1]
    return pl.pallas_call(
        dense_kernel,
        out_shape=[jax.ShapeDtypeStruct((2 * tile, HELD * tile), jnp.bfloat16)] * 2,
        in_specs=[VMEM, SMEM, SMEM, VMEM],
        out_specs=[VMEM, VMEM],
        scratch_shapes=[pltpu.VMEM((4, tile, tile), jnp.float32)],
        compiler_params=pltpu.CompilerParams(vmem_limit_bytes=MIDDLE),
        cost_estimate=pl.CostEstimate(flops=1, bytes_accessed=1, transcendentals=0),
    )(mark, tile_counts, tile_coords, tile_values)


def product_kernel(matrix, mark, *refs):
    out = refs[-1]
    total = jnp.zeros(out.shape, jnp.float32)
    start = 0
    for block in refs[:-1]:
        depth = block.shape[0]
        total += jnp.dot(matrix[:, pl.ds(start, depth)], block[...], preferred_element_type=jnp.float32)
        start += depth
    out[...] = total.astype(out.dtype)


def products(matrix, blocks, mark, dtype):
    rows = matrix.shape[0]
    width = blocks[0].shape[1]
    return pl.pallas_call(
        product_kernel,
        out_shape=jax.ShapeDtypeStruct((rows, width), dtype),
        in_specs=[VMEM] * (2 + len(blocks)),
        out_specs=VMEM,
        compiler_params=pltpu.CompilerParams(vmem_limit_bytes=MIDDLE),
        cost_estimate=pl.CostEstimate(flops=168_000_000, bytes_accessed=1_000_000, transcendentals=0),
    )(matrix, mark, *blocks)


def sum_kernel(mine, other, out):
    rows = pl.ds(out.shape[0], out.shape[0])
    out[...] = (mine[rows] + other[rows].astype(jnp.float32)).astype(out.dtype)


def partner_sum(mine, other):
    return pl.pallas_call(
        sum_kernel,
        out_shape=jax.ShapeDtypeStruct((mine.shape[0] // 2, mine.shape[1]), other.dtype),
        in_specs=[VMEM] * 2,
        out_specs=VMEM,
        compiler_params=pltpu.CompilerParams(vmem_limit_bytes=SMALL),
        cost_estimate=pl.CostEstimate(flops=32_768, bytes_accessed=300_000, transcendentals=0),
    )(mine, other)


def last_kernel(mine, other, theirs, weight, out):
    rows = pl.ds(0, out.shape[0])
    sums = mine[rows] + other[rows].astype(jnp.float32) + theirs[...].astype(jnp.float32)
    product = jnp.dot(sums.astype(jnp.bfloat16), weight[...], preferred_element_type=jnp.float32)
    out[...] = jnp.maximum(product, 0.0).astype(out.dtype)


def last(mine, other, theirs, weight):
    return pl.pallas_call(
        last_kernel,
        out_shape=jax.ShapeDtypeStruct(theirs.shape, jnp.bfloat16),
        in_specs=[VMEM] * 4,
        out_specs=VMEM,
        compiler_params=pltpu.CompilerParams(vmem_limit_bytes=SMALL),
        cost_estimate=pl.CostEstimate(flops=17_000_000, bytes_accessed=400_000, transcendentals=0),
    )(mine, other, theirs, weight)


def pairs(features, weight, tile_values, tile_coords, tile_counts):
    planes = lax.axis_size("loop") // 4
    mine, other, theirs = spread(features, planes, tile_counts, tile_coords.T, tile_values)
    return last(mine, other, theirs, weight)


def solution(mesh):
    placed = (
        P(AXES, None),
        P(),
        P(AXES, None, None),
        P(AXES, None),
        P(AXES, None),
    )
    local = pairs if dict(mesh.shape) == {"loop": 16, "rep": 2} else ring
    return jax.shard_map(local, mesh=mesh, in_specs=placed, out_specs=P(AXES, None), check_vma=False)
```

time: 27.3 us -> 26.4 us (0.967)
  local copies, waits for them, and re-layouts: 2.3 us -> 0.02 us
  starting transfers between devices: 12.5 us -> 14.6 us
  Pallas kernels: 4.52 us -> 3.21 us
  waiting for transfers between devices: 7.68 us -> 7.96 us
    ppermute x7 -> x11, starting transfers between devices: 10.7 us -> 14.6 us  [send(): return lax.ppermute(value, AXES, route(planes, move))]
    ppermute x7 -> x11, waiting for transfers between devices: 5.52 us -> 7.96 us  [send(): return lax.ppermute(value, AXES, route(planes, move))]
    unnamed x13 -> x10, local copies, waits for them, and re-layouts: 2.29 us -> 0.02 us
    ppermute x1 -> x0, waiting for transfers between devices: 2.16 us -> none  [pairs(): theirs = lax.ppermute(theirs, 'rep', [(0, 1), (1, 0)])]
    ppermute x1 -> x0, starting transfers between devices: 1.81 us -> none  [pairs(): theirs = lax.ppermute(theirs, 'rep', [(0, 1), (1, 0)])]
    pallas_call x5 -> x11, Pallas kernels: 4.49 us -> 3.17 us  [the longest x1 1.56 us: dense(): pl.pallas_call(dense_kernel, out_shape=[jax.ShapeDtypeStruct((2 * tile, H...]
  transfers between devices with their start and end apart: 8 -> 11, of which waited for: 8 -> 6; matrix products, arithmetic and copies ran while one was open for 0% -> 0% of each run, Pallas kernels for 12% -> 8%
where the time goes in v5:
time: 26.4 us; the launch traced here: 25.9 us
  starting transfers between devices  14.6 us (55%)
  waiting for transfers between devices  7.96 us (30%)
  Pallas kernels  3.21 us (12%)
    ppermute x11, starting transfers between devices, send(): return lax.ppermute(value, AXES, route(planes, move))  14.6 us
    ppermute x11, waiting for transfers between devices, send(): return lax.ppermute(value, AXES, route(planes, move))  7.96 us
    pallas_call x1, Pallas kernels, dense(): pl.pallas_call(dense_kernel, out_shape=[jax.ShapeDtypeStruct((2 * tile, H...  1.56 us
    pallas_call x1, Pallas kernels, last(): pl.pallas_call(last_kernel, out_shape=jax.ShapeDtypeStruct(theirs.shape,...  0.8 us
    pallas_call x2, Pallas kernels, products(): pl.pallas_call(product_kernel, out_shape=jax.ShapeDtypeStruct((rows, widt...  0.78 us
  transfers between devices with their start and end apart: 11, of which 6 were waited for; matrix products, arithmetic and copies ran while one was open for 0% of the time, Pallas kernels for 8%

profile of v5, /device:TPU:0, one launch (start us, length us, event | category | flops | bytes accessed | tf_op | source)
XLA Modules:
  0.0 25.9 jit_solution(17812152394640491139)
XLA Ops:
  0.0 5.1 %collective-permute-start = (bf16[128,256]{1,0:T(8,128)(2,1)}, bf16[128,256]{1,0:T(8,128)(2,1)S(1)}, u32[]{:S(2)}, u32[]{:S(2)}) collective-permute-start(bf16[128,256]{1,0:T(8,128)(2,1)} %value.1), channel_id=1, source_target_pairs={{0,24},{1,9},{2,26},{3,11},{4,28},{5,13},{6,30},{7,15},{8,0},{9,17... | collective-permute-start | bytes 196616 | tf_op jit(solution)/shard_map/ppermute | solution.py:148
  5.1 0.0 collective-permute-start.1
  5.1 0.0 collective-permute-start.4
  5.1 0.0 copy-start.2
  5.1 0.0 copy-done.4
  5.1 0.0 copy-done.3
  5.2 0.0 copy-done
  5.2 1.6 %shard_map.56 = (bf16[256,1408]{1,0:T(8,128)(2,1)S(1)}, bf16[256,1408]{1,0:T(8,128)(2,1)S(1)}) custom-call(bf16[16,128]{1,0:T(8,128)(2,1)S(1)} %shard_map.55.mark, s32[1,8]{1,0:T(1,128)S(1)} %copy-done.4, s32[2,96]{1,0:T(2,128)S(1)} %bitcast.1, bf16[96,128,128]{2,1,0:T(8,128)(2,1)S(1)} %copy-done), custom_call_target="tpu_custom_call" | custom-call | flops 1 | bytes 1 | tf_op jit(solution)/shard_map/pallas_call | solution.py:231
  6.7 0.4 %collective-permute-start.2 = (bf16[256,1408]{1,0:T(8,128)(2,1)S(1)}, bf16[256,1408]{1,0:T(8,128)(2,1)S(1)}, u32[]{:S(2)}, u32[]{:S(2)}) collective-permute-start(bf16[256,1408]{1,0:T(8,128)(2,1)S(1)} %get-tuple-element.10), channel_id=1, source_target_pairs={{0,2},{1,3},{2,0},{3,1},{4,6},{5,7},{6,4},{7,5},{8,10},{9,11},{10,... | collective-permute-start | bytes 2162696 | tf_op jit(solution)/shard_map/ppermute | solution.py:148
  7.2 0.3 %collective-permute-done.refs_0_.refs_1_ = bf16[128,256]{1,0:T(8,128)(2,1)S(1)} collective-permute-done((bf16[128,256]{1,0:T(8,128)(2,1)}, bf16[128,256]{1,0:T(8,128)(2,1)S(1)}, u32[]{:S(2)}, u32[]{:S(2)}) %collective-permute-start) | collective-permute-done | bytes 65568 | tf_op jit(solution)/shard_map/ppermute | solution.py:148
  7.5 0.0 collective-permute-done.4.mate
  7.5 0.0 copy-done.2
  7.5 2.3 %collective-permute-start.7 = (bf16[256,256]{1,0:T(8,128)(2,1)S(1)}, bf16[256,256]{1,0:T(8,128)(2,1)S(1)}, u32[]{:S(2)}, u32[]{:S(2)}) collective-permute-start(bf16[256,256]{1,0:T(8,128)(2,1)S(1)} %get-tuple-element.12), channel_id=1, source_target_pairs={{0,1},{1,0},{2,10},{3,27},{4,5},{5,4},{6,14},{7,31},{8,9},{9,8},{1... | collective-permute-start | bytes 393224 | tf_op jit(solution)/shard_map/ppermute | solution.py:148
  9.8 0.7 %collective-permute-done.1.refs_0_.refs_1_.refs_2_ = bf16[128,256]{1,0:T(8,128)(2,1)S(1)} collective-permute-done((bf16[128,256]{1,0:T(8,128)(2,1)}, bf16[128,256]{1,0:T(8,128)(2,1)S(1)}, u32[]{:S(2)}, u32[]{:S(2)}) %collective-permute-start.1) | collective-permute-done | bytes 65568 | tf_op jit(solution)/shard_map/ppermute | solution.py:148
  10.5 0.0 collective-permute-done.2.refs_0_.matrix
  10.5 1.3 %collective-permute-start.3 = (bf16[256,256]{1,0:T(8,128)(2,1)S(1)}, bf16[256,256]{1,0:T(8,128)(2,1)S(1)}, u32[]{:S(2)}, u32[]{:S(2)}) collective-permute-start(bf16[256,256]{1,0:T(8,128)(2,1)S(1)} %shard_map.59), channel_id=1, source_target_pairs={{0,1},{1,0},{2,3},{3,2},{4,5},{5,4},{6,7},{7,6},{8,9},{9,8},{10,11... | collective-permute-start | bytes 393224 | tf_op jit(solution)/shard_map/ppermute | solution.py:148
  11.9 1.7 %collective-permute-start.5 = (bf16[256,256]{1,0:T(8,128)(2,1)S(1)}, bf16[256,256]{1,0:T(8,128)(2,1)S(1)}, u32[]{:S(2)}, u32[]{:S(2)}) collective-permute-start(bf16[256,256]{1,0:T(8,128)(2,1)S(1)} %shard_map.62), channel_id=1, source_target_pairs={{0,5},{1,4},{2,7},{3,6},{4,1},{5,0},{6,3},{7,2},{8,13},{9,12},{10,... | collective-permute-start | bytes 393224 | tf_op jit(solution)/shard_map/ppermute | solution.py:148
  13.6 0.5 %collective-permute-start.6 = (bf16[128,256]{1,0:T(8,128)(2,1)S(1)}, bf16[128,256]{1,0:T(8,128)(2,1)S(1)}, u32[]{:S(2)}, u32[]{:S(2)}) collective-permute-start(bf16[128,256]{1,0:T(8,128)(2,1)S(1)} %shard_map.63), channel_id=1, source_target_pairs={{0,4},{1,5},{2,6},{3,7},{4,0},{5,1},{6,2},{7,3},{8,12},{9,13},{10,... | collective-permute-start | bytes 196616 | tf_op jit(solution)/shard_map/ppermute | solution.py:148
  14.2 0.0 collective-permute-done.7.refs_5_
  14.2 0.7 %collective-permute-start.8 = (bf16[256,256]{1,0:T(8,128)(2,1)S(1)}, bf16[256,256]{1,0:T(8,128)(2,1)S(1)}, u32[]{:S(2)}, u32[]{:S(2)}) collective-permute-start(bf16[256,256]{1,0:T(8,128)(2,1)S(1)} %collective-permute-done.7.refs_5_), channel_id=1, source_target_pairs={{0,0},{1,1},{2,6},{3,7},{4,4},{5,5},{6,2},{7,3},{8,8},{9,9},{10,14... | collective-permute-start | bytes 393224 | tf_op jit(solution)/shard_map/ppermute | solution.py:148
  14.8 3.2 %collective-permute-done.6.refs_2_.refs_4_ = bf16[128,256]{1,0:T(8,128)(2,1)S(1)} collective-permute-done((bf16[128,256]{1,0:T(8,128)(2,1)S(1)}, bf16[128,256]{1,0:T(8,128)(2,1)S(1)}, u32[]{:S(2)}, u32[]{:S(2)}) %collective-permute-start.6) | collective-permute-done | bytes 65568 | tf_op jit(solution)/shard_map/ppermute | solution.py:148
  18.0 0.0 collective-permute-done.3.refs_0_.refs_2_
  18.0 0.5 %collective-permute-done.5.refs_1_.refs_3_ = bf16[256,256]{1,0:T(8,128)(2,1)S(1)} collective-permute-done((bf16[256,256]{1,0:T(8,128)(2,1)S(1)}, bf16[256,256]{1,0:T(8,128)(2,1)S(1)}, u32[]{:S(2)}, u32[]{:S(2)}) %collective-permute-start.5) | collective-permute-done | bytes 131104 | tf_op jit(solution)/shard_map/ppermute | solution.py:148
  18.5 0.0 collective-permute-done.8.refs_6_
  18.5 0.4 %shard_map.66 = bf16[256,256]{1,0:T(8,128)(2,1)S(1)} custom-call(bf16[256,1408]{1,0:T(8,128)(2,1)S(1)} %collective-permute-done.2.refs_0_.matrix, bf16[16,128]{1,0:T(8,128)(2,1)S(1)} %shard_map.64.mark, bf16[128,256]{1,0:T(8,128)(2,1)S(1)} %get-tuple-element.11.refs_0_, bf16[128,256]{1,0:T(8,128)(2,1)S(1)} %collective-permute-done.1.refs_0_.refs_1_.refs_2_, ...), custom_call_target="tpu_custom_call" | custom-call | flops 168000000 | bytes 1000000 | tf_op jit(solution)/shard_map/pallas_call | solution.py:256
  18.9 0.8 %collective-permute-start.9 = (bf16[256,256]{1,0:T(8,128)(2,1)S(1)}, bf16[256,256]{1,0:T(8,128)(2,1)S(1)}, u32[]{:S(2)}, u32[]{:S(2)}) collective-permute-start(bf16[256,256]{1,0:T(8,128)(2,1)S(1)} %shard_map.66), channel_id=1, source_target_pairs={{0,2},{1,3},{2,0},{3,1},{4,6},{5,7},{6,4},{7,5},{8,10},{9,11},{10,... | collective-permute-start | bytes 393224 | tf_op jit(solution)/shard_map/ppermute | solution.py:148
  19.7 0.4 %shard_map.65.mine = f32[256,256]{1,0:T(8,128)S(1)} custom-call(bf16[256,1408]{1,0:T(8,128)(2,1)S(1)} %get-tuple-element.9.matrix, bf16[16,128]{1,0:T(8,128)(2,1)S(1)} %shard_map.64.mark, bf16[128,256]{1,0:T(8,128)(2,1)S(1)} %get-tuple-element.11.refs_0_, bf16[128,256]{1,0:T(8,128)(2,1)S(1)} %collective-permute-done.1.refs_0_.refs_1_.refs_2_, ...), custom_call_target="tpu_custom_call" | custom-call | flops 168000000 | bytes 1000000 | tf_op jit(solution)/shard_map/pallas_call | solution.py:256
  20.1 0.6 %collective-permute-done.9.other = bf16[256,256]{1,0:T(8,128)(2,1)S(1)} collective-permute-done((bf16[256,256]{1,0:T(8,128)(2,1)S(1)}, bf16[256,256]{1,0:T(8,128)(2,1)S(1)}, u32[]{:S(2)}, u32[]{:S(2)}) %collective-permute-start.9) | collective-permute-done | bytes 131104 | tf_op jit(solution)/shard_map/ppermute | solution.py:148
  20.7 1.7 %collective-permute-start.10 = (bf16[128,256]{1,0:T(8,128)(2,1)S(1)}, bf16[128,256]{1,0:T(8,128)(2,1)S(1)}, u32[]{:S(2)}, u32[]{:S(2)}) collective-permute-start(bf16[128,256]{1,0:T(8,128)(2,1)S(1)} %shard_map.67), channel_id=1, source_target_pairs={{0,1},{1,0},{2,3},{3,2},{4,5},{5,4},{6,7},{7,6},{8,9},{9,8},{10,11... | collective-permute-start | bytes 196616 | tf_op jit(solution)/shard_map/ppermute | solution.py:148
  22.4 2.7 %collective-permute-done.10.theirs = bf16[128,256]{1,0:T(8,128)(2,1)S(1)} collective-permute-done((bf16[128,256]{1,0:T(8,128)(2,1)S(1)}, bf16[128,256]{1,0:T(8,128)(2,1)S(1)}, u32[]{:S(2)}, u32[]{:S(2)}) %collective-permute-start.10) | collective-permute-done | bytes 65568 | tf_op jit(solution)/shard_map/ppermute | solution.py:148
  25.1 0.0 copy-done.1
  25.1 0.8 %shard_map.68 = bf16[128,256]{1,0:T(8,128)(2,1)} custom-call(f32[256,256]{1,0:T(8,128)S(1)} %shard_map.65.mine, bf16[256,256]{1,0:T(8,128)(2,1)S(1)} %collective-permute-done.9.other, bf16[128,256]{1,0:T(8,128)(2,1)S(1)} %collective-permute-done.10.theirs, bf16[256,256]{1,0:T(8,128)(2,1)S(1)} %copy-done.1), custom_call_target="tpu_custom_call" | custom-call | flops 17000000 | bytes 400000 | tf_op jit(solution)/shard_map/pallas_call | solution.py:290
  (14 shorter events, 0.1 us)
Async XLA Ops:
  0.0 5.1 %copy-start.4 = (s32[1,8]{1,0:T(1,128)S(1)}, s32[1,8]{1,0:T(1,128)}, u32[]{:S(2)}) copy-start(s32[1,8]{1,0:T(1,128)} %counts.1) | copy-start | bytes 100
  0.0 5.1 %copy-start.3 = (s32[96,2]{0,1:T(2,128)S(1)}, s32[96,2]{0,1:T(2,128)}, u32[]{:S(2)}) copy-start(s32[96,2]{0,1:T(2,128)} %param.8) | copy-start | bytes 2308
  0.0 5.2 %copy-start = (bf16[96,128,128]{2,1,0:T(8,128)(2,1)S(1)}, bf16[96,128,128]{2,1,0:T(8,128)(2,1)}, u32[]{:S(2)}) copy-start(bf16[96,128,128]{2,1,0:T(8,128)(2,1)} %values.1) | copy-start | bytes 9437188
  0.0 7.5 %collective-permute-start = (bf16[128,256]{1,0:T(8,128)(2,1)}, bf16[128,256]{1,0:T(8,128)(2,1)S(1)}, u32[]{:S(2)}, u32[]{:S(2)}) collective-permute-start(bf16[128,256]{1,0:T(8,128)(2,1)} %value.1), channel_id=1, source_target_pairs={{0,24},{1,9},{2,26},{3,11},{4,28},{5,13},{6,30},{7,15},{8,0},{9,17... | collective-permute-start | bytes 196616 | tf_op jit(solution)/shard_map/ppermute | solution.py:148
  5.1 5.4 %collective-permute-start.1 = (bf16[128,256]{1,0:T(8,128)(2,1)}, bf16[128,256]{1,0:T(8,128)(2,1)S(1)}, u32[]{:S(2)}, u32[]{:S(2)}) collective-permute-start(bf16[128,256]{1,0:T(8,128)(2,1)} %value.1), channel_id=1, source_target_pairs={{0,16},{1,17},{2,18},{3,19},{4,20},{5,21},{6,22},{7,23},{8,24},{9,... | collective-permute-start | bytes 196616 | tf_op jit(solution)/shard_map/ppermute | solution.py:148
  5.1 2.4 %collective-permute-start.4 = (bf16[128,256]{1,0:T(8,128)(2,1)}, bf16[128,256]{1,0:T(8,128)(2,1)S(1)}, u32[]{:S(2)}, u32[]{:S(2)}) collective-permute-start(bf16[128,256]{1,0:T(8,128)(2,1)} %value.1), channel_id=1, source_target_pairs={{0,2},{1,3},{2,0},{3,1},{4,6},{5,7},{6,4},{7,5},{8,10},{9,11},{10,... | collective-permute-start | bytes 196616 | tf_op jit(solution)/shard_map/ppermute | solution.py:148
  5.1 2.4 %copy-start.2 = (bf16[128,256]{1,0:T(8,128)(2,1)S(1)}, bf16[128,256]{1,0:T(8,128)(2,1)}, u32[]{:S(2)}) copy-start(bf16[128,256]{1,0:T(8,128)(2,1)} %value.1) | copy-start | bytes 196612
  6.7 3.8 %collective-permute-start.2 = (bf16[256,1408]{1,0:T(8,128)(2,1)S(1)}, bf16[256,1408]{1,0:T(8,128)(2,1)S(1)}, u32[]{:S(2)}, u32[]{:S(2)}) collective-permute-start(bf16[256,1408]{1,0:T(8,128)(2,1)S(1)} %get-tuple-element.10), channel_id=1, source_target_pairs={{0,2},{1,3},{2,0},{3,1},{4,6},{5,7},{6,4},{7,5},{8,10},{9,11},{10,... | collective-permute-start | bytes 2162696 | tf_op jit(solution)/shard_map/ppermute | solution.py:148
  7.5 6.7 %collective-permute-start.7 = (bf16[256,256]{1,0:T(8,128)(2,1)S(1)}, bf16[256,256]{1,0:T(8,128)(2,1)S(1)}, u32[]{:S(2)}, u32[]{:S(2)}) collective-permute-start(bf16[256,256]{1,0:T(8,128)(2,1)S(1)} %get-tuple-element.12), channel_id=1, source_target_pairs={{0,1},{1,0},{2,10},{3,27},{4,5},{5,4},{6,14},{7,31},{8,9},{9,8},{1... | collective-permute-start | bytes 393224 | tf_op jit(solution)/shard_map/ppermute | solution.py:148
  10.5 7.5 %collective-permute-start.3 = (bf16[256,256]{1,0:T(8,128)(2,1)S(1)}, bf16[256,256]{1,0:T(8,128)(2,1)S(1)}, u32[]{:S(2)}, u32[]{:S(2)}) collective-permute-start(bf16[256,256]{1,0:T(8,128)(2,1)S(1)} %shard_map.59), channel_id=1, source_target_pairs={{0,1},{1,0},{2,3},{3,2},{4,5},{5,4},{6,7},{7,6},{8,9},{9,8},{10,11... | collective-permute-start | bytes 393224 | tf_op jit(solution)/shard_map/ppermute | solution.py:148
  11.9 6.6 %collective-permute-start.5 = (bf16[256,256]{1,0:T(8,128)(2,1)S(1)}, bf16[256,256]{1,0:T(8,128)(2,1)S(1)}, u32[]{:S(2)}, u32[]{:S(2)}) collective-permute-start(bf16[256,256]{1,0:T(8,128)(2,1)S(1)} %shard_map.62), channel_id=1, source_target_pairs={{0,5},{1,4},{2,7},{3,6},{4,1},{5,0},{6,3},{7,2},{8,13},{9,12},{10,... | collective-permute-start | bytes 393224 | tf_op jit(solution)/shard_map/ppermute | solution.py:148
  13.6 4.4 %collective-permute-start.6 = (bf16[128,256]{1,0:T(8,128)(2,1)S(1)}, bf16[128,256]{1,0:T(8,128)(2,1)S(1)}, u32[]{:S(2)}, u32[]{:S(2)}) collective-permute-start(bf16[128,256]{1,0:T(8,128)(2,1)S(1)} %shard_map.63), channel_id=1, source_target_pairs={{0,4},{1,5},{2,6},{3,7},{4,0},{5,1},{6,2},{7,3},{8,12},{9,13},{10,... | collective-permute-start | bytes 196616 | tf_op jit(solution)/shard_map/ppermute | solution.py:148
  14.2 4.3 %collective-permute-start.8 = (bf16[256,256]{1,0:T(8,128)(2,1)S(1)}, bf16[256,256]{1,0:T(8,128)(2,1)S(1)}, u32[]{:S(2)}, u32[]{:S(2)}) collective-permute-start(bf16[256,256]{1,0:T(8,128)(2,1)S(1)} %collective-permute-done.7.refs_5_), channel_id=1, source_target_pairs={{0,0},{1,1},{2,6},{3,7},{4,4},{5,5},{6,2},{7,3},{8,8},{9,9},{10,14... | collective-permute-start | bytes 393224 | tf_op jit(solution)/shard_map/ppermute | solution.py:148
  18.5 6.6 %copy-start.1 = (bf16[256,256]{1,0:T(8,128)(2,1)S(1)}, bf16[256,256]{1,0:T(8,128)(2,1)}, u32[]{:S(2)}) copy-start(bf16[256,256]{1,0:T(8,128)(2,1)} %weight.1) | copy-start | bytes 393220
  18.9 1.8 %collective-permute-start.9 = (bf16[256,256]{1,0:T(8,128)(2,1)S(1)}, bf16[256,256]{1,0:T(8,128)(2,1)S(1)}, u32[]{:S(2)}, u32[]{:S(2)}) collective-permute-start(bf16[256,256]{1,0:T(8,128)(2,1)S(1)} %shard_map.66), channel_id=1, source_target_pairs={{0,2},{1,3},{2,0},{3,1},{4,6},{5,7},{6,4},{7,5},{8,10},{9,11},{10,... | collective-permute-start | bytes 393224 | tf_op jit(solution)/shard_map/ppermute | solution.py:148
  20.7 4.4 %collective-permute-start.10 = (bf16[128,256]{1,0:T(8,128)(2,1)S(1)}, bf16[128,256]{1,0:T(8,128)(2,1)S(1)}, u32[]{:S(2)}, u32[]{:S(2)}) collective-permute-start(bf16[128,256]{1,0:T(8,128)(2,1)S(1)} %shard_map.67), channel_id=1, source_target_pairs={{0,1},{1,0},{2,3},{3,2},{4,5},{5,4},{6,7},{7,6},{8,9},{9,8},{10,11... | collective-permute-start | bytes 196616 | tf_op jit(solution)/shard_map/ppermute | solution.py:148

commit v6 on v5

--- a/solution.py
+++ b/solution.py
@@ -168,10 +168,12 @@
     beside = send(ahead, lambda z, x, c, y: (z, 1 - x, c, y) if c else (z, x, c, y))
     arrived = mark(4_000_000_000, along_y, across, along_x)
     held = [own, far, along_y, across, along_x, ahead, beside]
-    other = send(products(taken, held, arrived, jnp.bfloat16), core)
-    mine = products(kept, held, arrived, jnp.float32)
-    theirs = send(partner_sum(mine, other), lambda z, x, c, y: (z, x, c, 1 - y))
-    return mine, other, theirs
+    other = send(products(1, taken, held, arrived, jnp.bfloat16), core)
+    theirs = partner_sum(products(1, kept, held, arrived, jnp.float32), other)
+    theirs = send(theirs, lambda z, x, c, y: (z, x, c, 1 - y))
+    other = send(products(0, taken, held, arrived, jnp.float32), core)
+    mine = products(0, kept, held, arrived, jnp.float32)
+    return mine, other, theirs, mark(2_000_000_000, theirs)
 
 
 def dense_kernel(mark, counts, coords, values, kept, given, total):
@@ -239,39 +241,41 @@
     )(mark, tile_counts, tile_coords, tile_values)
 
 
-def product_kernel(matrix, mark, *refs):
+def product_kernel(first, matrix, mark, *refs):
     out = refs[-1]
+    span = pl.ds(first, out.shape[0])
     total = jnp.zeros(out.shape, jnp.float32)
+    groups = [refs[:2]] + [[ref] for ref in refs[2:4]] + [refs[4:5]] + [[ref] for ref in refs[5:-1]]
     start = 0
-    for block in refs[:-1]:
-        depth = block.shape[0]
-        total += jnp.dot(matrix[:, pl.ds(start, depth)], block[...], preferred_element_type=jnp.float32)
+    for group in groups:
+        rows = jnp.concatenate([ref[...] for ref in group])
+        depth = rows.shape[0]
+        total += jnp.dot(matrix[span, pl.ds(start, depth)], rows, preferred_element_type=jnp.float32)
         start += depth
     out[...] = total.astype(out.dtype)
 
 
-def products(matrix, blocks, mark, dtype):
-    rows = matrix.shape[0]
+def products(half, matrix, blocks, mark, dtype):
+    rows = matrix.shape[0] // 2
     width = blocks[0].shape[1]
     return pl.pallas_call(
-        product_kernel,
+        functools.partial(product_kernel, half * rows),
         out_shape=jax.ShapeDtypeStruct((rows, width), dtype),
         in_specs=[VMEM] * (2 + len(blocks)),
         out_specs=VMEM,
         compiler_params=pltpu.CompilerParams(vmem_limit_bytes=MIDDLE),
-        cost_estimate=pl.CostEstimate(flops=168_000_000, bytes_accessed=1_000_000, transcendentals=0),
+        cost_estimate=pl.CostEstimate(flops=84_000_000, bytes_accessed=1_000_000, transcendentals=0),
     )(matrix, mark, *blocks)
 
 
 def sum_kernel(mine, other, out):
-    rows = pl.ds(out.shape[0], out.shape[0])
-    out[...] = (mine[rows] + other[rows].astype(jnp.float32)).astype(out.dtype)
+    out[...] = (mine[...] + other[...].astype(jnp.float32)).astype(out.dtype)
 
 
 def partner_sum(mine, other):
     return pl.pallas_call(
         sum_kernel,
-        out_shape=jax.ShapeDtypeStruct((mine.shape[0] // 2, mine.shape[1]), other.dtype),
+        out_shape=jax.ShapeDtypeStruct(other.shape, other.dtype),
         in_specs=[VMEM] * 2,
         out_specs=VMEM,
         compiler_params=pltpu.CompilerParams(vmem_limit_bytes=SMALL),
@@ -279,28 +283,27 @@
     )(mine, other)
 
 
-def last_kernel(mine, other, theirs, weight, out):
-    rows = pl.ds(0, out.shape[0])
-    sums = mine[rows] + other[rows].astype(jnp.float32) + theirs[...].astype(jnp.float32)
+def last_kernel(theirs, mine, other, weight, mark, out):
+    sums = mine[...] + other[...] + theirs[...].astype(jnp.float32)
     product = jnp.dot(sums.astype(jnp.bfloat16), weight[...], preferred_element_type=jnp.float32)
     out[...] = jnp.maximum(product, 0.0).astype(out.dtype)
 
 
-def last(mine, other, theirs, weight):
+def last(mine, other, theirs, weight, mark):
     return pl.pallas_call(
         last_kernel,
         out_shape=jax.ShapeDtypeStruct(theirs.shape, jnp.bfloat16),
-        in_specs=[VMEM] * 4,
+        in_specs=[VMEM] * 5,
         out_specs=VMEM,
         compiler_params=pltpu.CompilerParams(vmem_limit_bytes=SMALL),
         cost_estimate=pl.CostEstimate(flops=17_000_000, bytes_accessed=400_000, transcendentals=0),
-    )(mine, other, theirs, weight)
+    )(theirs, mine, other, weight, mark)
 
 
 def pairs(features, weight, tile_values, tile_coords, tile_counts):
     planes = lax.axis_size("loop") // 4
-    mine, other, theirs = spread(features, planes, tile_counts, tile_coords.T, tile_values)
-    return last(mine, other, theirs, weight)
+    mine, other, theirs, arrived = spread(features, planes, tile_counts, tile_coords.T, tile_values)
+    return last(mine, other, theirs, weight, arrived)
 
 
 def solution(mesh):

time: 26.4 us -> 26.1 us (0.989); the launches traced: 25.9 us -> 26.1 us
  Pallas kernels: 3.21 us -> 3.49 us
    pallas_call x3 -> x5, Pallas kernels: 0.79 us -> 1.1 us  [the longest x4 1.08 us: products(): pl.pallas_call(functools.partial(product_kernel, half * rows), out_shape=...]
    ppermute x11 -> x12, starting transfers between devices: 14.6 us -> 14.6 us  [send(): return lax.ppermute(value, AXES, route(planes, move))]
    ppermute x11 -> x12, waiting for transfers between devices: 7.96 us -> 7.89 us  [send(): return lax.ppermute(value, AXES, route(planes, move))]
  transfers between devices with their start and end apart: 11 -> 12, of which waited for: 6 -> 5; matrix products, arithmetic and copies ran while one was open for 0% -> 0% of each run, Pallas kernels for 8% -> 9%
where the time goes in v6:
time: 26.1 us
  starting transfers between devices  14.6 us (56%)
  waiting for transfers between devices  7.89 us (30%)
  Pallas kernels  3.49 us (13%)
    ppermute x12, starting transfers between devices, send(): return lax.ppermute(value, AXES, route(planes, move))  14.6 us
    ppermute x12, waiting for transfers between devices, send(): return lax.ppermute(value, AXES, route(planes, move))  7.89 us
    pallas_call x1, Pallas kernels, dense(): pl.pallas_call(dense_kernel, out_shape=[jax.ShapeDtypeStruct((2 * tile, H...  1.52 us
    pallas_call x4, Pallas kernels, products(): pl.pallas_call(functools.partial(product_kernel, half * rows), out_shape=...  1.08 us
    pallas_call x1, Pallas kernels, last(): pl.pallas_call(last_kernel, out_shape=jax.ShapeDtypeStruct(theirs.shape,...  0.81 us
  transfers between devices with their start and end apart: 12, of which 5 were waited for; matrix products, arithmetic and copies ran while one was open for 0% of the time, Pallas kernels for 9%

profile of v6, /device:TPU:0, one launch (start us, length us, event | category | flops | bytes accessed | tf_op | source)
XLA Modules:
  0.0 26.1 jit_solution(16254563018472683118)
XLA Ops:
  0.0 5.1 %collective-permute-start = (bf16[128,256]{1,0:T(8,128)(2,1)}, bf16[128,256]{1,0:T(8,128)(2,1)S(1)}, u32[]{:S(2)}, u32[]{:S(2)}) collective-permute-start(bf16[128,256]{1,0:T(8,128)(2,1)} %value.1), channel_id=1, source_target_pairs={{0,24},{1,9},{2,26},{3,11},{4,28},{5,13},{6,30},{7,15},{8,0},{9,17... | collective-permute-start | bytes 196616 | tf_op jit(solution)/shard_map/ppermute | solution.py:148
  5.1 0.0 collective-permute-start.1
  5.1 0.0 collective-permute-start.4
  5.1 0.0 copy-start.2
  5.2 1.5 %shard_map.56 = (bf16[256,1408]{1,0:T(8,128)(2,1)S(1)}, bf16[256,1408]{1,0:T(8,128)(2,1)S(1)}) custom-call(bf16[16,128]{1,0:T(8,128)(2,1)S(1)} %shard_map.55.mark, s32[1,8]{1,0:T(1,128)S(1)} %copy-done.4, s32[2,96]{1,0:T(2,128)S(1)} %bitcast.1, bf16[96,128,128]{2,1,0:T(8,128)(2,1)S(1)} %copy-done), custom_call_target="tpu_custom_call" | custom-call | flops 1 | bytes 1 | tf_op jit(solution)/shard_map/pallas_call | solution.py:233
  6.7 0.5 %collective-permute-start.2 = (bf16[256,1408]{1,0:T(8,128)(2,1)S(1)}, bf16[256,1408]{1,0:T(8,128)(2,1)S(1)}, u32[]{:S(2)}, u32[]{:S(2)}) collective-permute-start(bf16[256,1408]{1,0:T(8,128)(2,1)S(1)} %get-tuple-element.10), channel_id=1, source_target_pairs={{0,2},{1,3},{2,0},{3,1},{4,6},{5,7},{6,4},{7,5},{8,10},{9,11},{10,... | collective-permute-start | bytes 2162696 | tf_op jit(solution)/shard_map/ppermute | solution.py:148
  7.2 0.3 %collective-permute-done.refs_0_.refs_1_ = bf16[128,256]{1,0:T(8,128)(2,1)S(1)} collective-permute-done((bf16[128,256]{1,0:T(8,128)(2,1)}, bf16[128,256]{1,0:T(8,128)(2,1)S(1)}, u32[]{:S(2)}, u32[]{:S(2)}) %collective-permute-start) | collective-permute-done | bytes 65568 | tf_op jit(solution)/shard_map/ppermute | solution.py:148
  7.5 0.0 collective-permute-done.4.mate
  7.5 2.3 %collective-permute-start.7 = (bf16[256,256]{1,0:T(8,128)(2,1)S(1)}, bf16[256,256]{1,0:T(8,128)(2,1)S(1)}, u32[]{:S(2)}, u32[]{:S(2)}) collective-permute-start(bf16[256,256]{1,0:T(8,128)(2,1)S(1)} %get-tuple-element.12), channel_id=1, source_target_pairs={{0,1},{1,0},{2,10},{3,27},{4,5},{5,4},{6,14},{7,31},{8,9},{9,8},{1... | collective-permute-start | bytes 393224 | tf_op jit(solution)/shard_map/ppermute | solution.py:148
  9.8 0.7 %collective-permute-done.1.refs_0_.refs_1_.refs_2_ = bf16[128,256]{1,0:T(8,128)(2,1)S(1)} collective-permute-done((bf16[128,256]{1,0:T(8,128)(2,1)}, bf16[128,256]{1,0:T(8,128)(2,1)S(1)}, u32[]{:S(2)}, u32[]{:S(2)}) %collective-permute-start.1) | collective-permute-done | bytes 65568 | tf_op jit(solution)/shard_map/ppermute | solution.py:148
  10.5 0.0 collective-permute-done.2.refs_0_.matrix
  10.5 1.3 %collective-permute-start.3 = (bf16[256,256]{1,0:T(8,128)(2,1)S(1)}, bf16[256,256]{1,0:T(8,128)(2,1)S(1)}, u32[]{:S(2)}, u32[]{:S(2)}) collective-permute-start(bf16[256,256]{1,0:T(8,128)(2,1)S(1)} %shard_map.59), channel_id=1, source_target_pairs={{0,1},{1,0},{2,3},{3,2},{4,5},{5,4},{6,7},{7,6},{8,9},{9,8},{10,11... | collective-permute-start | bytes 393224 | tf_op jit(solution)/shard_map/ppermute | solution.py:148
  11.9 1.8 %collective-permute-start.5 = (bf16[256,256]{1,0:T(8,128)(2,1)S(1)}, bf16[256,256]{1,0:T(8,128)(2,1)S(1)}, u32[]{:S(2)}, u32[]{:S(2)}) collective-permute-start(bf16[256,256]{1,0:T(8,128)(2,1)S(1)} %shard_map.62), channel_id=1, source_target_pairs={{0,5},{1,4},{2,7},{3,6},{4,1},{5,0},{6,3},{7,2},{8,13},{9,12},{10,... | collective-permute-start | bytes 393224 | tf_op jit(solution)/shard_map/ppermute | solution.py:148
  13.6 0.5 %collective-permute-start.6 = (bf16[128,256]{1,0:T(8,128)(2,1)S(1)}, bf16[128,256]{1,0:T(8,128)(2,1)S(1)}, u32[]{:S(2)}, u32[]{:S(2)}) collective-permute-start(bf16[128,256]{1,0:T(8,128)(2,1)S(1)} %shard_map.63), channel_id=1, source_target_pairs={{0,4},{1,5},{2,6},{3,7},{4,0},{5,1},{6,2},{7,3},{8,12},{9,13},{10,... | collective-permute-start | bytes 196616 | tf_op jit(solution)/shard_map/ppermute | solution.py:148
  14.2 0.0 collective-permute-done.7.refs_5_
  14.2 0.7 %collective-permute-start.8 = (bf16[256,256]{1,0:T(8,128)(2,1)S(1)}, bf16[256,256]{1,0:T(8,128)(2,1)S(1)}, u32[]{:S(2)}, u32[]{:S(2)}) collective-permute-start(bf16[256,256]{1,0:T(8,128)(2,1)S(1)} %collective-permute-done.7.refs_5_), channel_id=1, source_target_pairs={{0,0},{1,1},{2,6},{3,7},{4,4},{5,5},{6,2},{7,3},{8,8},{9,9},{10,14... | collective-permute-start | bytes 393224 | tf_op jit(solution)/shard_map/ppermute | solution.py:148
  14.8 4.4 %collective-permute-done.6.refs_2_.refs_4_ = bf16[128,256]{1,0:T(8,128)(2,1)S(1)} collective-permute-done((bf16[128,256]{1,0:T(8,128)(2,1)S(1)}, bf16[128,256]{1,0:T(8,128)(2,1)S(1)}, u32[]{:S(2)}, u32[]{:S(2)}) %collective-permute-start.6) | collective-permute-done | bytes 65568 | tf_op jit(solution)/shard_map/ppermute | solution.py:148
  19.2 0.0 collective-permute-done.3.refs_0_.refs_2_
  19.2 0.0 collective-permute-done.5.refs_1_.refs_3_
  19.2 0.0 collective-permute-done.8.refs_6_
  19.2 0.3 %shard_map.66 = bf16[128,256]{1,0:T(8,128)(2,1)S(1)} custom-call(bf16[256,1408]{1,0:T(8,128)(2,1)S(1)} %collective-permute-done.2.refs_0_.matrix, bf16[16,128]{1,0:T(8,128)(2,1)S(1)} %shard_map.64.mark, bf16[128,256]{1,0:T(8,128)(2,1)S(1)} %get-tuple-element.11.refs_0_, bf16[128,256]{1,0:T(8,128)(2,1)S(1)} %collective-permute-done.1.refs_0_.refs_1_.refs_2_, ...), custom_call_target="tpu_custom_call" | custom-call | flops 84000000 | bytes 1000000 | tf_op jit(solution)/shard_map/pallas_call | solution.py:261
  19.5 0.4 %collective-permute-start.9 = (bf16[128,256]{1,0:T(8,128)(2,1)S(1)}, bf16[128,256]{1,0:T(8,128)(2,1)S(1)}, u32[]{:S(2)}, u32[]{:S(2)}) collective-permute-start(bf16[128,256]{1,0:T(8,128)(2,1)S(1)} %shard_map.66), channel_id=1, source_target_pairs={{0,2},{1,3},{2,0},{3,1},{4,6},{5,7},{6,4},{7,5},{8,10},{9,11},{10,... | collective-permute-start | bytes 196616 | tf_op jit(solution)/shard_map/ppermute | solution.py:148
  19.9 0.3 %shard_map.65.mine = f32[128,256]{1,0:T(8,128)S(1)} custom-call(bf16[256,1408]{1,0:T(8,128)(2,1)S(1)} %get-tuple-element.9.matrix, bf16[16,128]{1,0:T(8,128)(2,1)S(1)} %shard_map.64.mark, bf16[128,256]{1,0:T(8,128)(2,1)S(1)} %get-tuple-element.11.refs_0_, bf16[128,256]{1,0:T(8,128)(2,1)S(1)} %collective-permute-done.1.refs_0_.refs_1_.refs_2_, ...), custom_call_target="tpu_custom_call" | custom-call | flops 84000000 | bytes 1000000 | tf_op jit(solution)/shard_map/pallas_call | solution.py:261
  20.2 0.6 %collective-permute-done.9.other = bf16[128,256]{1,0:T(8,128)(2,1)S(1)} collective-permute-done((bf16[128,256]{1,0:T(8,128)(2,1)S(1)}, bf16[128,256]{1,0:T(8,128)(2,1)S(1)}, u32[]{:S(2)}, u32[]{:S(2)}) %collective-permute-start.9) | collective-permute-done | bytes 65568 | tf_op jit(solution)/shard_map/ppermute | solution.py:148
  20.9 1.8 %collective-permute-start.10 = (bf16[128,256]{1,0:T(8,128)(2,1)S(1)}, bf16[128,256]{1,0:T(8,128)(2,1)S(1)}, u32[]{:S(2)}, u32[]{:S(2)}) collective-permute-start(bf16[128,256]{1,0:T(8,128)(2,1)S(1)} %shard_map.67), channel_id=1, source_target_pairs={{0,1},{1,0},{2,3},{3,2},{4,5},{5,4},{6,7},{7,6},{8,9},{9,8},{10,11... | collective-permute-start | bytes 196616 | tf_op jit(solution)/shard_map/ppermute | solution.py:148
  22.6 0.3 %shard_map.69 = f32[128,256]{1,0:T(8,128)S(1)} custom-call(bf16[256,1408]{1,0:T(8,128)(2,1)S(1)} %collective-permute-done.2.refs_0_.matrix, bf16[16,128]{1,0:T(8,128)(2,1)S(1)} %shard_map.64.mark, bf16[128,256]{1,0:T(8,128)(2,1)S(1)} %get-tuple-element.11.refs_0_, bf16[128,256]{1,0:T(8,128)(2,1)S(1)} %collective-permute-done.1.refs_0_.refs_1_.refs_2_, ...), custom_call_target="tpu_custom_call" | custom-call | flops 84000000 | bytes 1000000 | tf_op jit(solution)/shard_map/pallas_call | solution.py:261
  22.9 0.1 collective-permute-start.11
  23.1 0.3 %shard_map.68.mine = f32[128,256]{1,0:T(8,128)S(1)} custom-call(bf16[256,1408]{1,0:T(8,128)(2,1)S(1)} %get-tuple-element.9.matrix, bf16[16,128]{1,0:T(8,128)(2,1)S(1)} %shard_map.64.mark, bf16[128,256]{1,0:T(8,128)(2,1)S(1)} %get-tuple-element.11.refs_0_, bf16[128,256]{1,0:T(8,128)(2,1)S(1)} %collective-permute-done.1.refs_0_.refs_1_.refs_2_, ...), custom_call_target="tpu_custom_call" | custom-call | flops 84000000 | bytes 1000000 | tf_op jit(solution)/shard_map/pallas_call | solution.py:261
  23.3 0.0 copy-start.1
  23.3 1.9 %collective-permute-done.10.refs_0_.theirs = bf16[128,256]{1,0:T(8,128)(2,1)S(1)} collective-permute-done((bf16[128,256]{1,0:T(8,128)(2,1)S(1)}, bf16[128,256]{1,0:T(8,128)(2,1)S(1)}, u32[]{:S(2)}, u32[]{:S(2)}) %collective-permute-start.10) | collective-permute-done | bytes 65568 | tf_op jit(solution)/shard_map/ppermute | solution.py:148
  25.3 0.0 collective-permute-done.11.other
  25.3 0.8 %shard_map.71 = bf16[128,256]{1,0:T(8,128)(2,1)} custom-call(bf16[128,256]{1,0:T(8,128)(2,1)S(1)} %collective-permute-done.10.refs_0_.theirs, f32[128,256]{1,0:T(8,128)S(1)} %shard_map.68.mine, f32[128,256]{1,0:T(8,128)S(1)} %collective-permute-done.11.other, bf16[256,256]{1,0:T(8,128)(2,1)S(1)} %copy-done.1, bf16[16,128]{1,0:T(8,128)(2,1)S(1)} %shard_map.70.mark), custom_call_target="tpu_custom_call" | custom-call | flops 17000000 | bytes 400000 | tf_op jit(solution)/shard_map/pallas_call | solution.py:293
  (19 shorter events, 0.1 us)
Async XLA Ops:
  0.0 5.1 %copy-start.4 = (s32[1,8]{1,0:T(1,128)S(1)}, s32[1,8]{1,0:T(1,128)}, u32[]{:S(2)}) copy-start(s32[1,8]{1,0:T(1,128)} %counts.1) | copy-start | bytes 100
  0.0 5.1 %copy-start.3 = (s32[96,2]{0,1:T(2,128)S(1)}, s32[96,2]{0,1:T(2,128)}, u32[]{:S(2)}) copy-start(s32[96,2]{0,1:T(2,128)} %param.8) | copy-start | bytes 2308
  0.0 5.2 %copy-start = (bf16[96,128,128]{2,1,0:T(8,128)(2,1)S(1)}, bf16[96,128,128]{2,1,0:T(8,128)(2,1)}, u32[]{:S(2)}) copy-start(bf16[96,128,128]{2,1,0:T(8,128)(2,1)} %values.1) | copy-start | bytes 9437188
  0.0 7.5 %collective-permute-start = (bf16[128,256]{1,0:T(8,128)(2,1)}, bf16[128,256]{1,0:T(8,128)(2,1)S(1)}, u32[]{:S(2)}, u32[]{:S(2)}) collective-permute-start(bf16[128,256]{1,0:T(8,128)(2,1)} %value.1), channel_id=1, source_target_pairs={{0,24},{1,9},{2,26},{3,11},{4,28},{5,13},{6,30},{7,15},{8,0},{9,17... | collective-permute-start | bytes 196616 | tf_op jit(solution)/shard_map/ppermute | solution.py:148
  5.1 5.4 %collective-permute-start.1 = (bf16[128,256]{1,0:T(8,128)(2,1)}, bf16[128,256]{1,0:T(8,128)(2,1)S(1)}, u32[]{:S(2)}, u32[]{:S(2)}) collective-permute-start(bf16[128,256]{1,0:T(8,128)(2,1)} %value.1), channel_id=1, source_target_pairs={{0,16},{1,17},{2,18},{3,19},{4,20},{5,21},{6,22},{7,23},{8,24},{9,... | collective-permute-start | bytes 196616 | tf_op jit(solution)/shard_map/ppermute | solution.py:148
  5.1 2.4 %collective-permute-start.4 = (bf16[128,256]{1,0:T(8,128)(2,1)}, bf16[128,256]{1,0:T(8,128)(2,1)S(1)}, u32[]{:S(2)}, u32[]{:S(2)}) collective-permute-start(bf16[128,256]{1,0:T(8,128)(2,1)} %value.1), channel_id=1, source_target_pairs={{0,2},{1,3},{2,0},{3,1},{4,6},{5,7},{6,4},{7,5},{8,10},{9,11},{10,... | collective-permute-start | bytes 196616 | tf_op jit(solution)/shard_map/ppermute | solution.py:148
  5.1 2.4 %copy-start.2 = (bf16[128,256]{1,0:T(8,128)(2,1)S(1)}, bf16[128,256]{1,0:T(8,128)(2,1)}, u32[]{:S(2)}) copy-start(bf16[128,256]{1,0:T(8,128)(2,1)} %value.1) | copy-start | bytes 196612
  6.7 3.8 %collective-permute-start.2 = (bf16[256,1408]{1,0:T(8,128)(2,1)S(1)}, bf16[256,1408]{1,0:T(8,128)(2,1)S(1)}, u32[]{:S(2)}, u32[]{:S(2)}) collective-permute-start(bf16[256,1408]{1,0:T(8,128)(2,1)S(1)} %get-tuple-element.10), channel_id=1, source_target_pairs={{0,2},{1,3},{2,0},{3,1},{4,6},{5,7},{6,4},{7,5},{8,10},{9,11},{10,... | collective-permute-start | bytes 2162696 | tf_op jit(solution)/shard_map/ppermute | solution.py:148
  7.5 6.7 %collective-permute-start.7 = (bf16[256,256]{1,0:T(8,128)(2,1)S(1)}, bf16[256,256]{1,0:T(8,128)(2,1)S(1)}, u32[]{:S(2)}, u32[]{:S(2)}) collective-permute-start(bf16[256,256]{1,0:T(8,128)(2,1)S(1)} %get-tuple-element.12), channel_id=1, source_target_pairs={{0,1},{1,0},{2,10},{3,27},{4,5},{5,4},{6,14},{7,31},{8,9},{9,8},{1... | collective-permute-start | bytes 393224 | tf_op jit(solution)/shard_map/ppermute | solution.py:148
  10.5 8.7 %collective-permute-start.3 = (bf16[256,256]{1,0:T(8,128)(2,1)S(1)}, bf16[256,256]{1,0:T(8,128)(2,1)S(1)}, u32[]{:S(2)}, u32[]{:S(2)}) collective-permute-start(bf16[256,256]{1,0:T(8,128)(2,1)S(1)} %shard_map.59), channel_id=1, source_target_pairs={{0,1},{1,0},{2,3},{3,2},{4,5},{5,4},{6,7},{7,6},{8,9},{9,8},{10,11... | collective-permute-start | bytes 393224 | tf_op jit(solution)/shard_map/ppermute | solution.py:148
  11.9 7.4 %collective-permute-start.5 = (bf16[256,256]{1,0:T(8,128)(2,1)S(1)}, bf16[256,256]{1,0:T(8,128)(2,1)S(1)}, u32[]{:S(2)}, u32[]{:S(2)}) collective-permute-start(bf16[256,256]{1,0:T(8,128)(2,1)S(1)} %shard_map.62), channel_id=1, source_target_pairs={{0,5},{1,4},{2,7},{3,6},{4,1},{5,0},{6,3},{7,2},{8,13},{9,12},{10,... | collective-permute-start | bytes 393224 | tf_op jit(solution)/shard_map/ppermute | solution.py:148
  13.6 5.6 %collective-permute-start.6 = (bf16[128,256]{1,0:T(8,128)(2,1)S(1)}, bf16[128,256]{1,0:T(8,128)(2,1)S(1)}, u32[]{:S(2)}, u32[]{:S(2)}) collective-permute-start(bf16[128,256]{1,0:T(8,128)(2,1)S(1)} %shard_map.63), channel_id=1, source_target_pairs={{0,4},{1,5},{2,6},{3,7},{4,0},{5,1},{6,2},{7,3},{8,12},{9,13},{10,... | collective-permute-start | bytes 196616 | tf_op jit(solution)/shard_map/ppermute | solution.py:148
  14.2 5.0 %collective-permute-start.8 = (bf16[256,256]{1,0:T(8,128)(2,1)S(1)}, bf16[256,256]{1,0:T(8,128)(2,1)S(1)}, u32[]{:S(2)}, u32[]{:S(2)}) collective-permute-start(bf16[256,256]{1,0:T(8,128)(2,1)S(1)} %collective-permute-done.7.refs_5_), channel_id=1, source_target_pairs={{0,0},{1,1},{2,6},{3,7},{4,4},{5,5},{6,2},{7,3},{8,8},{9,9},{10,14... | collective-permute-start | bytes 393224 | tf_op jit(solution)/shard_map/ppermute | solution.py:148
  19.5 1.3 %collective-permute-start.9 = (bf16[128,256]{1,0:T(8,128)(2,1)S(1)}, bf16[128,256]{1,0:T(8,128)(2,1)S(1)}, u32[]{:S(2)}, u32[]{:S(2)}) collective-permute-start(bf16[128,256]{1,0:T(8,128)(2,1)S(1)} %shard_map.66), channel_id=1, source_target_pairs={{0,2},{1,3},{2,0},{3,1},{4,6},{5,7},{6,4},{7,5},{8,10},{9,11},{10,... | collective-permute-start | bytes 196616 | tf_op jit(solution)/shard_map/ppermute | solution.py:148
  20.9 4.4 %collective-permute-start.10 = (bf16[128,256]{1,0:T(8,128)(2,1)S(1)}, bf16[128,256]{1,0:T(8,128)(2,1)S(1)}, u32[]{:S(2)}, u32[]{:S(2)}) collective-permute-start(bf16[128,256]{1,0:T(8,128)(2,1)S(1)} %shard_map.67), channel_id=1, source_target_pairs={{0,1},{1,0},{2,3},{3,2},{4,5},{5,4},{6,7},{7,6},{8,9},{9,8},{10,11... | collective-permute-start | bytes 196616 | tf_op jit(solution)/shard_map/ppermute | solution.py:148
  22.9 2.4 %collective-permute-start.11 = (f32[128,256]{1,0:T(8,128)S(1)}, f32[128,256]{1,0:T(8,128)S(1)}, u32[]{:S(2)}, u32[]{:S(2)}) collective-permute-start(f32[128,256]{1,0:T(8,128)S(1)} %shard_map.69), channel_id=1, source_target_pairs={{0,2},{1,3},{2,0},{3,1},{4,6},{5,7},{6,4},{7,5},{8,10},{9,11},{10,... | collective-permute-start | bytes 393224 | tf_op jit(solution)/shard_map/ppermute | solution.py:148
  23.3 2.0 %copy-start.1 = (bf16[256,256]{1,0:T(8,128)(2,1)S(1)}, bf16[256,256]{1,0:T(8,128)(2,1)}, u32[]{:S(2)}) copy-start(bf16[256,256]{1,0:T(8,128)(2,1)} %weight.1) | copy-start | bytes 393220

commit v7 on v6

--- a/solution.py
+++ b/solution.py
@@ -168,9 +168,9 @@
     beside = send(ahead, lambda z, x, c, y: (z, 1 - x, c, y) if c else (z, x, c, y))
     arrived = mark(4_000_000_000, along_y, across, along_x)
     held = [own, far, along_y, across, along_x, ahead, beside]
-    other = send(products(1, taken, held, arrived, jnp.bfloat16), core)
-    theirs = partner_sum(products(1, kept, held, arrived, jnp.float32), other)
-    theirs = send(theirs, lambda z, x, c, y: (z, x, c, 1 - y))
+    crossing = send(products(1, kept, held, arrived, jnp.bfloat16), core)
+    theirs = partner_sum(products(1, taken, held, arrived, jnp.float32), crossing)
+    theirs = send(theirs, lambda z, x, c, y: (z, x, 1 - c, 1 - y))
     other = send(products(0, taken, held, arrived, jnp.float32), core)
     mine = products(0, kept, held, arrived, jnp.float32)
     return mine, other, theirs, mark(2_000_000_000, theirs)
@@ -186,7 +186,7 @@
     kept[...] = jnp.zeros_like(kept)
     given[...] = jnp.zeros_like(given)
 
-    def one(step, carry):
+    def one(step):
         total[...] = jnp.zeros_like(total)
 
         def add(slot, carry):
@@ -223,9 +223,8 @@
                         piece = total[row * 2 + column].astype(jnp.bfloat16)
                         out[pl.ds(row * tile, tile), pl.ds(start, tile)] = piece
 
-        return carry
-
-    lax.fori_loop(0, steps, one, 0)
+    for step in range(steps):
+        one(step)
 
 
 def dense(mark, tile_counts, tile_coords, tile_values):
@@ -241,16 +240,24 @@
     )(mark, tile_counts, tile_coords, tile_values)
 
 
+def dots(matrix, rows, blocks):
+    total = jnp.zeros((rows.size, blocks[0].shape[1]), jnp.float32)
+    start = 0
+    for block in blocks:
+        depth = block.shape[0]
+        total += jnp.dot(matrix[rows, pl.ds(start, depth)], block[...], preferred_element_type=jnp.float32)
+        start += depth
+    return total
+
+
 def product_kernel(first, matrix, mark, *refs):
     out = refs[-1]
-    span = pl.ds(first, out.shape[0])
+    rows = pl.ds(first, out.shape[0])
     total = jnp.zeros(out.shape, jnp.float32)
-    groups = [refs[:2]] + [[ref] for ref in refs[2:4]] + [refs[4:5]] + [[ref] for ref in refs[5:-1]]
     start = 0
-    for group in groups:
-        rows = jnp.concatenate([ref[...] for ref in group])
-        depth = rows.shape[0]
-        total += jnp.dot(matrix[span, pl.ds(start, depth)], rows, preferred_element_type=jnp.float32)
+    for block in refs[:-1]:
+        depth = block.shape[0]
+        total += jnp.dot(matrix[rows, pl.ds(start, depth)], block[...], preferred_element_type=jnp.float32)
         start += depth
     out[...] = total.astype(out.dtype)
 
@@ -275,7 +282,7 @@
 def partner_sum(mine, other):
     return pl.pallas_call(
         sum_kernel,
-        out_shape=jax.ShapeDtypeStruct(other.shape, other.dtype),
+        out_shape=jax.ShapeDtypeStruct(mine.shape, other.dtype),
         in_specs=[VMEM] * 2,
         out_specs=VMEM,
         compiler_params=pltpu.CompilerParams(vmem_limit_bytes=SMALL),
@@ -302,8 +309,8 @@
 
 def pairs(features, weight, tile_values, tile_coords, tile_counts):
     planes = lax.axis_size("loop") // 4
-    mine, other, theirs, arrived = spread(features, planes, tile_counts, tile_coords.T, tile_values)
-    return last(mine, other, theirs, weight, arrived)
+    mine, other, theirs, late = spread(features, planes, tile_counts, tile_coords.T, tile_values)
+    return last(mine, other, theirs, weight, late)
 
 
 def solution(mesh):

time: 26.1 us -> 26 us (level)
  starting transfers between devices: 14.6 us -> 14.3 us
    ppermute x12, starting transfers between devices: 14.6 us -> 14.3 us  [send(): return lax.ppermute(value, AXES, route(planes, move))]
where the time goes in v7:
time: 26 us; the launch traced here: 25.9 us
  starting transfers between devices  14.3 us (55%)
  waiting for transfers between devices  8.08 us (31%)
  Pallas kernels  3.42 us (13%)
    ppermute x12, starting transfers between devices, send(): return lax.ppermute(value, AXES, route(planes, move))  14.3 us
    ppermute x12, waiting for transfers between devices, send(): return lax.ppermute(value, AXES, route(planes, move))  8.08 us
    pallas_call x1, Pallas kernels, dense(): pl.pallas_call(dense_kernel, out_shape=[jax.ShapeDtypeStruct((2 * tile, H...  1.42 us
    pallas_call x4, Pallas kernels, products(): pl.pallas_call(functools.partial(product_kernel, half * rows), out_shape=...  1.11 us
    pallas_call x1, Pallas kernels, last(): pl.pallas_call(last_kernel, out_shape=jax.ShapeDtypeStruct(theirs.shape,...  0.81 us
  transfers between devices with their start and end apart: 12, of which 5 were waited for; matrix products, arithmetic and copies ran while one was open for 0% of the time, Pallas kernels for 9%

profile of v7, /device:TPU:0, one launch (start us, length us, event | category | flops | bytes accessed | tf_op | source)
XLA Modules:
  0.0 25.9 jit_solution(7668522990849449271)
XLA Ops:
  0.0 5.1 %collective-permute-start.1 = (bf16[128,256]{1,0:T(8,128)(2,1)}, bf16[128,256]{1,0:T(8,128)(2,1)S(1)}, u32[]{:S(2)}, u32[]{:S(2)}) collective-permute-start(bf16[128,256]{1,0:T(8,128)(2,1)} %value.1), channel_id=1, source_target_pairs={{0,24},{1,9},{2,26},{3,11},{4,28},{5,13},{6,30},{7,15},{8,0},{9,17... | collective-permute-start | bytes 196616 | tf_op jit(solution)/shard_map/ppermute | solution.py:148
  5.1 0.0 collective-permute-start.2
  5.1 0.0 collective-permute-start.4
  5.1 0.0 copy-start.2
  5.2 1.4 %shard_map.56 = (bf16[256,1408]{1,0:T(8,128)(2,1)S(1)}, bf16[256,1408]{1,0:T(8,128)(2,1)S(1)}) custom-call(bf16[16,128]{1,0:T(8,128)(2,1)S(1)} %shard_map.55.mark, s32[1,8]{1,0:T(1,128)S(1)} %copy-done.4, s32[2,96]{1,0:T(2,128)S(1)} %bitcast.1, bf16[96,128,128]{2,1,0:T(8,128)(2,1)S(1)} %copy-done), custom_call_target="tpu_custom_call" | custom-call | flops 1 | bytes 1 | tf_op jit(solution)/shard_map/pallas_call | solution.py:232
  6.6 0.5 %collective-permute-start = (bf16[256,1408]{1,0:T(8,128)(2,1)S(1)}, bf16[256,1408]{1,0:T(8,128)(2,1)S(1)}, u32[]{:S(2)}, u32[]{:S(2)}) collective-permute-start(bf16[256,1408]{1,0:T(8,128)(2,1)S(1)} %get-tuple-element.9), channel_id=1, source_target_pairs={{0,2},{1,3},{2,0},{3,1},{4,6},{5,7},{6,4},{7,5},{8,10},{9,11},{10,... | collective-permute-start | bytes 2162696 | tf_op jit(solution)/shard_map/ppermute | solution.py:148
  7.1 0.4 %collective-permute-done.1.refs_0_.refs_1_ = bf16[128,256]{1,0:T(8,128)(2,1)S(1)} collective-permute-done((bf16[128,256]{1,0:T(8,128)(2,1)}, bf16[128,256]{1,0:T(8,128)(2,1)S(1)}, u32[]{:S(2)}, u32[]{:S(2)}) %collective-permute-start.1) | collective-permute-done | bytes 65568 | tf_op jit(solution)/shard_map/ppermute | solution.py:148
  7.5 0.0 collective-permute-done.4.mate
  7.5 2.3 %collective-permute-start.7 = (bf16[256,256]{1,0:T(8,128)(2,1)S(1)}, bf16[256,256]{1,0:T(8,128)(2,1)S(1)}, u32[]{:S(2)}, u32[]{:S(2)}) collective-permute-start(bf16[256,256]{1,0:T(8,128)(2,1)S(1)} %get-tuple-element.12), channel_id=1, source_target_pairs={{0,1},{1,0},{2,10},{3,27},{4,5},{5,4},{6,14},{7,31},{8,9},{9,8},{1... | collective-permute-start | bytes 393224 | tf_op jit(solution)/shard_map/ppermute | solution.py:148
  9.8 0.7 %collective-permute-done.2.refs_0_.refs_1_.refs_2_ = bf16[128,256]{1,0:T(8,128)(2,1)S(1)} collective-permute-done((bf16[128,256]{1,0:T(8,128)(2,1)}, bf16[128,256]{1,0:T(8,128)(2,1)S(1)}, u32[]{:S(2)}, u32[]{:S(2)}) %collective-permute-start.2) | collective-permute-done | bytes 65568 | tf_op jit(solution)/shard_map/ppermute | solution.py:148
  10.5 0.0 collective-permute-done.refs_0_.matrix
  10.5 1.3 %collective-permute-start.3 = (bf16[256,256]{1,0:T(8,128)(2,1)S(1)}, bf16[256,256]{1,0:T(8,128)(2,1)S(1)}, u32[]{:S(2)}, u32[]{:S(2)}) collective-permute-start(bf16[256,256]{1,0:T(8,128)(2,1)S(1)} %shard_map.59), channel_id=1, source_target_pairs={{0,1},{1,0},{2,3},{3,2},{4,5},{5,4},{6,7},{7,6},{8,9},{9,8},{10,11... | collective-permute-start | bytes 393224 | tf_op jit(solution)/shard_map/ppermute | solution.py:148
  11.9 1.8 %collective-permute-start.5 = (bf16[256,256]{1,0:T(8,128)(2,1)S(1)}, bf16[256,256]{1,0:T(8,128)(2,1)S(1)}, u32[]{:S(2)}, u32[]{:S(2)}) collective-permute-start(bf16[256,256]{1,0:T(8,128)(2,1)S(1)} %shard_map.62), channel_id=1, source_target_pairs={{0,5},{1,4},{2,7},{3,6},{4,1},{5,0},{6,3},{7,2},{8,13},{9,12},{10,... | collective-permute-start | bytes 393224 | tf_op jit(solution)/shard_map/ppermute | solution.py:148
  13.6 0.5 %collective-permute-start.6 = (bf16[128,256]{1,0:T(8,128)(2,1)S(1)}, bf16[128,256]{1,0:T(8,128)(2,1)S(1)}, u32[]{:S(2)}, u32[]{:S(2)}) collective-permute-start(bf16[128,256]{1,0:T(8,128)(2,1)S(1)} %shard_map.63), channel_id=1, source_target_pairs={{0,4},{1,5},{2,6},{3,7},{4,0},{5,1},{6,2},{7,3},{8,12},{9,13},{10,... | collective-permute-start | bytes 196616 | tf_op jit(solution)/shard_map/ppermute | solution.py:148
  14.2 0.0 collective-permute-done.7.refs_5_
  14.2 0.7 %collective-permute-start.8 = (bf16[256,256]{1,0:T(8,128)(2,1)S(1)}, bf16[256,256]{1,0:T(8,128)(2,1)S(1)}, u32[]{:S(2)}, u32[]{:S(2)}) collective-permute-start(bf16[256,256]{1,0:T(8,128)(2,1)S(1)} %collective-permute-done.7.refs_5_), channel_id=1, source_target_pairs={{0,0},{1,1},{2,6},{3,7},{4,4},{5,5},{6,2},{7,3},{8,8},{9,9},{10,14... | collective-permute-start | bytes 393224 | tf_op jit(solution)/shard_map/ppermute | solution.py:148
  14.8 4.5 %collective-permute-done.6.refs_2_.refs_4_ = bf16[128,256]{1,0:T(8,128)(2,1)S(1)} collective-permute-done((bf16[128,256]{1,0:T(8,128)(2,1)S(1)}, bf16[128,256]{1,0:T(8,128)(2,1)S(1)}, u32[]{:S(2)}, u32[]{:S(2)}) %collective-permute-start.6) | collective-permute-done | bytes 65568 | tf_op jit(solution)/shard_map/ppermute | solution.py:148
  19.3 0.0 collective-permute-done.3.refs_0_.refs_2_
  19.3 0.0 collective-permute-done.5.refs_1_.refs_3_
  19.4 0.0 collective-permute-done.8.refs_6_
  19.4 0.3 %shard_map.66 = bf16[128,256]{1,0:T(8,128)(2,1)S(1)} custom-call(bf16[256,1408]{1,0:T(8,128)(2,1)S(1)} %get-tuple-element.10.matrix, bf16[16,128]{1,0:T(8,128)(2,1)S(1)} %shard_map.64.mark, bf16[128,256]{1,0:T(8,128)(2,1)S(1)} %get-tuple-element.11.refs_0_, bf16[128,256]{1,0:T(8,128)(2,1)S(1)} %collective-permute-done.2.refs_0_.refs_1_.refs_2_, ...), custom_call_target="tpu_custom_call" | custom-call | flops 84000000 | bytes 1000000 | tf_op jit(solution)/shard_map/pallas_call | solution.py:268
  19.7 0.5 %collective-permute-start.9 = (bf16[128,256]{1,0:T(8,128)(2,1)S(1)}, bf16[128,256]{1,0:T(8,128)(2,1)S(1)}, u32[]{:S(2)}, u32[]{:S(2)}) collective-permute-start(bf16[128,256]{1,0:T(8,128)(2,1)S(1)} %shard_map.66), channel_id=1, source_target_pairs={{0,2},{1,3},{2,0},{3,1},{4,6},{5,7},{6,4},{7,5},{8,10},{9,11},{10,... | collective-permute-start | bytes 196616 | tf_op jit(solution)/shard_map/ppermute | solution.py:148
  20.2 0.3 %shard_map.65.mine = f32[128,256]{1,0:T(8,128)S(1)} custom-call(bf16[256,1408]{1,0:T(8,128)(2,1)S(1)} %collective-permute-done.refs_0_.matrix, bf16[16,128]{1,0:T(8,128)(2,1)S(1)} %shard_map.64.mark, bf16[128,256]{1,0:T(8,128)(2,1)S(1)} %get-tuple-element.11.refs_0_, bf16[128,256]{1,0:T(8,128)(2,1)S(1)} %collective-permute-done.2.refs_0_.refs_1_.refs_2_, ...), custom_call_target="tpu_custom_call" | custom-call | flops 84000000 | bytes 1000000 | tf_op jit(solution)/shard_map/pallas_call | solution.py:268
  20.5 0.6 %collective-permute-done.9.other = bf16[128,256]{1,0:T(8,128)(2,1)S(1)} collective-permute-done((bf16[128,256]{1,0:T(8,128)(2,1)S(1)}, bf16[128,256]{1,0:T(8,128)(2,1)S(1)}, u32[]{:S(2)}, u32[]{:S(2)}) %collective-permute-start.9) | collective-permute-done | bytes 65568 | tf_op jit(solution)/shard_map/ppermute | solution.py:148
  21.1 1.3 %collective-permute-start.10 = (bf16[128,256]{1,0:T(8,128)(2,1)S(1)}, bf16[128,256]{1,0:T(8,128)(2,1)S(1)}, u32[]{:S(2)}, u32[]{:S(2)}) collective-permute-start(bf16[128,256]{1,0:T(8,128)(2,1)S(1)} %shard_map.67), channel_id=1, source_target_pairs={{0,3},{1,2},{2,1},{3,0},{4,7},{5,6},{6,5},{7,4},{8,11},{9,10},{10,... | collective-permute-start | bytes 196616 | tf_op jit(solution)/shard_map/ppermute | solution.py:148
  22.5 0.3 %shard_map.69 = f32[128,256]{1,0:T(8,128)S(1)} custom-call(bf16[256,1408]{1,0:T(8,128)(2,1)S(1)} %collective-permute-done.refs_0_.matrix, bf16[16,128]{1,0:T(8,128)(2,1)S(1)} %shard_map.64.mark, bf16[128,256]{1,0:T(8,128)(2,1)S(1)} %get-tuple-element.11.refs_0_, bf16[128,256]{1,0:T(8,128)(2,1)S(1)} %collective-permute-done.2.refs_0_.refs_1_.refs_2_, ...), custom_call_target="tpu_custom_call" | custom-call | flops 84000000 | bytes 1000000 | tf_op jit(solution)/shard_map/pallas_call | solution.py:268
  22.7 0.2 collective-permute-start.11
  23.0 0.3 %shard_map.68.mine = f32[128,256]{1,0:T(8,128)S(1)} custom-call(bf16[256,1408]{1,0:T(8,128)(2,1)S(1)} %get-tuple-element.10.matrix, bf16[16,128]{1,0:T(8,128)(2,1)S(1)} %shard_map.64.mark, bf16[128,256]{1,0:T(8,128)(2,1)S(1)} %get-tuple-element.11.refs_0_, bf16[128,256]{1,0:T(8,128)(2,1)S(1)} %collective-permute-done.2.refs_0_.refs_1_.refs_2_, ...), custom_call_target="tpu_custom_call" | custom-call | flops 84000000 | bytes 1000000 | tf_op jit(solution)/shard_map/pallas_call | solution.py:268
  23.2 0.0 copy-start.1
  23.3 1.8 %collective-permute-done.10.refs_0_.theirs = bf16[128,256]{1,0:T(8,128)(2,1)S(1)} collective-permute-done((bf16[128,256]{1,0:T(8,128)(2,1)S(1)}, bf16[128,256]{1,0:T(8,128)(2,1)S(1)}, u32[]{:S(2)}, u32[]{:S(2)}) %collective-permute-start.10) | collective-permute-done | bytes 65568 | tf_op jit(solution)/shard_map/ppermute | solution.py:148
  25.1 0.0 collective-permute-done.11.other
  25.1 0.8 %shard_map.71 = bf16[128,256]{1,0:T(8,128)(2,1)} custom-call(bf16[128,256]{1,0:T(8,128)(2,1)S(1)} %collective-permute-done.10.refs_0_.theirs, f32[128,256]{1,0:T(8,128)S(1)} %shard_map.68.mine, f32[128,256]{1,0:T(8,128)S(1)} %collective-permute-done.11.other, bf16[256,256]{1,0:T(8,128)(2,1)S(1)} %copy-done.1, bf16[16,128]{1,0:T(8,128)(2,1)S(1)} %shard_map.70.mark), custom_call_target="tpu_custom_call" | custom-call | flops 17000000 | bytes 400000 | tf_op jit(solution)/shard_map/pallas_call | solution.py:300
  (19 shorter events, 0.1 us)
Async XLA Ops:
  0.0 5.1 %copy-start.4 = (s32[1,8]{1,0:T(1,128)S(1)}, s32[1,8]{1,0:T(1,128)}, u32[]{:S(2)}) copy-start(s32[1,8]{1,0:T(1,128)} %counts.1) | copy-start | bytes 100
  0.0 5.1 %copy-start.3 = (s32[96,2]{0,1:T(2,128)S(1)}, s32[96,2]{0,1:T(2,128)}, u32[]{:S(2)}) copy-start(s32[96,2]{0,1:T(2,128)} %param.8) | copy-start | bytes 2308
  0.0 5.2 %copy-start = (bf16[96,128,128]{2,1,0:T(8,128)(2,1)S(1)}, bf16[96,128,128]{2,1,0:T(8,128)(2,1)}, u32[]{:S(2)}) copy-start(bf16[96,128,128]{2,1,0:T(8,128)(2,1)} %values.1) | copy-start | bytes 9437188
  0.0 7.5 %collective-permute-start.1 = (bf16[128,256]{1,0:T(8,128)(2,1)}, bf16[128,256]{1,0:T(8,128)(2,1)S(1)}, u32[]{:S(2)}, u32[]{:S(2)}) collective-permute-start(bf16[128,256]{1,0:T(8,128)(2,1)} %value.1), channel_id=1, source_target_pairs={{0,24},{1,9},{2,26},{3,11},{4,28},{5,13},{6,30},{7,15},{8,0},{9,17... | collective-permute-start | bytes 196616 | tf_op jit(solution)/shard_map/ppermute | solution.py:148
  5.1 5.4 %collective-permute-start.2 = (bf16[128,256]{1,0:T(8,128)(2,1)}, bf16[128,256]{1,0:T(8,128)(2,1)S(1)}, u32[]{:S(2)}, u32[]{:S(2)}) collective-permute-start(bf16[128,256]{1,0:T(8,128)(2,1)} %value.1), channel_id=1, source_target_pairs={{0,16},{1,17},{2,18},{3,19},{4,20},{5,21},{6,22},{7,23},{8,24},{9,... | collective-permute-start | bytes 196616 | tf_op jit(solution)/shard_map/ppermute | solution.py:148
  5.1 2.4 %collective-permute-start.4 = (bf16[128,256]{1,0:T(8,128)(2,1)}, bf16[128,256]{1,0:T(8,128)(2,1)S(1)}, u32[]{:S(2)}, u32[]{:S(2)}) collective-permute-start(bf16[128,256]{1,0:T(8,128)(2,1)} %value.1), channel_id=1, source_target_pairs={{0,2},{1,3},{2,0},{3,1},{4,6},{5,7},{6,4},{7,5},{8,10},{9,11},{10,... | collective-permute-start | bytes 196616 | tf_op jit(solution)/shard_map/ppermute | solution.py:148
  5.1 2.4 %copy-start.2 = (bf16[128,256]{1,0:T(8,128)(2,1)S(1)}, bf16[128,256]{1,0:T(8,128)(2,1)}, u32[]{:S(2)}) copy-start(bf16[128,256]{1,0:T(8,128)(2,1)} %value.1) | copy-start | bytes 196612
  6.6 3.9 %collective-permute-start = (bf16[256,1408]{1,0:T(8,128)(2,1)S(1)}, bf16[256,1408]{1,0:T(8,128)(2,1)S(1)}, u32[]{:S(2)}, u32[]{:S(2)}) collective-permute-start(bf16[256,1408]{1,0:T(8,128)(2,1)S(1)} %get-tuple-element.9), channel_id=1, source_target_pairs={{0,2},{1,3},{2,0},{3,1},{4,6},{5,7},{6,4},{7,5},{8,10},{9,11},{10,... | collective-permute-start | bytes 2162696 | tf_op jit(solution)/shard_map/ppermute | solution.py:148
  7.5 6.7 %collective-permute-start.7 = (bf16[256,256]{1,0:T(8,128)(2,1)S(1)}, bf16[256,256]{1,0:T(8,128)(2,1)S(1)}, u32[]{:S(2)}, u32[]{:S(2)}) collective-permute-start(bf16[256,256]{1,0:T(8,128)(2,1)S(1)} %get-tuple-element.12), channel_id=1, source_target_pairs={{0,1},{1,0},{2,10},{3,27},{4,5},{5,4},{6,14},{7,31},{8,9},{9,8},{1... | collective-permute-start | bytes 393224 | tf_op jit(solution)/shard_map/ppermute | solution.py:148
  10.5 8.8 %collective-permute-start.3 = (bf16[256,256]{1,0:T(8,128)(2,1)S(1)}, bf16[256,256]{1,0:T(8,128)(2,1)S(1)}, u32[]{:S(2)}, u32[]{:S(2)}) collective-permute-start(bf16[256,256]{1,0:T(8,128)(2,1)S(1)} %shard_map.59), channel_id=1, source_target_pairs={{0,1},{1,0},{2,3},{3,2},{4,5},{5,4},{6,7},{7,6},{8,9},{9,8},{10,11... | collective-permute-start | bytes 393224 | tf_op jit(solution)/shard_map/ppermute | solution.py:148
  11.9 7.5 %collective-permute-start.5 = (bf16[256,256]{1,0:T(8,128)(2,1)S(1)}, bf16[256,256]{1,0:T(8,128)(2,1)S(1)}, u32[]{:S(2)}, u32[]{:S(2)}) collective-permute-start(bf16[256,256]{1,0:T(8,128)(2,1)S(1)} %shard_map.62), channel_id=1, source_target_pairs={{0,5},{1,4},{2,7},{3,6},{4,1},{5,0},{6,3},{7,2},{8,13},{9,12},{10,... | collective-permute-start | bytes 393224 | tf_op jit(solution)/shard_map/ppermute | solution.py:148
  13.6 5.7 %collective-permute-start.6 = (bf16[128,256]{1,0:T(8,128)(2,1)S(1)}, bf16[128,256]{1,0:T(8,128)(2,1)S(1)}, u32[]{:S(2)}, u32[]{:S(2)}) collective-permute-start(bf16[128,256]{1,0:T(8,128)(2,1)S(1)} %shard_map.63), channel_id=1, source_target_pairs={{0,4},{1,5},{2,6},{3,7},{4,0},{5,1},{6,2},{7,3},{8,12},{9,13},{10,... | collective-permute-start | bytes 196616 | tf_op jit(solution)/shard_map/ppermute | solution.py:148
  14.2 5.2 %collective-permute-start.8 = (bf16[256,256]{1,0:T(8,128)(2,1)S(1)}, bf16[256,256]{1,0:T(8,128)(2,1)S(1)}, u32[]{:S(2)}, u32[]{:S(2)}) collective-permute-start(bf16[256,256]{1,0:T(8,128)(2,1)S(1)} %collective-permute-done.7.refs_5_), channel_id=1, source_target_pairs={{0,0},{1,1},{2,6},{3,7},{4,4},{5,5},{6,2},{7,3},{8,8},{9,9},{10,14... | collective-permute-start | bytes 393224 | tf_op jit(solution)/shard_map/ppermute | solution.py:148
  19.7 1.4 %collective-permute-start.9 = (bf16[128,256]{1,0:T(8,128)(2,1)S(1)}, bf16[128,256]{1,0:T(8,128)(2,1)S(1)}, u32[]{:S(2)}, u32[]{:S(2)}) collective-permute-start(bf16[128,256]{1,0:T(8,128)(2,1)S(1)} %shard_map.66), channel_id=1, source_target_pairs={{0,2},{1,3},{2,0},{3,1},{4,6},{5,7},{6,4},{7,5},{8,10},{9,11},{10,... | collective-permute-start | bytes 196616 | tf_op jit(solution)/shard_map/ppermute | solution.py:148
  21.1 4.0 %collective-permute-start.10 = (bf16[128,256]{1,0:T(8,128)(2,1)S(1)}, bf16[128,256]{1,0:T(8,128)(2,1)S(1)}, u32[]{:S(2)}, u32[]{:S(2)}) collective-permute-start(bf16[128,256]{1,0:T(8,128)(2,1)S(1)} %shard_map.67), channel_id=1, source_target_pairs={{0,3},{1,2},{2,1},{3,0},{4,7},{5,6},{6,5},{7,4},{8,11},{9,10},{10,... | collective-permute-start | bytes 196616 | tf_op jit(solution)/shard_map/ppermute | solution.py:148
  22.7 2.4 %collective-permute-start.11 = (f32[128,256]{1,0:T(8,128)S(1)}, f32[128,256]{1,0:T(8,128)S(1)}, u32[]{:S(2)}, u32[]{:S(2)}) collective-permute-start(f32[128,256]{1,0:T(8,128)S(1)} %shard_map.69), channel_id=1, source_target_pairs={{0,2},{1,3},{2,0},{3,1},{4,6},{5,7},{6,4},{7,5},{8,10},{9,11},{10,... | collective-permute-start | bytes 393224 | tf_op jit(solution)/shard_map/ppermute | solution.py:148
  23.2 1.9 %copy-start.1 = (bf16[256,256]{1,0:T(8,128)(2,1)S(1)}, bf16[256,256]{1,0:T(8,128)(2,1)}, u32[]{:S(2)}) copy-start(bf16[256,256]{1,0:T(8,128)(2,1)} %weight.1) | copy-start | bytes 393220

commit v8 on v7

--- a/solution.py
+++ b/solution.py
@@ -187,16 +187,19 @@
     given[...] = jnp.zeros_like(given)
 
     def one(step):
-        total[...] = jnp.zeros_like(total)
-
-        def add(slot, carry):
-            row = coords[0, step * slots + slot] ^ rank
-            column = coords[1, step * slots + slot] ^ rank
-            spot = row * 2 + column
-            total[spot] = total[spot] + values[step * slots + slot].astype(jnp.float32)
+        for spot in range(4):
+            total[spot] = jnp.zeros_like(total[spot])
+
+        def add(group, carry):
+            for i in range(3):
+                slot = group * 3 + i
+                row = coords[0, step * slots + slot] ^ rank
+                column = coords[1, step * slots + slot] ^ rank
+                spot = jnp.where(slot < counts[0, step], row * 2 + column, 4)
+                total[spot] = total[spot] + values[step * slots + slot].astype(jnp.float32)
             return carry
 
-        lax.fori_loop(0, counts[0, step], add, 0)
+        lax.fori_loop(0, (counts[0, step] + 2) // 3, add, 0)
         odd = step & 1
         there = odd * (1 - 2 * core)
         k = jnp.where(rank == 0, step + there, steps - step - there) >> 1
@@ -234,7 +237,7 @@
         out_shape=[jax.ShapeDtypeStruct((2 * tile, HELD * tile), jnp.bfloat16)] * 2,
         in_specs=[VMEM, SMEM, SMEM, VMEM],
         out_specs=[VMEM, VMEM],
-        scratch_shapes=[pltpu.VMEM((4, tile, tile), jnp.float32)],
+        scratch_shapes=[pltpu.VMEM((5, tile, tile), jnp.float32)],
         compiler_params=pltpu.CompilerParams(vmem_limit_bytes=MIDDLE),
         cost_estimate=pl.CostEstimate(flops=1, bytes_accessed=1, transcendentals=0),
     )(mark, tile_counts, tile_coords, tile_values)

time: 26 us -> 25.6 us (0.985)
  waiting for transfers between devices: 8.08 us -> 6.58 us
  starting transfers between devices: 14.3 us -> 14.8 us
  Pallas kernels: 3.42 us -> 3.91 us
    ppermute x12, waiting for transfers between devices: 8.08 us -> 6.58 us  [send(): return lax.ppermute(value, AXES, route(planes, move))]
    ppermute x12, starting transfers between devices: 14.3 us -> 14.8 us  [send(): return lax.ppermute(value, AXES, route(planes, move))]
    pallas_call x1, Pallas kernels: 1.42 us -> 1.9 us  [dense(): pl.pallas_call(dense_kernel, out_shape=[jax.ShapeDtypeStruct((2 * tile, H...]
  transfers between devices with their start and end apart: 12 -> 12, of which waited for: 5 -> 5; matrix products, arithmetic and copies ran while one was open for 0% -> 0% of each run, Pallas kernels for 9% -> 11%
where the time goes in v8:
time: 25.6 us; the launch traced here: 25.4 us
  starting transfers between devices  14.8 us (58%)
  waiting for transfers between devices  6.58 us (26%)
  Pallas kernels  3.91 us (15%)
    ppermute x12, starting transfers between devices, send(): return lax.ppermute(value, AXES, route(planes, move))  14.8 us
    ppermute x12, waiting for transfers between devices, send(): return lax.ppermute(value, AXES, route(planes, move))  6.58 us
    pallas_call x1, Pallas kernels, dense(): pl.pallas_call(dense_kernel, out_shape=[jax.ShapeDtypeStruct((2 * tile, H...  1.9 us
    pallas_call x4, Pallas kernels, products(): pl.pallas_call(functools.partial(product_kernel, half * rows), out_shape=...  1.11 us
    pallas_call x1, Pallas kernels, last(): pl.pallas_call(last_kernel, out_shape=jax.ShapeDtypeStruct(theirs.shape,...  0.81 us
  transfers between devices with their start and end apart: 12, of which 5 were waited for; matrix products, arithmetic and copies ran while one was open for 0% of the time, Pallas kernels for 11%

profile of v8, /device:TPU:0, one launch (start us, length us, event | category | flops | bytes accessed | tf_op | source)
XLA Modules:
  0.0 25.4 jit_solution(3170175619684813504)
XLA Ops:
  0.0 5.1 %collective-permute-start.1 = (bf16[128,256]{1,0:T(8,128)(2,1)}, bf16[128,256]{1,0:T(8,128)(2,1)S(1)}, u32[]{:S(2)}, u32[]{:S(2)}) collective-permute-start(bf16[128,256]{1,0:T(8,128)(2,1)} %value.1), channel_id=1, source_target_pairs={{0,24},{1,9},{2,26},{3,11},{4,28},{5,13},{6,30},{7,15},{8,0},{9,17... | collective-permute-start | bytes 196616 | tf_op jit(solution)/shard_map/ppermute | solution.py:148
  5.1 0.0 collective-permute-start.2
  5.1 0.0 collective-permute-start.4
  5.1 0.0 copy-start.2
  5.2 1.9 %shard_map.56 = (bf16[256,1408]{1,0:T(8,128)(2,1)S(1)}, bf16[256,1408]{1,0:T(8,128)(2,1)S(1)}) custom-call(bf16[16,128]{1,0:T(8,128)(2,1)S(1)} %shard_map.55.mark, s32[1,8]{1,0:T(1,128)S(1)} %copy-done.4, s32[2,96]{1,0:T(2,128)S(1)} %bitcast.1, bf16[96,128,128]{2,1,0:T(8,128)(2,1)S(1)} %copy-done), custom_call_target="tpu_custom_call" | custom-call | flops 1 | bytes 1 | tf_op jit(solution)/shard_map/pallas_call | solution.py:235
  7.1 0.6 %collective-permute-start = (bf16[256,1408]{1,0:T(8,128)(2,1)S(1)}, bf16[256,1408]{1,0:T(8,128)(2,1)S(1)}, u32[]{:S(2)}, u32[]{:S(2)}) collective-permute-start(bf16[256,1408]{1,0:T(8,128)(2,1)S(1)} %get-tuple-element.9), channel_id=1, source_target_pairs={{0,2},{1,3},{2,0},{3,1},{4,6},{5,7},{6,4},{7,5},{8,10},{9,11},{10,... | collective-permute-start | bytes 2162696 | tf_op jit(solution)/shard_map/ppermute | solution.py:148
  7.7 0.0 collective-permute-done.1.refs_0_.refs_1_
  7.7 0.0 collective-permute-done.4.mate
  7.7 2.1 %collective-permute-start.7 = (bf16[256,256]{1,0:T(8,128)(2,1)S(1)}, bf16[256,256]{1,0:T(8,128)(2,1)S(1)}, u32[]{:S(2)}, u32[]{:S(2)}) collective-permute-start(bf16[256,256]{1,0:T(8,128)(2,1)S(1)} %get-tuple-element.12), channel_id=1, source_target_pairs={{0,1},{1,0},{2,10},{3,27},{4,5},{5,4},{6,14},{7,31},{8,9},{9,8},{1... | collective-permute-start | bytes 393224 | tf_op jit(solution)/shard_map/ppermute | solution.py:148
  9.8 0.7 %collective-permute-done.2.refs_0_.refs_1_.refs_2_ = bf16[128,256]{1,0:T(8,128)(2,1)S(1)} collective-permute-done((bf16[128,256]{1,0:T(8,128)(2,1)}, bf16[128,256]{1,0:T(8,128)(2,1)S(1)}, u32[]{:S(2)}, u32[]{:S(2)}) %collective-permute-start.2) | collective-permute-done | bytes 65568 | tf_op jit(solution)/shard_map/ppermute | solution.py:148
  10.5 0.0 collective-permute-done.refs_0_.matrix
  10.5 1.3 %collective-permute-start.3 = (bf16[256,256]{1,0:T(8,128)(2,1)S(1)}, bf16[256,256]{1,0:T(8,128)(2,1)S(1)}, u32[]{:S(2)}, u32[]{:S(2)}) collective-permute-start(bf16[256,256]{1,0:T(8,128)(2,1)S(1)} %shard_map.59), channel_id=1, source_target_pairs={{0,1},{1,0},{2,3},{3,2},{4,5},{5,4},{6,7},{7,6},{8,9},{9,8},{10,11... | collective-permute-start | bytes 393224 | tf_op jit(solution)/shard_map/ppermute | solution.py:148
  11.9 1.8 %collective-permute-start.5 = (bf16[256,256]{1,0:T(8,128)(2,1)S(1)}, bf16[256,256]{1,0:T(8,128)(2,1)S(1)}, u32[]{:S(2)}, u32[]{:S(2)}) collective-permute-start(bf16[256,256]{1,0:T(8,128)(2,1)S(1)} %shard_map.62), channel_id=1, source_target_pairs={{0,5},{1,4},{2,7},{3,6},{4,1},{5,0},{6,3},{7,2},{8,13},{9,12},{10,... | collective-permute-start | bytes 393224 | tf_op jit(solution)/shard_map/ppermute | solution.py:148
  13.6 0.5 %collective-permute-start.6 = (bf16[128,256]{1,0:T(8,128)(2,1)S(1)}, bf16[128,256]{1,0:T(8,128)(2,1)S(1)}, u32[]{:S(2)}, u32[]{:S(2)}) collective-permute-start(bf16[128,256]{1,0:T(8,128)(2,1)S(1)} %shard_map.63), channel_id=1, source_target_pairs={{0,4},{1,5},{2,6},{3,7},{4,0},{5,1},{6,2},{7,3},{8,12},{9,13},{10,... | collective-permute-start | bytes 196616 | tf_op jit(solution)/shard_map/ppermute | solution.py:148
  14.2 0.0 collective-permute-done.7.refs_5_
  14.2 0.7 %collective-permute-start.8 = (bf16[256,256]{1,0:T(8,128)(2,1)S(1)}, bf16[256,256]{1,0:T(8,128)(2,1)S(1)}, u32[]{:S(2)}, u32[]{:S(2)}) collective-permute-start(bf16[256,256]{1,0:T(8,128)(2,1)S(1)} %collective-permute-done.7.refs_5_), channel_id=1, source_target_pairs={{0,0},{1,1},{2,6},{3,7},{4,4},{5,5},{6,2},{7,3},{8,8},{9,9},{10,14... | collective-permute-start | bytes 393224 | tf_op jit(solution)/shard_map/ppermute | solution.py:148
  14.8 3.4 %collective-permute-done.6.refs_2_.refs_4_ = bf16[128,256]{1,0:T(8,128)(2,1)S(1)} collective-permute-done((bf16[128,256]{1,0:T(8,128)(2,1)S(1)}, bf16[128,256]{1,0:T(8,128)(2,1)S(1)}, u32[]{:S(2)}, u32[]{:S(2)}) %collective-permute-start.6) | collective-permute-done | bytes 65568 | tf_op jit(solution)/shard_map/ppermute | solution.py:148
  18.2 0.0 collective-permute-done.3.refs_0_.refs_2_
  18.2 0.3 %collective-permute-done.5.refs_1_.refs_3_ = bf16[256,256]{1,0:T(8,128)(2,1)S(1)} collective-permute-done((bf16[256,256]{1,0:T(8,128)(2,1)S(1)}, bf16[256,256]{1,0:T(8,128)(2,1)S(1)}, u32[]{:S(2)}, u32[]{:S(2)}) %collective-permute-start.5) | collective-permute-done | bytes 131104 | tf_op jit(solution)/shard_map/ppermute | solution.py:148
  18.5 0.0 collective-permute-done.8.refs_6_
  18.5 0.3 %shard_map.66 = bf16[128,256]{1,0:T(8,128)(2,1)S(1)} custom-call(bf16[256,1408]{1,0:T(8,128)(2,1)S(1)} %get-tuple-element.10.matrix, bf16[16,128]{1,0:T(8,128)(2,1)S(1)} %shard_map.64.mark, bf16[128,256]{1,0:T(8,128)(2,1)S(1)} %get-tuple-element.11.refs_0_, bf16[128,256]{1,0:T(8,128)(2,1)S(1)} %collective-permute-done.2.refs_0_.refs_1_.refs_2_, ...), custom_call_target="tpu_custom_call" | custom-call | flops 84000000 | bytes 1000000 | tf_op jit(solution)/shard_map/pallas_call | solution.py:271
  18.8 0.9 %collective-permute-start.9 = (bf16[128,256]{1,0:T(8,128)(2,1)S(1)}, bf16[128,256]{1,0:T(8,128)(2,1)S(1)}, u32[]{:S(2)}, u32[]{:S(2)}) collective-permute-start(bf16[128,256]{1,0:T(8,128)(2,1)S(1)} %shard_map.66), channel_id=1, source_target_pairs={{0,2},{1,3},{2,0},{3,1},{4,6},{5,7},{6,4},{7,5},{8,10},{9,11},{10,... | collective-permute-start | bytes 196616 | tf_op jit(solution)/shard_map/ppermute | solution.py:148
  19.7 0.3 %shard_map.65.mine = f32[128,256]{1,0:T(8,128)S(1)} custom-call(bf16[256,1408]{1,0:T(8,128)(2,1)S(1)} %collective-permute-done.refs_0_.matrix, bf16[16,128]{1,0:T(8,128)(2,1)S(1)} %shard_map.64.mark, bf16[128,256]{1,0:T(8,128)(2,1)S(1)} %get-tuple-element.11.refs_0_, bf16[128,256]{1,0:T(8,128)(2,1)S(1)} %collective-permute-done.2.refs_0_.refs_1_.refs_2_, ...), custom_call_target="tpu_custom_call" | custom-call | flops 84000000 | bytes 1000000 | tf_op jit(solution)/shard_map/pallas_call | solution.py:271
  20.0 0.6 %collective-permute-done.9.other = bf16[128,256]{1,0:T(8,128)(2,1)S(1)} collective-permute-done((bf16[128,256]{1,0:T(8,128)(2,1)S(1)}, bf16[128,256]{1,0:T(8,128)(2,1)S(1)}, u32[]{:S(2)}, u32[]{:S(2)}) %collective-permute-start.9) | collective-permute-done | bytes 65568 | tf_op jit(solution)/shard_map/ppermute | solution.py:148
  20.6 1.6 %collective-permute-start.10 = (bf16[128,256]{1,0:T(8,128)(2,1)S(1)}, bf16[128,256]{1,0:T(8,128)(2,1)S(1)}, u32[]{:S(2)}, u32[]{:S(2)}) collective-permute-start(bf16[128,256]{1,0:T(8,128)(2,1)S(1)} %shard_map.67), channel_id=1, source_target_pairs={{0,3},{1,2},{2,1},{3,0},{4,7},{5,6},{6,5},{7,4},{8,11},{9,10},{10,... | collective-permute-start | bytes 196616 | tf_op jit(solution)/shard_map/ppermute | solution.py:148
  22.2 0.3 %shard_map.69 = f32[128,256]{1,0:T(8,128)S(1)} custom-call(bf16[256,1408]{1,0:T(8,128)(2,1)S(1)} %collective-permute-done.refs_0_.matrix, bf16[16,128]{1,0:T(8,128)(2,1)S(1)} %shard_map.64.mark, bf16[128,256]{1,0:T(8,128)(2,1)S(1)} %get-tuple-element.11.refs_0_, bf16[128,256]{1,0:T(8,128)(2,1)S(1)} %collective-permute-done.2.refs_0_.refs_1_.refs_2_, ...), custom_call_target="tpu_custom_call" | custom-call | flops 84000000 | bytes 1000000 | tf_op jit(solution)/shard_map/pallas_call | solution.py:271
  22.5 0.2 collective-permute-start.11
  22.7 0.3 %shard_map.68.mine = f32[128,256]{1,0:T(8,128)S(1)} custom-call(bf16[256,1408]{1,0:T(8,128)(2,1)S(1)} %get-tuple-element.10.matrix, bf16[16,128]{1,0:T(8,128)(2,1)S(1)} %shard_map.64.mark, bf16[128,256]{1,0:T(8,128)(2,1)S(1)} %get-tuple-element.11.refs_0_, bf16[128,256]{1,0:T(8,128)(2,1)S(1)} %collective-permute-done.2.refs_0_.refs_1_.refs_2_, ...), custom_call_target="tpu_custom_call" | custom-call | flops 84000000 | bytes 1000000 | tf_op jit(solution)/shard_map/pallas_call | solution.py:271
  23.0 0.0 copy-start.1
  23.0 1.6 %collective-permute-done.10.refs_0_.theirs = bf16[128,256]{1,0:T(8,128)(2,1)S(1)} collective-permute-done((bf16[128,256]{1,0:T(8,128)(2,1)S(1)}, bf16[128,256]{1,0:T(8,128)(2,1)S(1)}, u32[]{:S(2)}, u32[]{:S(2)}) %collective-permute-start.10) | collective-permute-done | bytes 65568 | tf_op jit(solution)/shard_map/ppermute | solution.py:148
  24.6 0.0 collective-permute-done.11.other
  24.6 0.8 %shard_map.71 = bf16[128,256]{1,0:T(8,128)(2,1)} custom-call(bf16[128,256]{1,0:T(8,128)(2,1)S(1)} %collective-permute-done.10.refs_0_.theirs, f32[128,256]{1,0:T(8,128)S(1)} %shard_map.68.mine, f32[128,256]{1,0:T(8,128)S(1)} %collective-permute-done.11.other, bf16[256,256]{1,0:T(8,128)(2,1)S(1)} %copy-done.1, bf16[16,128]{1,0:T(8,128)(2,1)S(1)} %shard_map.70.mark), custom_call_target="tpu_custom_call" | custom-call | flops 17000000 | bytes 400000 | tf_op jit(solution)/shard_map/pallas_call | solution.py:303
  (19 shorter events, 0.1 us)
Async XLA Ops:
  0.0 5.1 %copy-start.4 = (s32[1,8]{1,0:T(1,128)S(1)}, s32[1,8]{1,0:T(1,128)}, u32[]{:S(2)}) copy-start(s32[1,8]{1,0:T(1,128)} %counts.1) | copy-start | bytes 100
  0.0 5.1 %copy-start.3 = (s32[96,2]{0,1:T(2,128)S(1)}, s32[96,2]{0,1:T(2,128)}, u32[]{:S(2)}) copy-start(s32[96,2]{0,1:T(2,128)} %param.8) | copy-start | bytes 2308
  0.0 5.2 %copy-start = (bf16[96,128,128]{2,1,0:T(8,128)(2,1)S(1)}, bf16[96,128,128]{2,1,0:T(8,128)(2,1)}, u32[]{:S(2)}) copy-start(bf16[96,128,128]{2,1,0:T(8,128)(2,1)} %values.1) | copy-start | bytes 9437188
  0.0 7.6 %collective-permute-start.1 = (bf16[128,256]{1,0:T(8,128)(2,1)}, bf16[128,256]{1,0:T(8,128)(2,1)S(1)}, u32[]{:S(2)}, u32[]{:S(2)}) collective-permute-start(bf16[128,256]{1,0:T(8,128)(2,1)} %value.1), channel_id=1, source_target_pairs={{0,24},{1,9},{2,26},{3,11},{4,28},{5,13},{6,30},{7,15},{8,0},{9,17... | collective-permute-start | bytes 196616 | tf_op jit(solution)/shard_map/ppermute | solution.py:148
  5.1 5.4 %collective-permute-start.2 = (bf16[128,256]{1,0:T(8,128)(2,1)}, bf16[128,256]{1,0:T(8,128)(2,1)S(1)}, u32[]{:S(2)}, u32[]{:S(2)}) collective-permute-start(bf16[128,256]{1,0:T(8,128)(2,1)} %value.1), channel_id=1, source_target_pairs={{0,16},{1,17},{2,18},{3,19},{4,20},{5,21},{6,22},{7,23},{8,24},{9,... | collective-permute-start | bytes 196616 | tf_op jit(solution)/shard_map/ppermute | solution.py:148
  5.1 2.5 %collective-permute-start.4 = (bf16[128,256]{1,0:T(8,128)(2,1)}, bf16[128,256]{1,0:T(8,128)(2,1)S(1)}, u32[]{:S(2)}, u32[]{:S(2)}) collective-permute-start(bf16[128,256]{1,0:T(8,128)(2,1)} %value.1), channel_id=1, source_target_pairs={{0,2},{1,3},{2,0},{3,1},{4,6},{5,7},{6,4},{7,5},{8,10},{9,11},{10,... | collective-permute-start | bytes 196616 | tf_op jit(solution)/shard_map/ppermute | solution.py:148
  5.1 2.5 %copy-start.2 = (bf16[128,256]{1,0:T(8,128)(2,1)S(1)}, bf16[128,256]{1,0:T(8,128)(2,1)}, u32[]{:S(2)}) copy-start(bf16[128,256]{1,0:T(8,128)(2,1)} %value.1) | copy-start | bytes 196612
  7.1 3.4 %collective-permute-start = (bf16[256,1408]{1,0:T(8,128)(2,1)S(1)}, bf16[256,1408]{1,0:T(8,128)(2,1)S(1)}, u32[]{:S(2)}, u32[]{:S(2)}) collective-permute-start(bf16[256,1408]{1,0:T(8,128)(2,1)S(1)} %get-tuple-element.9), channel_id=1, source_target_pairs={{0,2},{1,3},{2,0},{3,1},{4,6},{5,7},{6,4},{7,5},{8,10},{9,11},{10,... | collective-permute-start | bytes 2162696 | tf_op jit(solution)/shard_map/ppermute | solution.py:148
  7.7 6.5 %collective-permute-start.7 = (bf16[256,256]{1,0:T(8,128)(2,1)S(1)}, bf16[256,256]{1,0:T(8,128)(2,1)S(1)}, u32[]{:S(2)}, u32[]{:S(2)}) collective-permute-start(bf16[256,256]{1,0:T(8,128)(2,1)S(1)} %get-tuple-element.12), channel_id=1, source_target_pairs={{0,1},{1,0},{2,10},{3,27},{4,5},{5,4},{6,14},{7,31},{8,9},{9,8},{1... | collective-permute-start | bytes 393224 | tf_op jit(solution)/shard_map/ppermute | solution.py:148
  10.5 7.7 %collective-permute-start.3 = (bf16[256,256]{1,0:T(8,128)(2,1)S(1)}, bf16[256,256]{1,0:T(8,128)(2,1)S(1)}, u32[]{:S(2)}, u32[]{:S(2)}) collective-permute-start(bf16[256,256]{1,0:T(8,128)(2,1)S(1)} %shard_map.59), channel_id=1, source_target_pairs={{0,1},{1,0},{2,3},{3,2},{4,5},{5,4},{6,7},{7,6},{8,9},{9,8},{10,11... | collective-permute-start | bytes 393224 | tf_op jit(solution)/shard_map/ppermute | solution.py:148
  11.9 6.7 %collective-permute-start.5 = (bf16[256,256]{1,0:T(8,128)(2,1)S(1)}, bf16[256,256]{1,0:T(8,128)(2,1)S(1)}, u32[]{:S(2)}, u32[]{:S(2)}) collective-permute-start(bf16[256,256]{1,0:T(8,128)(2,1)S(1)} %shard_map.62), channel_id=1, source_target_pairs={{0,5},{1,4},{2,7},{3,6},{4,1},{5,0},{6,3},{7,2},{8,13},{9,12},{10,... | collective-permute-start | bytes 393224 | tf_op jit(solution)/shard_map/ppermute | solution.py:148
  13.6 4.6 %collective-permute-start.6 = (bf16[128,256]{1,0:T(8,128)(2,1)S(1)}, bf16[128,256]{1,0:T(8,128)(2,1)S(1)}, u32[]{:S(2)}, u32[]{:S(2)}) collective-permute-start(bf16[128,256]{1,0:T(8,128)(2,1)S(1)} %shard_map.63), channel_id=1, source_target_pairs={{0,4},{1,5},{2,6},{3,7},{4,0},{5,1},{6,2},{7,3},{8,12},{9,13},{10,... | collective-permute-start | bytes 196616 | tf_op jit(solution)/shard_map/ppermute | solution.py:148
  14.2 4.3 %collective-permute-start.8 = (bf16[256,256]{1,0:T(8,128)(2,1)S(1)}, bf16[256,256]{1,0:T(8,128)(2,1)S(1)}, u32[]{:S(2)}, u32[]{:S(2)}) collective-permute-start(bf16[256,256]{1,0:T(8,128)(2,1)S(1)} %collective-permute-done.7.refs_5_), channel_id=1, source_target_pairs={{0,0},{1,1},{2,6},{3,7},{4,4},{5,5},{6,2},{7,3},{8,8},{9,9},{10,14... | collective-permute-start | bytes 393224 | tf_op jit(solution)/shard_map/ppermute | solution.py:148
  18.8 1.8 %collective-permute-start.9 = (bf16[128,256]{1,0:T(8,128)(2,1)S(1)}, bf16[128,256]{1,0:T(8,128)(2,1)S(1)}, u32[]{:S(2)}, u32[]{:S(2)}) collective-permute-start(bf16[128,256]{1,0:T(8,128)(2,1)S(1)} %shard_map.66), channel_id=1, source_target_pairs={{0,2},{1,3},{2,0},{3,1},{4,6},{5,7},{6,4},{7,5},{8,10},{9,11},{10,... | collective-permute-start | bytes 196616 | tf_op jit(solution)/shard_map/ppermute | solution.py:148
  20.6 4.0 %collective-permute-start.10 = (bf16[128,256]{1,0:T(8,128)(2,1)S(1)}, bf16[128,256]{1,0:T(8,128)(2,1)S(1)}, u32[]{:S(2)}, u32[]{:S(2)}) collective-permute-start(bf16[128,256]{1,0:T(8,128)(2,1)S(1)} %shard_map.67), channel_id=1, source_target_pairs={{0,3},{1,2},{2,1},{3,0},{4,7},{5,6},{6,5},{7,4},{8,11},{9,10},{10,... | collective-permute-start | bytes 196616 | tf_op jit(solution)/shard_map/ppermute | solution.py:148
  22.5 2.1 %collective-permute-start.11 = (f32[128,256]{1,0:T(8,128)S(1)}, f32[128,256]{1,0:T(8,128)S(1)}, u32[]{:S(2)}, u32[]{:S(2)}) collective-permute-start(f32[128,256]{1,0:T(8,128)S(1)} %shard_map.69), channel_id=1, source_target_pairs={{0,2},{1,3},{2,0},{3,1},{4,6},{5,7},{6,4},{7,5},{8,10},{9,11},{10,... | collective-permute-start | bytes 393224 | tf_op jit(solution)/shard_map/ppermute | solution.py:148
  23.0 1.6 %copy-start.1 = (bf16[256,256]{1,0:T(8,128)(2,1)S(1)}, bf16[256,256]{1,0:T(8,128)(2,1)}, u32[]{:S(2)}) copy-start(bf16[256,256]{1,0:T(8,128)(2,1)} %weight.1) | copy-start | bytes 393220

commit v9 on v8

--- a/solution.py
+++ b/solution.py
@@ -166,13 +166,15 @@
     across = send(pick((0, 1), (1, 2), own, behind, far, done, ready), lambda z, x, c, y: (z, 1 - x, c, 1 - y))
     along_x = send(pick((1,), (0,), own, far, done, ready), lambda z, x, c, y: (z, 1 - x, c, y))
     beside = send(ahead, lambda z, x, c, y: (z, 1 - x, c, y) if c else (z, x, c, y))
-    arrived = mark(4_000_000_000, along_y, across, along_x)
+    kept_sums, taken_sums = early_products(far, own, ahead, kept, taken)
+    arrived = mark(4_000_000_000, along_y, across, along_x, kept_sums)
+    late = [along_y, across, along_x, beside]
     held = [own, far, along_y, across, along_x, ahead, beside]
-    crossing = send(products(1, kept, held, arrived, jnp.bfloat16), core)
-    theirs = partner_sum(products(1, taken, held, arrived, jnp.float32), crossing)
+    crossing = send(late_products(kept, kept_sums, late, arrived, jnp.bfloat16), core)
+    theirs = partner_sum(late_products(taken, taken_sums, late, arrived, jnp.float32), crossing)
     theirs = send(theirs, lambda z, x, c, y: (z, x, 1 - c, 1 - y))
-    other = send(products(0, taken, held, arrived, jnp.float32), core)
-    mine = products(0, kept, held, arrived, jnp.float32)
+    other = send(products(taken, held, arrived), core)
+    mine = products(kept, held, arrived)
     return mine, other, theirs, mark(2_000_000_000, theirs)
 
 
@@ -183,8 +185,10 @@
     core = lax.axis_index("loop") & 1
     rank = lax.axis_index("rep")
     near = (lax.axis_index("loop") >> 1 & 1) == rank
-    kept[...] = jnp.zeros_like(kept)
-    given[...] = jnp.zeros_like(given)
+    for out in (kept, given):
+        for first, count in ((0, 2), (3, 1), (7, 4)):
+            span = pl.ds(first * tile, count * tile)
+            out[:, span] = jnp.zeros((2 * tile, count * tile), out.dtype)
 
     def one(step):
         for spot in range(4):
@@ -253,24 +257,60 @@
     return total
 
 
-def product_kernel(first, matrix, mark, *refs):
+def dots(matrix, rows, starts, blocks, total):
+    for start, block in zip(starts, blocks, strict=True):
+        part = matrix[rows, pl.ds(start * rows.size, block.shape[0])]
+        total += jnp.dot(part, block[...], preferred_element_type=jnp.float32)
+    return total
+
+
+def early_kernel(far, own, ahead, kept, taken, *outs):
+    for matrix, out in zip((kept, taken), outs, strict=True):
+        rows = pl.ds(out.shape[0], out.shape[0])
+        out[...] = dots(matrix, rows, (0, 1, 7), (own, far, ahead), jnp.zeros(out.shape, jnp.float32))
+
+
+def early_products(far, own, ahead, kept, taken):
+    return pl.pallas_call(
+        early_kernel,
+        out_shape=[jax.ShapeDtypeStruct((kept.shape[0] // 2, own.shape[1]), jnp.float32)] * 2,
+        in_specs=[VMEM] * 5,
+        out_specs=[VMEM] * 2,
+        compiler_params=pltpu.CompilerParams(vmem_limit_bytes=MIDDLE),
+        cost_estimate=pl.CostEstimate(flops=1, bytes_accessed=1, transcendentals=0),
+    )(far, own, ahead, kept, taken)
+
+
+def late_kernel(matrix, mark, sums, *refs):
     out = refs[-1]
-    rows = pl.ds(first, out.shape[0])
-    total = jnp.zeros(out.shape, jnp.float32)
-    start = 0
-    for block in refs[:-1]:
-        depth = block.shape[0]
-        total += jnp.dot(matrix[rows, pl.ds(start, depth)], block[...], preferred_element_type=jnp.float32)
-        start += depth
-    out[...] = total.astype(out.dtype)
-
-
-def products(half, matrix, blocks, mark, dtype):
+    rows = pl.ds(out.shape[0], out.shape[0])
+    out[...] = dots(matrix, rows, (2, 4, 6, 9), refs[:-1], sums[...]).astype(out.dtype)
+
+
+def late_products(matrix, sums, blocks, mark, dtype):
+    return pl.pallas_call(
+        late_kernel,
+        out_shape=jax.ShapeDtypeStruct(sums.shape, dtype),
+        in_specs=[VMEM] * (3 + len(blocks)),
+        out_specs=VMEM,
+        compiler_params=pltpu.CompilerParams(vmem_limit_bytes=MIDDLE),
+        cost_estimate=pl.CostEstimate(flops=54_000_000, bytes_accessed=700_000, transcendentals=0),
+    )(matrix, mark, sums, *blocks)
+
+
+def product_kernel(matrix, mark, *refs):
+    out = refs[-1]
+    rows = pl.ds(0, out.shape[0])
+    starts = (0, 1, 2, 4, 6, 7, 9)
+    out[...] = dots(matrix, rows, starts, refs[:-1], jnp.zeros(out.shape, jnp.float32))
+
+
+def products(matrix, blocks, mark):
     rows = matrix.shape[0] // 2
     width = blocks[0].shape[1]
     return pl.pallas_call(
-        functools.partial(product_kernel, half * rows),
-        out_shape=jax.ShapeDtypeStruct((rows, width), dtype),
+        product_kernel,
+        out_shape=jax.ShapeDtypeStruct((rows, width), jnp.float32),
         in_specs=[VMEM] * (2 + len(blocks)),
         out_specs=VMEM,
         compiler_params=pltpu.CompilerParams(vmem_limit_bytes=MIDDLE),

time: 25.6 us -> 25.6 us (level)
  starting transfers between devices: 14.8 us -> 14.4 us
    ppermute x12, starting transfers between devices: 14.8 us -> 14.4 us  [send(): return lax.ppermute(value, AXES, route(planes, move))]
    pallas_call x4 -> x5, Pallas kernels: 1.11 us -> 1.27 us  [the longest x2 0.56 us: products(): pl.pallas_call(product_kernel, out_shape=jax.ShapeDtypeStruct((rows, widt...]
  transfers between devices with their start and end apart: 12 -> 12, of which waited for: 5 -> 6; matrix products, arithmetic and copies ran while one was open for 0% -> 0% of each run, Pallas kernels for 11% -> 12%
where the time goes in v9:
time: 25.6 us; the launch traced here: 25.3 us
  starting transfers between devices  14.4 us (56%)
  waiting for transfers between devices  6.61 us (26%)
  Pallas kernels  4.1 us (16%)
    ppermute x12, starting transfers between devices, send(): return lax.ppermute(value, AXES, route(planes, move))  14.4 us
    ppermute x12, waiting for transfers between devices, send(): return lax.ppermute(value, AXES, route(planes, move))  6.61 us
    pallas_call x1, Pallas kernels, dense(): pl.pallas_call(dense_kernel, out_shape=[jax.ShapeDtypeStruct((2 * tile, H...  1.95 us
    pallas_call x1, Pallas kernels, last(): pl.pallas_call(last_kernel, out_shape=jax.ShapeDtypeStruct(theirs.shape,...  0.8 us
    pallas_call x2, Pallas kernels, products(): pl.pallas_call(product_kernel, out_shape=jax.ShapeDtypeStruct((rows, widt...  0.56 us
  transfers between devices with their start and end apart: 12, of which 6 were waited for; matrix products, arithmetic and copies ran while one was open for 0% of the time, Pallas kernels for 12%

profile of v9, /device:TPU:0, one launch (start us, length us, event | category | flops | bytes accessed | tf_op | source)
XLA Modules:
  0.0 25.3 jit_solution(17894129186580755543)
XLA Ops:
  0.0 5.1 %collective-permute-start.1 = (bf16[128,256]{1,0:T(8,128)(2,1)}, bf16[128,256]{1,0:T(8,128)(2,1)S(1)}, u32[]{:S(2)}, u32[]{:S(2)}) collective-permute-start(bf16[128,256]{1,0:T(8,128)(2,1)} %value.1), channel_id=1, source_target_pairs={{0,24},{1,9},{2,26},{3,11},{4,28},{5,13},{6,30},{7,15},{8,0},{9,17... | collective-permute-start | bytes 196616 | tf_op jit(solution)/shard_map/ppermute | solution.py:148
  5.1 0.0 collective-permute-start.2
  5.1 0.0 collective-permute-start.4
  5.1 0.0 copy-start.2
  5.2 2.0 %shard_map.56 = (bf16[256,1408]{1,0:T(8,128)(2,1)S(1)}, bf16[256,1408]{1,0:T(8,128)(2,1)S(1)}) custom-call(bf16[16,128]{1,0:T(8,128)(2,1)S(1)} %shard_map.55.mark, s32[1,8]{1,0:T(1,128)S(1)} %copy-done.4, s32[2,96]{1,0:T(2,128)S(1)} %bitcast.1, bf16[96,128,128]{2,1,0:T(8,128)(2,1)S(1)} %copy-done), custom_call_target="tpu_custom_call" | custom-call | flops 1 | bytes 1 | tf_op jit(solution)/shard_map/pallas_call | solution.py:239
  7.1 0.1 collective-permute-start
  7.2 0.3 %collective-permute-done.1.refs_0_.refs_1_ = bf16[128,256]{1,0:T(8,128)(2,1)S(1)} collective-permute-done((bf16[128,256]{1,0:T(8,128)(2,1)}, bf16[128,256]{1,0:T(8,128)(2,1)S(1)}, u32[]{:S(2)}, u32[]{:S(2)}) %collective-permute-start.1) | collective-permute-done | bytes 65568 | tf_op jit(solution)/shard_map/ppermute | solution.py:148
  7.5 0.0 collective-permute-done.4.mate
  7.5 2.3 %collective-permute-start.7 = (bf16[256,256]{1,0:T(8,128)(2,1)S(1)}, bf16[256,256]{1,0:T(8,128)(2,1)S(1)}, u32[]{:S(2)}, u32[]{:S(2)}) collective-permute-start(bf16[256,256]{1,0:T(8,128)(2,1)S(1)} %get-tuple-element.14), channel_id=1, source_target_pairs={{0,1},{1,0},{2,10},{3,27},{4,5},{5,4},{6,14},{7,31},{8,9},{9,8},{1... | collective-permute-start | bytes 393224 | tf_op jit(solution)/shard_map/ppermute | solution.py:148
  9.8 0.7 %collective-permute-done.2.refs_0_.refs_1_.refs_2_.far = bf16[128,256]{1,0:T(8,128)(2,1)S(1)} collective-permute-done((bf16[128,256]{1,0:T(8,128)(2,1)}, bf16[128,256]{1,0:T(8,128)(2,1)S(1)}, u32[]{:S(2)}, u32[]{:S(2)}) %collective-permute-start.2) | collective-permute-done | bytes 65568 | tf_op jit(solution)/shard_map/ppermute | solution.py:148
  10.5 0.0 collective-permute-done.refs_0_.taken.matrix
  10.5 1.4 %collective-permute-start.3 = (bf16[256,256]{1,0:T(8,128)(2,1)S(1)}, bf16[256,256]{1,0:T(8,128)(2,1)S(1)}, u32[]{:S(2)}, u32[]{:S(2)}) collective-permute-start(bf16[256,256]{1,0:T(8,128)(2,1)S(1)} %shard_map.59), channel_id=1, source_target_pairs={{0,1},{1,0},{2,3},{3,2},{4,5},{5,4},{6,7},{7,6},{8,9},{9,8},{10,11... | collective-permute-start | bytes 393224 | tf_op jit(solution)/shard_map/ppermute | solution.py:148
  11.9 1.7 %collective-permute-start.5 = (bf16[256,256]{1,0:T(8,128)(2,1)S(1)}, bf16[256,256]{1,0:T(8,128)(2,1)S(1)}, u32[]{:S(2)}, u32[]{:S(2)}) collective-permute-start(bf16[256,256]{1,0:T(8,128)(2,1)S(1)} %shard_map.62), channel_id=1, source_target_pairs={{0,5},{1,4},{2,7},{3,6},{4,1},{5,0},{6,3},{7,2},{8,13},{9,12},{10,... | collective-permute-start | bytes 393224 | tf_op jit(solution)/shard_map/ppermute | solution.py:148
  13.6 0.5 %collective-permute-start.6 = (bf16[128,256]{1,0:T(8,128)(2,1)S(1)}, bf16[128,256]{1,0:T(8,128)(2,1)S(1)}, u32[]{:S(2)}, u32[]{:S(2)}) collective-permute-start(bf16[128,256]{1,0:T(8,128)(2,1)S(1)} %shard_map.63), channel_id=1, source_target_pairs={{0,4},{1,5},{2,6},{3,7},{4,0},{5,1},{6,2},{7,3},{8,12},{9,13},{10,... | collective-permute-start | bytes 196616 | tf_op jit(solution)/shard_map/ppermute | solution.py:148
  14.2 0.0 collective-permute-done.7.ahead.refs_5_
  14.2 0.7 %collective-permute-start.8 = (bf16[256,256]{1,0:T(8,128)(2,1)S(1)}, bf16[256,256]{1,0:T(8,128)(2,1)S(1)}, u32[]{:S(2)}, u32[]{:S(2)}) collective-permute-start(bf16[256,256]{1,0:T(8,128)(2,1)S(1)} %collective-permute-done.7.ahead.refs_5_), channel_id=1, source_target_pairs={{0,0},{1,1},{2,6},{3,7},{4,4},{5,5},{6,2},{7,3},{8,8},{9,9},{10,14... | collective-permute-start | bytes 393224 | tf_op jit(solution)/shard_map/ppermute | solution.py:148
  14.8 0.2 shard_map.64
  15.1 3.1 %collective-permute-done.6.refs_2_.refs_4_ = bf16[128,256]{1,0:T(8,128)(2,1)S(1)} collective-permute-done((bf16[128,256]{1,0:T(8,128)(2,1)S(1)}, bf16[128,256]{1,0:T(8,128)(2,1)S(1)}, u32[]{:S(2)}, u32[]{:S(2)}) %collective-permute-start.6) | collective-permute-done | bytes 65568 | tf_op jit(solution)/shard_map/ppermute | solution.py:148
  18.2 0.4 %collective-permute-done.5.refs_1_.refs_3_ = bf16[256,256]{1,0:T(8,128)(2,1)S(1)} collective-permute-done((bf16[256,256]{1,0:T(8,128)(2,1)S(1)}, bf16[256,256]{1,0:T(8,128)(2,1)S(1)}, u32[]{:S(2)}, u32[]{:S(2)}) %collective-permute-start.5) | collective-permute-done | bytes 131104 | tf_op jit(solution)/shard_map/ppermute | solution.py:148
  18.6 0.0 collective-permute-done.8.refs_3_.refs_6_
  18.6 0.2 shard_map.67
  18.8 0.8 %collective-permute-start.9 = (bf16[128,256]{1,0:T(8,128)(2,1)S(1)}, bf16[128,256]{1,0:T(8,128)(2,1)S(1)}, u32[]{:S(2)}, u32[]{:S(2)}) collective-permute-start(bf16[128,256]{1,0:T(8,128)(2,1)S(1)} %shard_map.67), channel_id=1, source_target_pairs={{0,2},{1,3},{2,0},{3,1},{4,6},{5,7},{6,4},{7,5},{8,10},{9,11},{10,... | collective-permute-start | bytes 196616 | tf_op jit(solution)/shard_map/ppermute | solution.py:148
  19.6 0.2 shard_map.66.mine
  19.8 0.7 %collective-permute-done.9.other = bf16[128,256]{1,0:T(8,128)(2,1)S(1)} collective-permute-done((bf16[128,256]{1,0:T(8,128)(2,1)S(1)}, bf16[128,256]{1,0:T(8,128)(2,1)S(1)}, u32[]{:S(2)}, u32[]{:S(2)}) %collective-permute-start.9) | collective-permute-done | bytes 65568 | tf_op jit(solution)/shard_map/ppermute | solution.py:148
  20.5 1.7 %collective-permute-start.10 = (bf16[128,256]{1,0:T(8,128)(2,1)S(1)}, bf16[128,256]{1,0:T(8,128)(2,1)S(1)}, u32[]{:S(2)}, u32[]{:S(2)}) collective-permute-start(bf16[128,256]{1,0:T(8,128)(2,1)S(1)} %shard_map.68), channel_id=1, source_target_pairs={{0,3},{1,2},{2,1},{3,0},{4,7},{5,6},{6,5},{7,4},{8,11},{9,10},{10,... | collective-permute-start | bytes 196616 | tf_op jit(solution)/shard_map/ppermute | solution.py:148
  22.2 0.3 %shard_map.70 = f32[128,256]{1,0:T(8,128)S(1)} custom-call(bf16[256,1408]{1,0:T(8,128)(2,1)S(1)} %collective-permute-done.refs_0_.taken.matrix, bf16[16,128]{1,0:T(8,128)(2,1)S(1)} %shard_map.65.mark, bf16[128,256]{1,0:T(8,128)(2,1)S(1)} %get-tuple-element.13.refs_0_.own, bf16[128,256]{1,0:T(8,128)(2,1)S(1)} %collective-permute-done.2.refs_0_.refs_1_.refs_2_.far, ...), custom_call_target="tpu_custom_call" | custom-call | flops 84000000 | bytes 1000000 | tf_op jit(solution)/shard_map/pallas_call | solution.py:311
  22.5 0.2 collective-permute-start.11
  22.7 0.3 %shard_map.69.mine = f32[128,256]{1,0:T(8,128)S(1)} custom-call(bf16[256,1408]{1,0:T(8,128)(2,1)S(1)} %get-tuple-element.12.matrix.kept, bf16[16,128]{1,0:T(8,128)(2,1)S(1)} %shard_map.65.mark, bf16[128,256]{1,0:T(8,128)(2,1)S(1)} %get-tuple-element.13.refs_0_.own, bf16[128,256]{1,0:T(8,128)(2,1)S(1)} %collective-permute-done.2.refs_0_.refs_1_.refs_2_.far, ...), custom_call_target="tpu_custom_call" | custom-call | flops 84000000 | bytes 1000000 | tf_op jit(solution)/shard_map/pallas_call | solution.py:311
  23.0 0.0 copy-start.1
  23.0 1.5 %collective-permute-done.10.refs_0_.theirs = bf16[128,256]{1,0:T(8,128)(2,1)S(1)} collective-permute-done((bf16[128,256]{1,0:T(8,128)(2,1)S(1)}, bf16[128,256]{1,0:T(8,128)(2,1)S(1)}, u32[]{:S(2)}, u32[]{:S(2)}) %collective-permute-start.10) | collective-permute-done | bytes 65568 | tf_op jit(solution)/shard_map/ppermute | solution.py:148
  24.5 0.0 collective-permute-done.11.other
  24.5 0.8 %shard_map.72 = bf16[128,256]{1,0:T(8,128)(2,1)} custom-call(bf16[128,256]{1,0:T(8,128)(2,1)S(1)} %collective-permute-done.10.refs_0_.theirs, f32[128,256]{1,0:T(8,128)S(1)} %shard_map.69.mine, f32[128,256]{1,0:T(8,128)S(1)} %collective-permute-done.11.other, bf16[256,256]{1,0:T(8,128)(2,1)S(1)} %copy-done.1, bf16[16,128]{1,0:T(8,128)(2,1)S(1)} %shard_map.71.mark), custom_call_target="tpu_custom_call" | custom-call | flops 17000000 | bytes 400000 | tf_op jit(solution)/shard_map/pallas_call | solution.py:343
  (20 shorter events, 0.1 us)
Async XLA Ops:
  0.0 5.1 %copy-start.4 = (s32[1,8]{1,0:T(1,128)S(1)}, s32[1,8]{1,0:T(1,128)}, u32[]{:S(2)}) copy-start(s32[1,8]{1,0:T(1,128)} %counts.1) | copy-start | bytes 100
  0.0 5.1 %copy-start.3 = (s32[96,2]{0,1:T(2,128)S(1)}, s32[96,2]{0,1:T(2,128)}, u32[]{:S(2)}) copy-start(s32[96,2]{0,1:T(2,128)} %param.8) | copy-start | bytes 2308
  0.0 5.2 %copy-start = (bf16[96,128,128]{2,1,0:T(8,128)(2,1)S(1)}, bf16[96,128,128]{2,1,0:T(8,128)(2,1)}, u32[]{:S(2)}) copy-start(bf16[96,128,128]{2,1,0:T(8,128)(2,1)} %values.1) | copy-start | bytes 9437188
  0.0 7.5 %collective-permute-start.1 = (bf16[128,256]{1,0:T(8,128)(2,1)}, bf16[128,256]{1,0:T(8,128)(2,1)S(1)}, u32[]{:S(2)}, u32[]{:S(2)}) collective-permute-start(bf16[128,256]{1,0:T(8,128)(2,1)} %value.1), channel_id=1, source_target_pairs={{0,24},{1,9},{2,26},{3,11},{4,28},{5,13},{6,30},{7,15},{8,0},{9,17... | collective-permute-start | bytes 196616 | tf_op jit(solution)/shard_map/ppermute | solution.py:148
  5.1 5.4 %collective-permute-start.2 = (bf16[128,256]{1,0:T(8,128)(2,1)}, bf16[128,256]{1,0:T(8,128)(2,1)S(1)}, u32[]{:S(2)}, u32[]{:S(2)}) collective-permute-start(bf16[128,256]{1,0:T(8,128)(2,1)} %value.1), channel_id=1, source_target_pairs={{0,16},{1,17},{2,18},{3,19},{4,20},{5,21},{6,22},{7,23},{8,24},{9,... | collective-permute-start | bytes 196616 | tf_op jit(solution)/shard_map/ppermute | solution.py:148
  5.1 2.4 %collective-permute-start.4 = (bf16[128,256]{1,0:T(8,128)(2,1)}, bf16[128,256]{1,0:T(8,128)(2,1)S(1)}, u32[]{:S(2)}, u32[]{:S(2)}) collective-permute-start(bf16[128,256]{1,0:T(8,128)(2,1)} %value.1), channel_id=1, source_target_pairs={{0,2},{1,3},{2,0},{3,1},{4,6},{5,7},{6,4},{7,5},{8,10},{9,11},{10,... | collective-permute-start | bytes 196616 | tf_op jit(solution)/shard_map/ppermute | solution.py:148
  5.1 2.4 %copy-start.2 = (bf16[128,256]{1,0:T(8,128)(2,1)S(1)}, bf16[128,256]{1,0:T(8,128)(2,1)}, u32[]{:S(2)}) copy-start(bf16[128,256]{1,0:T(8,128)(2,1)} %value.1) | copy-start | bytes 196612
  7.1 3.4 %collective-permute-start = (bf16[256,1408]{1,0:T(8,128)(2,1)S(1)}, bf16[256,1408]{1,0:T(8,128)(2,1)S(1)}, u32[]{:S(2)}, u32[]{:S(2)}) collective-permute-start(bf16[256,1408]{1,0:T(8,128)(2,1)S(1)} %get-tuple-element.11), channel_id=1, source_target_pairs={{0,2},{1,3},{2,0},{3,1},{4,6},{5,7},{6,4},{7,5},{8,10},{9,11},{10,... | collective-permute-start | bytes 2162696 | tf_op jit(solution)/shard_map/ppermute | solution.py:148
  7.5 6.7 %collective-permute-start.7 = (bf16[256,256]{1,0:T(8,128)(2,1)S(1)}, bf16[256,256]{1,0:T(8,128)(2,1)S(1)}, u32[]{:S(2)}, u32[]{:S(2)}) collective-permute-start(bf16[256,256]{1,0:T(8,128)(2,1)S(1)} %get-tuple-element.14), channel_id=1, source_target_pairs={{0,1},{1,0},{2,10},{3,27},{4,5},{5,4},{6,14},{7,31},{8,9},{9,8},{1... | collective-permute-start | bytes 393224 | tf_op jit(solution)/shard_map/ppermute | solution.py:148
  10.5 7.6 %collective-permute-start.3 = (bf16[256,256]{1,0:T(8,128)(2,1)S(1)}, bf16[256,256]{1,0:T(8,128)(2,1)S(1)}, u32[]{:S(2)}, u32[]{:S(2)}) collective-permute-start(bf16[256,256]{1,0:T(8,128)(2,1)S(1)} %shard_map.59), channel_id=1, source_target_pairs={{0,1},{1,0},{2,3},{3,2},{4,5},{5,4},{6,7},{7,6},{8,9},{9,8},{10,11... | collective-permute-start | bytes 393224 | tf_op jit(solution)/shard_map/ppermute | solution.py:148
  11.9 6.7 %collective-permute-start.5 = (bf16[256,256]{1,0:T(8,128)(2,1)S(1)}, bf16[256,256]{1,0:T(8,128)(2,1)S(1)}, u32[]{:S(2)}, u32[]{:S(2)}) collective-permute-start(bf16[256,256]{1,0:T(8,128)(2,1)S(1)} %shard_map.62), channel_id=1, source_target_pairs={{0,5},{1,4},{2,7},{3,6},{4,1},{5,0},{6,3},{7,2},{8,13},{9,12},{10,... | collective-permute-start | bytes 393224 | tf_op jit(solution)/shard_map/ppermute | solution.py:148
  13.6 4.5 %collective-permute-start.6 = (bf16[128,256]{1,0:T(8,128)(2,1)S(1)}, bf16[128,256]{1,0:T(8,128)(2,1)S(1)}, u32[]{:S(2)}, u32[]{:S(2)}) collective-permute-start(bf16[128,256]{1,0:T(8,128)(2,1)S(1)} %shard_map.63), channel_id=1, source_target_pairs={{0,4},{1,5},{2,6},{3,7},{4,0},{5,1},{6,2},{7,3},{8,12},{9,13},{10,... | collective-permute-start | bytes 196616 | tf_op jit(solution)/shard_map/ppermute | solution.py:148
  14.2 4.4 %collective-permute-start.8 = (bf16[256,256]{1,0:T(8,128)(2,1)S(1)}, bf16[256,256]{1,0:T(8,128)(2,1)S(1)}, u32[]{:S(2)}, u32[]{:S(2)}) collective-permute-start(bf16[256,256]{1,0:T(8,128)(2,1)S(1)} %collective-permute-done.7.ahead.refs_5_), channel_id=1, source_target_pairs={{0,0},{1,1},{2,6},{3,7},{4,4},{5,5},{6,2},{7,3},{8,8},{9,9},{10,14... | collective-permute-start | bytes 393224 | tf_op jit(solution)/shard_map/ppermute | solution.py:148
  18.8 1.7 %collective-permute-start.9 = (bf16[128,256]{1,0:T(8,128)(2,1)S(1)}, bf16[128,256]{1,0:T(8,128)(2,1)S(1)}, u32[]{:S(2)}, u32[]{:S(2)}) collective-permute-start(bf16[128,256]{1,0:T(8,128)(2,1)S(1)} %shard_map.67), channel_id=1, source_target_pairs={{0,2},{1,3},{2,0},{3,1},{4,6},{5,7},{6,4},{7,5},{8,10},{9,11},{10,... | collective-permute-start | bytes 196616 | tf_op jit(solution)/shard_map/ppermute | solution.py:148
  20.5 4.0 %collective-permute-start.10 = (bf16[128,256]{1,0:T(8,128)(2,1)S(1)}, bf16[128,256]{1,0:T(8,128)(2,1)S(1)}, u32[]{:S(2)}, u32[]{:S(2)}) collective-permute-start(bf16[128,256]{1,0:T(8,128)(2,1)S(1)} %shard_map.68), channel_id=1, source_target_pairs={{0,3},{1,2},{2,1},{3,0},{4,7},{5,6},{6,5},{7,4},{8,11},{9,10},{10,... | collective-permute-start | bytes 196616 | tf_op jit(solution)/shard_map/ppermute | solution.py:148
  22.5 2.0 %collective-permute-start.11 = (f32[128,256]{1,0:T(8,128)S(1)}, f32[128,256]{1,0:T(8,128)S(1)}, u32[]{:S(2)}, u32[]{:S(2)}) collective-permute-start(f32[128,256]{1,0:T(8,128)S(1)} %shard_map.70), channel_id=1, source_target_pairs={{0,2},{1,3},{2,0},{3,1},{4,6},{5,7},{6,4},{7,5},{8,10},{9,11},{10,... | collective-permute-start | bytes 393224 | tf_op jit(solution)/shard_map/ppermute | solution.py:148
  23.0 1.5 %copy-start.1 = (bf16[256,256]{1,0:T(8,128)(2,1)S(1)}, bf16[256,256]{1,0:T(8,128)(2,1)}, u32[]{:S(2)}) copy-start(bf16[256,256]{1,0:T(8,128)(2,1)} %weight.1) | copy-start | bytes 393220

commit v10 on v8

--- a/solution.py
+++ b/solution.py
@@ -183,23 +183,25 @@
     core = lax.axis_index("loop") & 1
     rank = lax.axis_index("rep")
     near = (lax.axis_index("loop") >> 1 & 1) == rank
-    kept[...] = jnp.zeros_like(kept)
-    given[...] = jnp.zeros_like(given)
+    for out in (kept, given):
+        for first, count in ((0, 2), (3, 1), (7, 4)):
+            span = pl.ds(first * tile, count * tile)
+            out[:, span] = jnp.zeros((2 * tile, count * tile), out.dtype)
 
     def one(step):
         for spot in range(4):
             total[spot] = jnp.zeros_like(total[spot])
 
         def add(group, carry):
-            for i in range(3):
-                slot = group * 3 + i
+            for i in range(4):
+                slot = group * 4 + i
                 row = coords[0, step * slots + slot] ^ rank
                 column = coords[1, step * slots + slot] ^ rank
                 spot = jnp.where(slot < counts[0, step], row * 2 + column, 4)
                 total[spot] = total[spot] + values[step * slots + slot].astype(jnp.float32)
             return carry
 
-        lax.fori_loop(0, (counts[0, step] + 2) // 3, add, 0)
+        lax.fori_loop(0, (counts[0, step] + 3) // 4, add, 0)
         odd = step & 1
         there = odd * (1 - 2 * core)
         k = jnp.where(rank == 0, step + there, steps - step - there) >> 1

time: 25.6 us -> 25.8 us (level)
  waiting for transfers between devices: 6.58 us -> 7.65 us
  Pallas kernels: 3.91 us -> 3.39 us
  starting transfers between devices: 14.8 us -> 14.5 us
    ppermute x12, waiting for transfers between devices: 6.58 us -> 7.65 us  [send(): return lax.ppermute(value, AXES, route(planes, move))]
    pallas_call x1, Pallas kernels: 1.9 us -> 1.38 us  [dense(): pl.pallas_call(dense_kernel, out_shape=[jax.ShapeDtypeStruct((2 * tile, H...]
  transfers between devices with their start and end apart: 12 -> 12, of which waited for: 5 -> 5; matrix products, arithmetic and copies ran while one was open for 0% -> 0% of each run, Pallas kernels for 11% -> 9%
where the time goes in v10:
time: 25.8 us; the launch traced here: 25.7 us
  starting transfers between devices  14.5 us (56%)
  waiting for transfers between devices  7.65 us (30%)
  Pallas kernels  3.39 us (13%)
    ppermute x12, starting transfers between devices, send(): return lax.ppermute(value, AXES, route(planes, move))  14.5 us
    ppermute x12, waiting for transfers between devices, send(): return lax.ppermute(value, AXES, route(planes, move))  7.65 us
    pallas_call x1, Pallas kernels, dense(): pl.pallas_call(dense_kernel, out_shape=[jax.ShapeDtypeStruct((2 * tile, H...  1.38 us
    pallas_call x4, Pallas kernels, products(): pl.pallas_call(functools.partial(product_kernel, half * rows), out_shape=...  1.11 us
    pallas_call x1, Pallas kernels, last(): pl.pallas_call(last_kernel, out_shape=jax.ShapeDtypeStruct(theirs.shape,...  0.81 us
  transfers between devices with their start and end apart: 12, of which 5 were waited for; matrix products, arithmetic and copies ran while one was open for 0% of the time, Pallas kernels for 9%

profile of v10, /device:TPU:0, one launch (start us, length us, event | category | flops | bytes accessed | tf_op | source)
XLA Modules:
  0.0 25.7 jit_solution(14155204953157162486)
XLA Ops:
  0.0 5.1 %collective-permute-start.1 = (bf16[128,256]{1,0:T(8,128)(2,1)}, bf16[128,256]{1,0:T(8,128)(2,1)S(1)}, u32[]{:S(2)}, u32[]{:S(2)}) collective-permute-start(bf16[128,256]{1,0:T(8,128)(2,1)} %value.1), channel_id=1, source_target_pairs={{0,24},{1,9},{2,26},{3,11},{4,28},{5,13},{6,30},{7,15},{8,0},{9,17... | collective-permute-start | bytes 196616 | tf_op jit(solution)/shard_map/ppermute | solution.py:148
  5.1 0.0 collective-permute-start.2
  5.1 0.0 collective-permute-start.4
  5.1 0.0 copy-start.2
  5.2 1.4 %shard_map.56 = (bf16[256,1408]{1,0:T(8,128)(2,1)S(1)}, bf16[256,1408]{1,0:T(8,128)(2,1)S(1)}) custom-call(bf16[16,128]{1,0:T(8,128)(2,1)S(1)} %shard_map.55.mark, s32[1,8]{1,0:T(1,128)S(1)} %copy-done.4, s32[2,96]{1,0:T(2,128)S(1)} %bitcast.1, bf16[96,128,128]{2,1,0:T(8,128)(2,1)S(1)} %copy-done), custom_call_target="tpu_custom_call" | custom-call | flops 1 | bytes 1 | tf_op jit(solution)/shard_map/pallas_call | solution.py:237
  6.6 0.6 %collective-permute-start = (bf16[256,1408]{1,0:T(8,128)(2,1)S(1)}, bf16[256,1408]{1,0:T(8,128)(2,1)S(1)}, u32[]{:S(2)}, u32[]{:S(2)}) collective-permute-start(bf16[256,1408]{1,0:T(8,128)(2,1)S(1)} %get-tuple-element.9), channel_id=1, source_target_pairs={{0,2},{1,3},{2,0},{3,1},{4,6},{5,7},{6,4},{7,5},{8,10},{9,11},{10,... | collective-permute-start | bytes 2162696 | tf_op jit(solution)/shard_map/ppermute | solution.py:148
  7.1 0.4 %collective-permute-done.1.refs_0_.refs_1_ = bf16[128,256]{1,0:T(8,128)(2,1)S(1)} collective-permute-done((bf16[128,256]{1,0:T(8,128)(2,1)}, bf16[128,256]{1,0:T(8,128)(2,1)S(1)}, u32[]{:S(2)}, u32[]{:S(2)}) %collective-permute-start.1) | collective-permute-done | bytes 65568 | tf_op jit(solution)/shard_map/ppermute | solution.py:148
  7.5 0.0 collective-permute-done.4.mate
  7.5 2.3 %collective-permute-start.7 = (bf16[256,256]{1,0:T(8,128)(2,1)S(1)}, bf16[256,256]{1,0:T(8,128)(2,1)S(1)}, u32[]{:S(2)}, u32[]{:S(2)}) collective-permute-start(bf16[256,256]{1,0:T(8,128)(2,1)S(1)} %get-tuple-element.12), channel_id=1, source_target_pairs={{0,1},{1,0},{2,10},{3,27},{4,5},{5,4},{6,14},{7,31},{8,9},{9,8},{1... | collective-permute-start | bytes 393224 | tf_op jit(solution)/shard_map/ppermute | solution.py:148
  9.8 0.7 %collective-permute-done.2.refs_0_.refs_1_.refs_2_ = bf16[128,256]{1,0:T(8,128)(2,1)S(1)} collective-permute-done((bf16[128,256]{1,0:T(8,128)(2,1)}, bf16[128,256]{1,0:T(8,128)(2,1)S(1)}, u32[]{:S(2)}, u32[]{:S(2)}) %collective-permute-start.2) | collective-permute-done | bytes 65568 | tf_op jit(solution)/shard_map/ppermute | solution.py:148
  10.5 0.0 collective-permute-done.refs_0_.matrix
  10.5 1.4 %collective-permute-start.3 = (bf16[256,256]{1,0:T(8,128)(2,1)S(1)}, bf16[256,256]{1,0:T(8,128)(2,1)S(1)}, u32[]{:S(2)}, u32[]{:S(2)}) collective-permute-start(bf16[256,256]{1,0:T(8,128)(2,1)S(1)} %shard_map.59), channel_id=1, source_target_pairs={{0,1},{1,0},{2,3},{3,2},{4,5},{5,4},{6,7},{7,6},{8,9},{9,8},{10,11... | collective-permute-start | bytes 393224 | tf_op jit(solution)/shard_map/ppermute | solution.py:148
  12.0 1.7 %collective-permute-start.5 = (bf16[256,256]{1,0:T(8,128)(2,1)S(1)}, bf16[256,256]{1,0:T(8,128)(2,1)S(1)}, u32[]{:S(2)}, u32[]{:S(2)}) collective-permute-start(bf16[256,256]{1,0:T(8,128)(2,1)S(1)} %shard_map.62), channel_id=1, source_target_pairs={{0,5},{1,4},{2,7},{3,6},{4,1},{5,0},{6,3},{7,2},{8,13},{9,12},{10,... | collective-permute-start | bytes 393224 | tf_op jit(solution)/shard_map/ppermute | solution.py:148
  13.6 0.5 %collective-permute-start.6 = (bf16[128,256]{1,0:T(8,128)(2,1)S(1)}, bf16[128,256]{1,0:T(8,128)(2,1)S(1)}, u32[]{:S(2)}, u32[]{:S(2)}) collective-permute-start(bf16[128,256]{1,0:T(8,128)(2,1)S(1)} %shard_map.63), channel_id=1, source_target_pairs={{0,4},{1,5},{2,6},{3,7},{4,0},{5,1},{6,2},{7,3},{8,12},{9,13},{10,... | collective-permute-start | bytes 196616 | tf_op jit(solution)/shard_map/ppermute | solution.py:148
  14.2 0.0 collective-permute-done.7.refs_5_
  14.2 0.7 %collective-permute-start.8 = (bf16[256,256]{1,0:T(8,128)(2,1)S(1)}, bf16[256,256]{1,0:T(8,128)(2,1)S(1)}, u32[]{:S(2)}, u32[]{:S(2)}) collective-permute-start(bf16[256,256]{1,0:T(8,128)(2,1)S(1)} %collective-permute-done.7.refs_5_), channel_id=1, source_target_pairs={{0,0},{1,1},{2,6},{3,7},{4,4},{5,5},{6,2},{7,3},{8,8},{9,9},{10,14... | collective-permute-start | bytes 393224 | tf_op jit(solution)/shard_map/ppermute | solution.py:148
  14.8 4.3 %collective-permute-done.6.refs_2_.refs_4_ = bf16[128,256]{1,0:T(8,128)(2,1)S(1)} collective-permute-done((bf16[128,256]{1,0:T(8,128)(2,1)S(1)}, bf16[128,256]{1,0:T(8,128)(2,1)S(1)}, u32[]{:S(2)}, u32[]{:S(2)}) %collective-permute-start.6) | collective-permute-done | bytes 65568 | tf_op jit(solution)/shard_map/ppermute | solution.py:148
  19.1 0.0 collective-permute-done.3.refs_0_.refs_2_
  19.1 0.0 collective-permute-done.5.refs_1_.refs_3_
  19.1 0.0 collective-permute-done.8.refs_6_
  19.1 0.3 %shard_map.66 = bf16[128,256]{1,0:T(8,128)(2,1)S(1)} custom-call(bf16[256,1408]{1,0:T(8,128)(2,1)S(1)} %get-tuple-element.10.matrix, bf16[16,128]{1,0:T(8,128)(2,1)S(1)} %shard_map.64.mark, bf16[128,256]{1,0:T(8,128)(2,1)S(1)} %get-tuple-element.11.refs_0_, bf16[128,256]{1,0:T(8,128)(2,1)S(1)} %collective-permute-done.2.refs_0_.refs_1_.refs_2_, ...), custom_call_target="tpu_custom_call" | custom-call | flops 84000000 | bytes 1000000 | tf_op jit(solution)/shard_map/pallas_call | solution.py:273
  19.4 0.5 %collective-permute-start.9 = (bf16[128,256]{1,0:T(8,128)(2,1)S(1)}, bf16[128,256]{1,0:T(8,128)(2,1)S(1)}, u32[]{:S(2)}, u32[]{:S(2)}) collective-permute-start(bf16[128,256]{1,0:T(8,128)(2,1)S(1)} %shard_map.66), channel_id=1, source_target_pairs={{0,2},{1,3},{2,0},{3,1},{4,6},{5,7},{6,4},{7,5},{8,10},{9,11},{10,... | collective-permute-start | bytes 196616 | tf_op jit(solution)/shard_map/ppermute | solution.py:148
  20.0 0.3 %shard_map.65.mine = f32[128,256]{1,0:T(8,128)S(1)} custom-call(bf16[256,1408]{1,0:T(8,128)(2,1)S(1)} %collective-permute-done.refs_0_.matrix, bf16[16,128]{1,0:T(8,128)(2,1)S(1)} %shard_map.64.mark, bf16[128,256]{1,0:T(8,128)(2,1)S(1)} %get-tuple-element.11.refs_0_, bf16[128,256]{1,0:T(8,128)(2,1)S(1)} %collective-permute-done.2.refs_0_.refs_1_.refs_2_, ...), custom_call_target="tpu_custom_call" | custom-call | flops 84000000 | bytes 1000000 | tf_op jit(solution)/shard_map/pallas_call | solution.py:273
  20.3 0.6 %collective-permute-done.9.other = bf16[128,256]{1,0:T(8,128)(2,1)S(1)} collective-permute-done((bf16[128,256]{1,0:T(8,128)(2,1)S(1)}, bf16[128,256]{1,0:T(8,128)(2,1)S(1)}, u32[]{:S(2)}, u32[]{:S(2)}) %collective-permute-start.9) | collective-permute-done | bytes 65568 | tf_op jit(solution)/shard_map/ppermute | solution.py:148
  20.9 1.5 %collective-permute-start.10 = (bf16[128,256]{1,0:T(8,128)(2,1)S(1)}, bf16[128,256]{1,0:T(8,128)(2,1)S(1)}, u32[]{:S(2)}, u32[]{:S(2)}) collective-permute-start(bf16[128,256]{1,0:T(8,128)(2,1)S(1)} %shard_map.67), channel_id=1, source_target_pairs={{0,3},{1,2},{2,1},{3,0},{4,7},{5,6},{6,5},{7,4},{8,11},{9,10},{10,... | collective-permute-start | bytes 196616 | tf_op jit(solution)/shard_map/ppermute | solution.py:148
  22.4 0.3 %shard_map.69 = f32[128,256]{1,0:T(8,128)S(1)} custom-call(bf16[256,1408]{1,0:T(8,128)(2,1)S(1)} %collective-permute-done.refs_0_.matrix, bf16[16,128]{1,0:T(8,128)(2,1)S(1)} %shard_map.64.mark, bf16[128,256]{1,0:T(8,128)(2,1)S(1)} %get-tuple-element.11.refs_0_, bf16[128,256]{1,0:T(8,128)(2,1)S(1)} %collective-permute-done.2.refs_0_.refs_1_.refs_2_, ...), custom_call_target="tpu_custom_call" | custom-call | flops 84000000 | bytes 1000000 | tf_op jit(solution)/shard_map/pallas_call | solution.py:273
  22.7 0.2 collective-permute-start.11
  22.9 0.3 %shard_map.68.mine = f32[128,256]{1,0:T(8,128)S(1)} custom-call(bf16[256,1408]{1,0:T(8,128)(2,1)S(1)} %get-tuple-element.10.matrix, bf16[16,128]{1,0:T(8,128)(2,1)S(1)} %shard_map.64.mark, bf16[128,256]{1,0:T(8,128)(2,1)S(1)} %get-tuple-element.11.refs_0_, bf16[128,256]{1,0:T(8,128)(2,1)S(1)} %collective-permute-done.2.refs_0_.refs_1_.refs_2_, ...), custom_call_target="tpu_custom_call" | custom-call | flops 84000000 | bytes 1000000 | tf_op jit(solution)/shard_map/pallas_call | solution.py:273
  23.2 0.0 copy-start.1
  23.2 1.7 %collective-permute-done.10.refs_0_.theirs = bf16[128,256]{1,0:T(8,128)(2,1)S(1)} collective-permute-done((bf16[128,256]{1,0:T(8,128)(2,1)S(1)}, bf16[128,256]{1,0:T(8,128)(2,1)S(1)}, u32[]{:S(2)}, u32[]{:S(2)}) %collective-permute-start.10) | collective-permute-done | bytes 65568 | tf_op jit(solution)/shard_map/ppermute | solution.py:148
  24.9 0.0 collective-permute-done.11.other
  24.9 0.8 %shard_map.71 = bf16[128,256]{1,0:T(8,128)(2,1)} custom-call(bf16[128,256]{1,0:T(8,128)(2,1)S(1)} %collective-permute-done.10.refs_0_.theirs, f32[128,256]{1,0:T(8,128)S(1)} %shard_map.68.mine, f32[128,256]{1,0:T(8,128)S(1)} %collective-permute-done.11.other, bf16[256,256]{1,0:T(8,128)(2,1)S(1)} %copy-done.1, bf16[16,128]{1,0:T(8,128)(2,1)S(1)} %shard_map.70.mark), custom_call_target="tpu_custom_call" | custom-call | flops 17000000 | bytes 400000 | tf_op jit(solution)/shard_map/pallas_call | solution.py:305
  (19 shorter events, 0.1 us)
Async XLA Ops:
  0.0 5.1 %copy-start.4 = (s32[1,8]{1,0:T(1,128)S(1)}, s32[1,8]{1,0:T(1,128)}, u32[]{:S(2)}) copy-start(s32[1,8]{1,0:T(1,128)} %counts.1) | copy-start | bytes 100
  0.0 5.1 %copy-start.3 = (s32[96,2]{0,1:T(2,128)S(1)}, s32[96,2]{0,1:T(2,128)}, u32[]{:S(2)}) copy-start(s32[96,2]{0,1:T(2,128)} %param.8) | copy-start | bytes 2308
  0.0 5.2 %copy-start = (bf16[96,128,128]{2,1,0:T(8,128)(2,1)S(1)}, bf16[96,128,128]{2,1,0:T(8,128)(2,1)}, u32[]{:S(2)}) copy-start(bf16[96,128,128]{2,1,0:T(8,128)(2,1)} %values.1) | copy-start | bytes 9437188
  0.0 7.5 %collective-permute-start.1 = (bf16[128,256]{1,0:T(8,128)(2,1)}, bf16[128,256]{1,0:T(8,128)(2,1)S(1)}, u32[]{:S(2)}, u32[]{:S(2)}) collective-permute-start(bf16[128,256]{1,0:T(8,128)(2,1)} %value.1), channel_id=1, source_target_pairs={{0,24},{1,9},{2,26},{3,11},{4,28},{5,13},{6,30},{7,15},{8,0},{9,17... | collective-permute-start | bytes 196616 | tf_op jit(solution)/shard_map/ppermute | solution.py:148
  5.1 5.4 %collective-permute-start.2 = (bf16[128,256]{1,0:T(8,128)(2,1)}, bf16[128,256]{1,0:T(8,128)(2,1)S(1)}, u32[]{:S(2)}, u32[]{:S(2)}) collective-permute-start(bf16[128,256]{1,0:T(8,128)(2,1)} %value.1), channel_id=1, source_target_pairs={{0,16},{1,17},{2,18},{3,19},{4,20},{5,21},{6,22},{7,23},{8,24},{9,... | collective-permute-start | bytes 196616 | tf_op jit(solution)/shard_map/ppermute | solution.py:148
  5.1 2.4 %collective-permute-start.4 = (bf16[128,256]{1,0:T(8,128)(2,1)}, bf16[128,256]{1,0:T(8,128)(2,1)S(1)}, u32[]{:S(2)}, u32[]{:S(2)}) collective-permute-start(bf16[128,256]{1,0:T(8,128)(2,1)} %value.1), channel_id=1, source_target_pairs={{0,2},{1,3},{2,0},{3,1},{4,6},{5,7},{6,4},{7,5},{8,10},{9,11},{10,... | collective-permute-start | bytes 196616 | tf_op jit(solution)/shard_map/ppermute | solution.py:148
  5.1 2.4 %copy-start.2 = (bf16[128,256]{1,0:T(8,128)(2,1)S(1)}, bf16[128,256]{1,0:T(8,128)(2,1)}, u32[]{:S(2)}) copy-start(bf16[128,256]{1,0:T(8,128)(2,1)} %value.1) | copy-start | bytes 196612
  6.6 3.9 %collective-permute-start = (bf16[256,1408]{1,0:T(8,128)(2,1)S(1)}, bf16[256,1408]{1,0:T(8,128)(2,1)S(1)}, u32[]{:S(2)}, u32[]{:S(2)}) collective-permute-start(bf16[256,1408]{1,0:T(8,128)(2,1)S(1)} %get-tuple-element.9), channel_id=1, source_target_pairs={{0,2},{1,3},{2,0},{3,1},{4,6},{5,7},{6,4},{7,5},{8,10},{9,11},{10,... | collective-permute-start | bytes 2162696 | tf_op jit(solution)/shard_map/ppermute | solution.py:148
  7.5 6.7 %collective-permute-start.7 = (bf16[256,256]{1,0:T(8,128)(2,1)S(1)}, bf16[256,256]{1,0:T(8,128)(2,1)S(1)}, u32[]{:S(2)}, u32[]{:S(2)}) collective-permute-start(bf16[256,256]{1,0:T(8,128)(2,1)S(1)} %get-tuple-element.12), channel_id=1, source_target_pairs={{0,1},{1,0},{2,10},{3,27},{4,5},{5,4},{6,14},{7,31},{8,9},{9,8},{1... | collective-permute-start | bytes 393224 | tf_op jit(solution)/shard_map/ppermute | solution.py:148
  10.5 8.6 %collective-permute-start.3 = (bf16[256,256]{1,0:T(8,128)(2,1)S(1)}, bf16[256,256]{1,0:T(8,128)(2,1)S(1)}, u32[]{:S(2)}, u32[]{:S(2)}) collective-permute-start(bf16[256,256]{1,0:T(8,128)(2,1)S(1)} %shard_map.59), channel_id=1, source_target_pairs={{0,1},{1,0},{2,3},{3,2},{4,5},{5,4},{6,7},{7,6},{8,9},{9,8},{10,11... | collective-permute-start | bytes 393224 | tf_op jit(solution)/shard_map/ppermute | solution.py:148
  12.0 7.2 %collective-permute-start.5 = (bf16[256,256]{1,0:T(8,128)(2,1)S(1)}, bf16[256,256]{1,0:T(8,128)(2,1)S(1)}, u32[]{:S(2)}, u32[]{:S(2)}) collective-permute-start(bf16[256,256]{1,0:T(8,128)(2,1)S(1)} %shard_map.62), channel_id=1, source_target_pairs={{0,5},{1,4},{2,7},{3,6},{4,1},{5,0},{6,3},{7,2},{8,13},{9,12},{10,... | collective-permute-start | bytes 393224 | tf_op jit(solution)/shard_map/ppermute | solution.py:148
  13.6 5.5 %collective-permute-start.6 = (bf16[128,256]{1,0:T(8,128)(2,1)S(1)}, bf16[128,256]{1,0:T(8,128)(2,1)S(1)}, u32[]{:S(2)}, u32[]{:S(2)}) collective-permute-start(bf16[128,256]{1,0:T(8,128)(2,1)S(1)} %shard_map.63), channel_id=1, source_target_pairs={{0,4},{1,5},{2,6},{3,7},{4,0},{5,1},{6,2},{7,3},{8,12},{9,13},{10,... | collective-permute-start | bytes 196616 | tf_op jit(solution)/shard_map/ppermute | solution.py:148
  14.2 5.0 %collective-permute-start.8 = (bf16[256,256]{1,0:T(8,128)(2,1)S(1)}, bf16[256,256]{1,0:T(8,128)(2,1)S(1)}, u32[]{:S(2)}, u32[]{:S(2)}) collective-permute-start(bf16[256,256]{1,0:T(8,128)(2,1)S(1)} %collective-permute-done.7.refs_5_), channel_id=1, source_target_pairs={{0,0},{1,1},{2,6},{3,7},{4,4},{5,5},{6,2},{7,3},{8,8},{9,9},{10,14... | collective-permute-start | bytes 393224 | tf_op jit(solution)/shard_map/ppermute | solution.py:148
  19.4 1.4 %collective-permute-start.9 = (bf16[128,256]{1,0:T(8,128)(2,1)S(1)}, bf16[128,256]{1,0:T(8,128)(2,1)S(1)}, u32[]{:S(2)}, u32[]{:S(2)}) collective-permute-start(bf16[128,256]{1,0:T(8,128)(2,1)S(1)} %shard_map.66), channel_id=1, source_target_pairs={{0,2},{1,3},{2,0},{3,1},{4,6},{5,7},{6,4},{7,5},{8,10},{9,11},{10,... | collective-permute-start | bytes 196616 | tf_op jit(solution)/shard_map/ppermute | solution.py:148
  20.9 4.0 %collective-permute-start.10 = (bf16[128,256]{1,0:T(8,128)(2,1)S(1)}, bf16[128,256]{1,0:T(8,128)(2,1)S(1)}, u32[]{:S(2)}, u32[]{:S(2)}) collective-permute-start(bf16[128,256]{1,0:T(8,128)(2,1)S(1)} %shard_map.67), channel_id=1, source_target_pairs={{0,3},{1,2},{2,1},{3,0},{4,7},{5,6},{6,5},{7,4},{8,11},{9,10},{10,... | collective-permute-start | bytes 196616 | tf_op jit(solution)/shard_map/ppermute | solution.py:148
  22.7 2.2 %collective-permute-start.11 = (f32[128,256]{1,0:T(8,128)S(1)}, f32[128,256]{1,0:T(8,128)S(1)}, u32[]{:S(2)}, u32[]{:S(2)}) collective-permute-start(f32[128,256]{1,0:T(8,128)S(1)} %shard_map.69), channel_id=1, source_target_pairs={{0,2},{1,3},{2,0},{3,1},{4,6},{5,7},{6,4},{7,5},{8,10},{9,11},{10,... | collective-permute-start | bytes 393224 | tf_op jit(solution)/shard_map/ppermute | solution.py:148
  23.2 1.7 %copy-start.1 = (bf16[256,256]{1,0:T(8,128)(2,1)S(1)}, bf16[256,256]{1,0:T(8,128)(2,1)}, u32[]{:S(2)}) copy-start(bf16[256,256]{1,0:T(8,128)(2,1)} %weight.1) | copy-start | bytes 393220

commit v11 on v8

--- a/solution.py
+++ b/solution.py
@@ -159,13 +159,13 @@
     kept, given = dense(pause(1_000_000_000), counts, coords, tile_values)
     taken = send(given, core)
     both, own = pair(features, mate, mark(500_000_000, behind), kept)
-    ahead = send(both, lambda z, x, c, y: (z - sign(y), x, c, y) if c else (z, x, c, 1 - y))
+    ahead = send(both, lambda z, x, c, y: (z, x, c, 1 - y) if c else (z - sign(y), x, c, y))
     ready = mark(40_000_000_000, far)
     done = mark(1, taken)
     along_y = send(pick((0, 1), (0, 1), behind, far, done, ready), lambda z, x, c, y: (z, x, c, 1 - y))
     across = send(pick((0, 1), (1, 2), own, behind, far, done, ready), lambda z, x, c, y: (z, 1 - x, c, 1 - y))
     along_x = send(pick((1,), (0,), own, far, done, ready), lambda z, x, c, y: (z, 1 - x, c, y))
-    beside = send(ahead, lambda z, x, c, y: (z, 1 - x, c, y) if c else (z, x, c, y))
+    beside = send(ahead, lambda z, x, c, y: (z, x, 0, y) if c else (z, 1 - x, 1, y))
     arrived = mark(4_000_000_000, along_y, across, along_x)
     held = [own, far, along_y, across, along_x, ahead, beside]
     crossing = send(products(1, kept, held, arrived, jnp.bfloat16), core)
@@ -209,8 +209,8 @@
         paired = (k == 1) == near
         straight = jnp.where(k == 2, 7 + parity, half >> 1)
         homes = (
-            jnp.where(jnp.where(turned, paired, k == 2), 1, parity),
-            jnp.where(k == 0, 0, parity),
+            jnp.where(turned, jnp.where(paired, 1, parity), jnp.where(k == 2, 0, parity)),
+            jnp.where(k == 0, 1, parity),
         )
         places = (
             jnp.where(turned, jnp.where(paired, 9 + parity, 6), straight),

time: 25.6 us -> 25.7 us (level)
  starting transfers between devices: 14.8 us -> 12.5 us
  waiting for transfers between devices: 6.58 us -> 8.75 us
    ppermute x12, starting transfers between devices: 14.8 us -> 12.5 us  [send(): return lax.ppermute(value, AXES, route(planes, move))]
    ppermute x12, waiting for transfers between devices: 6.58 us -> 8.75 us  [send(): return lax.ppermute(value, AXES, route(planes, move))]
  transfers between devices with their start and end apart: 12 -> 12, of which waited for: 5 -> 6; matrix products, arithmetic and copies ran while one was open for 0% -> 0% of each run, Pallas kernels for 11% -> 11%
where the time goes in v11:
time: 25.7 us; the launch traced here: 25.4 us
  starting transfers between devices  12.5 us (49%)
  waiting for transfers between devices  8.75 us (34%)
  Pallas kernels  3.99 us (16%)
    ppermute x12, starting transfers between devices, send(): return lax.ppermute(value, AXES, route(planes, move))  12.5 us
    ppermute x12, waiting for transfers between devices, send(): return lax.ppermute(value, AXES, route(planes, move))  8.75 us
    pallas_call x1, Pallas kernels, dense(): pl.pallas_call(dense_kernel, out_shape=[jax.ShapeDtypeStruct((2 * tile, H...  1.98 us
    pallas_call x4, Pallas kernels, products(): pl.pallas_call(functools.partial(product_kernel, half * rows), out_shape=...  1.11 us
    pallas_call x1, Pallas kernels, last(): pl.pallas_call(last_kernel, out_shape=jax.ShapeDtypeStruct(theirs.shape,...  0.81 us
  transfers between devices with their start and end apart: 12, of which 6 were waited for; matrix products, arithmetic and copies ran while one was open for 0% of the time, Pallas kernels for 11%

profile of v11, /device:TPU:0, one launch (start us, length us, event | category | flops | bytes accessed | tf_op | source)
XLA Modules:
  0.0 25.4 jit_solution(9353124745078132911)
XLA Ops:
  0.0 5.1 %collective-permute-start.1 = (bf16[128,256]{1,0:T(8,128)(2,1)}, bf16[128,256]{1,0:T(8,128)(2,1)S(1)}, u32[]{:S(2)}, u32[]{:S(2)}) collective-permute-start(bf16[128,256]{1,0:T(8,128)(2,1)} %value.1), channel_id=1, source_target_pairs={{0,24},{1,9},{2,26},{3,11},{4,28},{5,13},{6,30},{7,15},{8,0},{9,17... | collective-permute-start | bytes 196616 | tf_op jit(solution)/shard_map/ppermute | solution.py:148
  5.1 0.0 collective-permute-start.2
  5.1 0.0 collective-permute-start.4
  5.1 0.0 copy-start.2
  5.2 2.0 %shard_map.56 = (bf16[256,1408]{1,0:T(8,128)(2,1)S(1)}, bf16[256,1408]{1,0:T(8,128)(2,1)S(1)}) custom-call(bf16[16,128]{1,0:T(8,128)(2,1)S(1)} %shard_map.55.mark, s32[1,8]{1,0:T(1,128)S(1)} %copy-done.4, s32[2,96]{1,0:T(2,128)S(1)} %bitcast.1, bf16[96,128,128]{2,1,0:T(8,128)(2,1)S(1)} %copy-done), custom_call_target="tpu_custom_call" | custom-call | flops 1 | bytes 1 | tf_op jit(solution)/shard_map/pallas_call | solution.py:235
  7.2 0.5 %collective-permute-start = (bf16[256,1408]{1,0:T(8,128)(2,1)S(1)}, bf16[256,1408]{1,0:T(8,128)(2,1)S(1)}, u32[]{:S(2)}, u32[]{:S(2)}) collective-permute-start(bf16[256,1408]{1,0:T(8,128)(2,1)S(1)} %get-tuple-element.9), channel_id=1, source_target_pairs={{0,2},{1,3},{2,0},{3,1},{4,6},{5,7},{6,4},{7,5},{8,10},{9,11},{10,... | collective-permute-start | bytes 2162696 | tf_op jit(solution)/shard_map/ppermute | solution.py:148
  7.7 0.0 collective-permute-done.1.refs_0_.refs_1_
  7.7 0.0 collective-permute-done.4.mate
  7.7 0.5 %collective-permute-start.7 = (bf16[256,256]{1,0:T(8,128)(2,1)S(1)}, bf16[256,256]{1,0:T(8,128)(2,1)S(1)}, u32[]{:S(2)}, u32[]{:S(2)}) collective-permute-start(bf16[256,256]{1,0:T(8,128)(2,1)S(1)} %get-tuple-element.12), channel_id=1, source_target_pairs={{0,8},{1,25},{2,3},{3,2},{4,12},{5,29},{6,7},{7,6},{8,16},{9,1},{1... | collective-permute-start | bytes 393224 | tf_op jit(solution)/shard_map/ppermute | solution.py:148
  8.2 2.3 %collective-permute-done.2.refs_0_.refs_1_.refs_2_ = bf16[128,256]{1,0:T(8,128)(2,1)S(1)} collective-permute-done((bf16[128,256]{1,0:T(8,128)(2,1)}, bf16[128,256]{1,0:T(8,128)(2,1)S(1)}, u32[]{:S(2)}, u32[]{:S(2)}) %collective-permute-start.2) | collective-permute-done | bytes 65568 | tf_op jit(solution)/shard_map/ppermute | solution.py:148
  10.5 0.0 collective-permute-done.refs_0_.matrix
  10.5 1.3 %collective-permute-start.3 = (bf16[256,256]{1,0:T(8,128)(2,1)S(1)}, bf16[256,256]{1,0:T(8,128)(2,1)S(1)}, u32[]{:S(2)}, u32[]{:S(2)}) collective-permute-start(bf16[256,256]{1,0:T(8,128)(2,1)S(1)} %shard_map.59), channel_id=1, source_target_pairs={{0,1},{1,0},{2,3},{3,2},{4,5},{5,4},{6,7},{7,6},{8,9},{9,8},{10,11... | collective-permute-start | bytes 393224 | tf_op jit(solution)/shard_map/ppermute | solution.py:148
  11.9 1.8 %collective-permute-start.5 = (bf16[256,256]{1,0:T(8,128)(2,1)S(1)}, bf16[256,256]{1,0:T(8,128)(2,1)S(1)}, u32[]{:S(2)}, u32[]{:S(2)}) collective-permute-start(bf16[256,256]{1,0:T(8,128)(2,1)S(1)} %shard_map.62), channel_id=1, source_target_pairs={{0,5},{1,4},{2,7},{3,6},{4,1},{5,0},{6,3},{7,2},{8,13},{9,12},{10,... | collective-permute-start | bytes 393224 | tf_op jit(solution)/shard_map/ppermute | solution.py:148
  13.6 0.5 %collective-permute-start.6 = (bf16[128,256]{1,0:T(8,128)(2,1)S(1)}, bf16[128,256]{1,0:T(8,128)(2,1)S(1)}, u32[]{:S(2)}, u32[]{:S(2)}) collective-permute-start(bf16[128,256]{1,0:T(8,128)(2,1)S(1)} %shard_map.63), channel_id=1, source_target_pairs={{0,4},{1,5},{2,6},{3,7},{4,0},{5,1},{6,2},{7,3},{8,12},{9,13},{10,... | collective-permute-start | bytes 196616 | tf_op jit(solution)/shard_map/ppermute | solution.py:148
  14.2 0.6 %collective-permute-done.7.refs_5_ = bf16[256,256]{1,0:T(8,128)(2,1)S(1)} collective-permute-done((bf16[256,256]{1,0:T(8,128)(2,1)S(1)}, bf16[256,256]{1,0:T(8,128)(2,1)S(1)}, u32[]{:S(2)}, u32[]{:S(2)}) %collective-permute-start.7) | collective-permute-done | bytes 131104 | tf_op jit(solution)/shard_map/ppermute | solution.py:148
  14.8 0.0 collective-permute-start.8
  14.8 3.3 %collective-permute-done.6.refs_2_.refs_4_ = bf16[128,256]{1,0:T(8,128)(2,1)S(1)} collective-permute-done((bf16[128,256]{1,0:T(8,128)(2,1)S(1)}, bf16[128,256]{1,0:T(8,128)(2,1)S(1)}, u32[]{:S(2)}, u32[]{:S(2)}) %collective-permute-start.6) | collective-permute-done | bytes 65568 | tf_op jit(solution)/shard_map/ppermute | solution.py:148
  18.1 0.0 collective-permute-done.3.refs_0_.refs_2_
  18.1 0.4 %collective-permute-done.5.refs_1_.refs_3_ = bf16[256,256]{1,0:T(8,128)(2,1)S(1)} collective-permute-done((bf16[256,256]{1,0:T(8,128)(2,1)S(1)}, bf16[256,256]{1,0:T(8,128)(2,1)S(1)}, u32[]{:S(2)}, u32[]{:S(2)}) %collective-permute-start.5) | collective-permute-done | bytes 131104 | tf_op jit(solution)/shard_map/ppermute | solution.py:148
  18.6 0.0 collective-permute-done.8.refs_6_
  18.6 0.3 %shard_map.66 = bf16[128,256]{1,0:T(8,128)(2,1)S(1)} custom-call(bf16[256,1408]{1,0:T(8,128)(2,1)S(1)} %get-tuple-element.10.matrix, bf16[16,128]{1,0:T(8,128)(2,1)S(1)} %shard_map.64.mark, bf16[128,256]{1,0:T(8,128)(2,1)S(1)} %get-tuple-element.11.refs_0_, bf16[128,256]{1,0:T(8,128)(2,1)S(1)} %collective-permute-done.2.refs_0_.refs_1_.refs_2_, ...), custom_call_target="tpu_custom_call" | custom-call | flops 84000000 | bytes 1000000 | tf_op jit(solution)/shard_map/pallas_call | solution.py:271
  18.9 0.8 %collective-permute-start.9 = (bf16[128,256]{1,0:T(8,128)(2,1)S(1)}, bf16[128,256]{1,0:T(8,128)(2,1)S(1)}, u32[]{:S(2)}, u32[]{:S(2)}) collective-permute-start(bf16[128,256]{1,0:T(8,128)(2,1)S(1)} %shard_map.66), channel_id=1, source_target_pairs={{0,2},{1,3},{2,0},{3,1},{4,6},{5,7},{6,4},{7,5},{8,10},{9,11},{10,... | collective-permute-start | bytes 196616 | tf_op jit(solution)/shard_map/ppermute | solution.py:148
  19.7 0.3 %shard_map.65.mine = f32[128,256]{1,0:T(8,128)S(1)} custom-call(bf16[256,1408]{1,0:T(8,128)(2,1)S(1)} %collective-permute-done.refs_0_.matrix, bf16[16,128]{1,0:T(8,128)(2,1)S(1)} %shard_map.64.mark, bf16[128,256]{1,0:T(8,128)(2,1)S(1)} %get-tuple-element.11.refs_0_, bf16[128,256]{1,0:T(8,128)(2,1)S(1)} %collective-permute-done.2.refs_0_.refs_1_.refs_2_, ...), custom_call_target="tpu_custom_call" | custom-call | flops 84000000 | bytes 1000000 | tf_op jit(solution)/shard_map/pallas_call | solution.py:271
  20.0 0.6 %collective-permute-done.9.other = bf16[128,256]{1,0:T(8,128)(2,1)S(1)} collective-permute-done((bf16[128,256]{1,0:T(8,128)(2,1)S(1)}, bf16[128,256]{1,0:T(8,128)(2,1)S(1)}, u32[]{:S(2)}, u32[]{:S(2)}) %collective-permute-start.9) | collective-permute-done | bytes 65568 | tf_op jit(solution)/shard_map/ppermute | solution.py:148
  20.6 1.7 %collective-permute-start.10 = (bf16[128,256]{1,0:T(8,128)(2,1)S(1)}, bf16[128,256]{1,0:T(8,128)(2,1)S(1)}, u32[]{:S(2)}, u32[]{:S(2)}) collective-permute-start(bf16[128,256]{1,0:T(8,128)(2,1)S(1)} %shard_map.67), channel_id=1, source_target_pairs={{0,3},{1,2},{2,1},{3,0},{4,7},{5,6},{6,5},{7,4},{8,11},{9,10},{10,... | collective-permute-start | bytes 196616 | tf_op jit(solution)/shard_map/ppermute | solution.py:148
  22.4 0.3 %shard_map.69 = f32[128,256]{1,0:T(8,128)S(1)} custom-call(bf16[256,1408]{1,0:T(8,128)(2,1)S(1)} %collective-permute-done.refs_0_.matrix, bf16[16,128]{1,0:T(8,128)(2,1)S(1)} %shard_map.64.mark, bf16[128,256]{1,0:T(8,128)(2,1)S(1)} %get-tuple-element.11.refs_0_, bf16[128,256]{1,0:T(8,128)(2,1)S(1)} %collective-permute-done.2.refs_0_.refs_1_.refs_2_, ...), custom_call_target="tpu_custom_call" | custom-call | flops 84000000 | bytes 1000000 | tf_op jit(solution)/shard_map/pallas_call | solution.py:271
  22.7 0.2 collective-permute-start.11
  22.9 0.3 %shard_map.68.mine = f32[128,256]{1,0:T(8,128)S(1)} custom-call(bf16[256,1408]{1,0:T(8,128)(2,1)S(1)} %get-tuple-element.10.matrix, bf16[16,128]{1,0:T(8,128)(2,1)S(1)} %shard_map.64.mark, bf16[128,256]{1,0:T(8,128)(2,1)S(1)} %get-tuple-element.11.refs_0_, bf16[128,256]{1,0:T(8,128)(2,1)S(1)} %collective-permute-done.2.refs_0_.refs_1_.refs_2_, ...), custom_call_target="tpu_custom_call" | custom-call | flops 84000000 | bytes 1000000 | tf_op jit(solution)/shard_map/pallas_call | solution.py:271
  23.2 0.0 copy-start.1
  23.2 1.5 %collective-permute-done.10.refs_0_.theirs = bf16[128,256]{1,0:T(8,128)(2,1)S(1)} collective-permute-done((bf16[128,256]{1,0:T(8,128)(2,1)S(1)}, bf16[128,256]{1,0:T(8,128)(2,1)S(1)}, u32[]{:S(2)}, u32[]{:S(2)}) %collective-permute-start.10) | collective-permute-done | bytes 65568 | tf_op jit(solution)/shard_map/ppermute | solution.py:148
  24.6 0.0 collective-permute-done.11.other
  24.6 0.8 %shard_map.71 = bf16[128,256]{1,0:T(8,128)(2,1)} custom-call(bf16[128,256]{1,0:T(8,128)(2,1)S(1)} %collective-permute-done.10.refs_0_.theirs, f32[128,256]{1,0:T(8,128)S(1)} %shard_map.68.mine, f32[128,256]{1,0:T(8,128)S(1)} %collective-permute-done.11.other, bf16[256,256]{1,0:T(8,128)(2,1)S(1)} %copy-done.1, bf16[16,128]{1,0:T(8,128)(2,1)S(1)} %shard_map.70.mark), custom_call_target="tpu_custom_call" | custom-call | flops 17000000 | bytes 400000 | tf_op jit(solution)/shard_map/pallas_call | solution.py:303
  (19 shorter events, 0.1 us)
Async XLA Ops:
  0.0 5.1 %copy-start.4 = (s32[1,8]{1,0:T(1,128)S(1)}, s32[1,8]{1,0:T(1,128)}, u32[]{:S(2)}) copy-start(s32[1,8]{1,0:T(1,128)} %counts.1) | copy-start | bytes 100
  0.0 5.1 %copy-start.3 = (s32[96,2]{0,1:T(2,128)S(1)}, s32[96,2]{0,1:T(2,128)}, u32[]{:S(2)}) copy-start(s32[96,2]{0,1:T(2,128)} %param.8) | copy-start | bytes 2308
  0.0 5.2 %copy-start = (bf16[96,128,128]{2,1,0:T(8,128)(2,1)S(1)}, bf16[96,128,128]{2,1,0:T(8,128)(2,1)}, u32[]{:S(2)}) copy-start(bf16[96,128,128]{2,1,0:T(8,128)(2,1)} %values.1) | copy-start | bytes 9437188
  0.0 7.7 %collective-permute-start.1 = (bf16[128,256]{1,0:T(8,128)(2,1)}, bf16[128,256]{1,0:T(8,128)(2,1)S(1)}, u32[]{:S(2)}, u32[]{:S(2)}) collective-permute-start(bf16[128,256]{1,0:T(8,128)(2,1)} %value.1), channel_id=1, source_target_pairs={{0,24},{1,9},{2,26},{3,11},{4,28},{5,13},{6,30},{7,15},{8,0},{9,17... | collective-permute-start | bytes 196616 | tf_op jit(solution)/shard_map/ppermute | solution.py:148
  5.1 5.4 %collective-permute-start.2 = (bf16[128,256]{1,0:T(8,128)(2,1)}, bf16[128,256]{1,0:T(8,128)(2,1)S(1)}, u32[]{:S(2)}, u32[]{:S(2)}) collective-permute-start(bf16[128,256]{1,0:T(8,128)(2,1)} %value.1), channel_id=1, source_target_pairs={{0,16},{1,17},{2,18},{3,19},{4,20},{5,21},{6,22},{7,23},{8,24},{9,... | collective-permute-start | bytes 196616 | tf_op jit(solution)/shard_map/ppermute | solution.py:148
  5.1 2.6 %collective-permute-start.4 = (bf16[128,256]{1,0:T(8,128)(2,1)}, bf16[128,256]{1,0:T(8,128)(2,1)S(1)}, u32[]{:S(2)}, u32[]{:S(2)}) collective-permute-start(bf16[128,256]{1,0:T(8,128)(2,1)} %value.1), channel_id=1, source_target_pairs={{0,2},{1,3},{2,0},{3,1},{4,6},{5,7},{6,4},{7,5},{8,10},{9,11},{10,... | collective-permute-start | bytes 196616 | tf_op jit(solution)/shard_map/ppermute | solution.py:148
  5.1 2.6 %copy-start.2 = (bf16[128,256]{1,0:T(8,128)(2,1)S(1)}, bf16[128,256]{1,0:T(8,128)(2,1)}, u32[]{:S(2)}) copy-start(bf16[128,256]{1,0:T(8,128)(2,1)} %value.1) | copy-start | bytes 196612
  7.2 3.3 %collective-permute-start = (bf16[256,1408]{1,0:T(8,128)(2,1)S(1)}, bf16[256,1408]{1,0:T(8,128)(2,1)S(1)}, u32[]{:S(2)}, u32[]{:S(2)}) collective-permute-start(bf16[256,1408]{1,0:T(8,128)(2,1)S(1)} %get-tuple-element.9), channel_id=1, source_target_pairs={{0,2},{1,3},{2,0},{3,1},{4,6},{5,7},{6,4},{7,5},{8,10},{9,11},{10,... | collective-permute-start | bytes 2162696 | tf_op jit(solution)/shard_map/ppermute | solution.py:148
  7.7 7.1 %collective-permute-start.7 = (bf16[256,256]{1,0:T(8,128)(2,1)S(1)}, bf16[256,256]{1,0:T(8,128)(2,1)S(1)}, u32[]{:S(2)}, u32[]{:S(2)}) collective-permute-start(bf16[256,256]{1,0:T(8,128)(2,1)S(1)} %get-tuple-element.12), channel_id=1, source_target_pairs={{0,8},{1,25},{2,3},{3,2},{4,12},{5,29},{6,7},{7,6},{8,16},{9,1},{1... | collective-permute-start | bytes 393224 | tf_op jit(solution)/shard_map/ppermute | solution.py:148
  10.5 7.6 %collective-permute-start.3 = (bf16[256,256]{1,0:T(8,128)(2,1)S(1)}, bf16[256,256]{1,0:T(8,128)(2,1)S(1)}, u32[]{:S(2)}, u32[]{:S(2)}) collective-permute-start(bf16[256,256]{1,0:T(8,128)(2,1)S(1)} %shard_map.59), channel_id=1, source_target_pairs={{0,1},{1,0},{2,3},{3,2},{4,5},{5,4},{6,7},{7,6},{8,9},{9,8},{10,11... | collective-permute-start | bytes 393224 | tf_op jit(solution)/shard_map/ppermute | solution.py:148
  11.9 6.7 %collective-permute-start.5 = (bf16[256,256]{1,0:T(8,128)(2,1)S(1)}, bf16[256,256]{1,0:T(8,128)(2,1)S(1)}, u32[]{:S(2)}, u32[]{:S(2)}) collective-permute-start(bf16[256,256]{1,0:T(8,128)(2,1)S(1)} %shard_map.62), channel_id=1, source_target_pairs={{0,5},{1,4},{2,7},{3,6},{4,1},{5,0},{6,3},{7,2},{8,13},{9,12},{10,... | collective-permute-start | bytes 393224 | tf_op jit(solution)/shard_map/ppermute | solution.py:148
  13.6 4.5 %collective-permute-start.6 = (bf16[128,256]{1,0:T(8,128)(2,1)S(1)}, bf16[128,256]{1,0:T(8,128)(2,1)S(1)}, u32[]{:S(2)}, u32[]{:S(2)}) collective-permute-start(bf16[128,256]{1,0:T(8,128)(2,1)S(1)} %shard_map.63), channel_id=1, source_target_pairs={{0,4},{1,5},{2,6},{3,7},{4,0},{5,1},{6,2},{7,3},{8,12},{9,13},{10,... | collective-permute-start | bytes 196616 | tf_op jit(solution)/shard_map/ppermute | solution.py:148
  14.8 3.8 %collective-permute-start.8 = (bf16[256,256]{1,0:T(8,128)(2,1)S(1)}, bf16[256,256]{1,0:T(8,128)(2,1)S(1)}, u32[]{:S(2)}, u32[]{:S(2)}) collective-permute-start(bf16[256,256]{1,0:T(8,128)(2,1)S(1)} %collective-permute-done.7.refs_5_), channel_id=1, source_target_pairs={{0,6},{1,7},{2,0},{3,1},{4,2},{5,3},{6,4},{7,5},{8,14},{9,15},{10,... | collective-permute-start | bytes 393224 | tf_op jit(solution)/shard_map/ppermute | solution.py:148
  18.9 1.7 %collective-permute-start.9 = (bf16[128,256]{1,0:T(8,128)(2,1)S(1)}, bf16[128,256]{1,0:T(8,128)(2,1)S(1)}, u32[]{:S(2)}, u32[]{:S(2)}) collective-permute-start(bf16[128,256]{1,0:T(8,128)(2,1)S(1)} %shard_map.66), channel_id=1, source_target_pairs={{0,2},{1,3},{2,0},{3,1},{4,6},{5,7},{6,4},{7,5},{8,10},{9,11},{10,... | collective-permute-start | bytes 196616 | tf_op jit(solution)/shard_map/ppermute | solution.py:148
  20.6 4.0 %collective-permute-start.10 = (bf16[128,256]{1,0:T(8,128)(2,1)S(1)}, bf16[128,256]{1,0:T(8,128)(2,1)S(1)}, u32[]{:S(2)}, u32[]{:S(2)}) collective-permute-start(bf16[128,256]{1,0:T(8,128)(2,1)S(1)} %shard_map.67), channel_id=1, source_target_pairs={{0,3},{1,2},{2,1},{3,0},{4,7},{5,6},{6,5},{7,4},{8,11},{9,10},{10,... | collective-permute-start | bytes 196616 | tf_op jit(solution)/shard_map/ppermute | solution.py:148
  22.7 2.0 %collective-permute-start.11 = (f32[128,256]{1,0:T(8,128)S(1)}, f32[128,256]{1,0:T(8,128)S(1)}, u32[]{:S(2)}, u32[]{:S(2)}) collective-permute-start(f32[128,256]{1,0:T(8,128)S(1)} %shard_map.69), channel_id=1, source_target_pairs={{0,2},{1,3},{2,0},{3,1},{4,6},{5,7},{6,4},{7,5},{8,10},{9,11},{10,... | collective-permute-start | bytes 393224 | tf_op jit(solution)/shard_map/ppermute | solution.py:148
  23.2 1.5 %copy-start.1 = (bf16[256,256]{1,0:T(8,128)(2,1)S(1)}, bf16[256,256]{1,0:T(8,128)(2,1)}, u32[]{:S(2)}) copy-start(bf16[256,256]{1,0:T(8,128)(2,1)} %weight.1) | copy-start | bytes 393220
